TPU v7x, 512 devices: a whole 4x8x8 slice. The times are simulated.
512 devices in a mesh: lag: 32 (over z_lo, x, core), row: 16 (over y, z_hi).
Axes of the slice: x: 4, y: 8, z: 8 (z_hi: 2, z_lo: 4; z = z_hi * 4 + z_lo), core: 2. Of those that a mesh axis runs over, the one named last changes fastest.
Arguments:
- z_blocks: bfloat16 [32, 192, 11, 128, 128], P('lag', 'row'), may hold values from -0.02734375 to 0.02734375
- block_cols: int32 [32, 192, 11], P('lag', 'row'), may hold values from 0 to 191, as said below
- history: bfloat16 [32, 24576, 128], P('lag', 'row'), may hold values from -6 to 6
- incident: bfloat16 [4, 24576, 128], P(None, 'row'), may hold values from -6 to 6
- near_inverse: float32 [192, 128, 128], P('row'), as said below
Outputs:
- current: bfloat16 [24576, 128], P('row')
Inputs may be any that keep to these rules, and one draw needn't show every extreme that they name: `block_cols`: the 11 block columns of one block row of one lag are distinct and lie from (i // 12 - 1) * 12 to (i // 12 + 2) * 12 - 1, within 0 to 191. Each block of near_inverse has a diagonal near 1 to 2 and off-diagonal entries of order one over the square root of 128.
All inputs are finite; a program needn't handle non-finite values.
Results may differ from a plain program's by a relative error of at most 0.0054.
Values may be sent and summed in bfloat16 or wider, within the bound.
No kernel may reach another device: no remote copies, remote signals or barrier semaphores. Data moves between devices by JAX's collectives and lax.ppermute only.
A program may use at most 128 MiB of HBM per device.

v0:
```python
import jax
import jax.numpy as jnp
from jax import lax
from jax.sharding import PartitionSpec as P


def extended(value, sides, width):
    for axis, dim in sides:
        size, length = (lax.axis_size(axis), value.shape[dim])
        up = [(i, (i + 1) % size) for i in range(size - 1)]
        down = [(j, i) for i, j in up]
        last = lax.slice_in_dim(value, length - width, length, axis=dim)
        initial = lax.slice_in_dim(value, 0, width, axis=dim)
        before = lax.ppermute(last, axis, up)
        after = lax.ppermute(initial, axis, down)
        value = jnp.concatenate([before, value, after], axis=dim)
    return value


def from_behind(value, axis, steps):
    count = lax.axis_size(axis)
    initial, last = (max(0, -steps), min(count, count - steps))
    return lax.ppermute(value, axis, [(source, source + steps) for source in range(initial, last)])


def near_solve(inverse, driven, blocks, width):
    solved = jnp.einsum(
        "bpq,bqc->bpc", inverse, driven.reshape(blocks, width, -1), precision=lax.Precision.HIGHEST
    )
    return solved.reshape(blocks * width, -1).astype(jnp.bfloat16)


def settle(partial_value, incident_step, near_inverse):
    blocks = near_inverse.shape[0]
    width = near_inverse.shape[1]
    total = None
    summed = lax.psum(partial_value, "lag")
    total = summed
    driven = incident_step.astype(jnp.float32) - total
    return near_solve(near_inverse, driven, blocks, width)


def per_device(z_blocks, block_cols, history, incident, near_inverse):
    blocks = near_inverse.shape[0]
    width = near_inverse.shape[1]
    rows = history.shape[1]
    waves = history.shape[2]
    steps = incident.shape[0]
    lag_pos = lax.axis_index("lag")
    row_pos = lax.axis_index("row")
    local_cols = block_cols[0] - (row_pos * blocks - blocks)
    zmat = z_blocks[0]
    slot = history[0]
    current = slot
    for step in range(steps):
        padded = extended(slot, (("row", 0),), rows)
        tiles = jnp.take(padded.reshape(3 * blocks, width, waves), local_cols, axis=0)
        partial_value = jnp.einsum(
            "bjpq,bjqc->bpc", zmat, tiles, preferred_element_type=jnp.float32
        ).reshape(rows, waves)
        current = settle(partial_value, incident[step], near_inverse)
        if step + 1 < steps:
            moved = from_behind(slot, "lag", 1)
            slot = jnp.where(lag_pos == 0, current, moved)
    return current


def solution(mesh):
    return jax.shard_map(
        per_device,
        mesh=mesh,
        in_specs=(
            P("lag", "row", None, None, None),
            P("lag", "row", None),
            P("lag", "row", None),
            P(None, "row", None),
            P("row", None, None),
        ),
        out_specs=P("row", None),
        check_vma=False,
    )
```

profile of v0, /device:TPU:1, one launch (start us, length us, event | category | flops | bytes accessed | tf_op | source)
XLA Modules:
  0.0 1368.6 jit_solution(4641498490348790625)
XLA Ops:
  6.5 0.0 copy-start
  6.5 0.0 all-reduce.5.cloned.1.call-start
  6.5 1.4 collective-permute-start.1
  8.0 12.1 collective-permute-start
  20.1 0.7 broadcast_subtract_fusion
  20.8 0.1 copy.10
  20.9 0.1 copy.14
  21.0 0.1 reshape.115
  21.1 3.7 collective-permute-done.1
  24.8 22.5 %collective-permute-done = bf16[1536,128]{1,0:T(8,128)(2,1)S(1)} collective-permute-done((bf16[1536,128]{1,0:T(8,128)(2,1)}, bf16[1536,128]{1,0:T(8,128)(2,1)S(1)}, u32[]{:S(2)}, u32[]{:S(2)}) %collective-permute-start) | collective-permute-done | bytes 393248 | tf_op jit(solution)/shard_map/ppermute | solution.py:14
  47.3 1.1 pad_maximum_fusion
  48.4 7.5 gather_fusion
  55.9 0.0 copy-start.1
  55.9 5.9 fusion
  61.7 0.0 all-reduce.5.cloned.1.call-update
  61.8 0.0 all-reduce.7.cloned.1.call-start
  61.8 0.0 copy-done.1
  61.8 3.5 collective-permute-start.2
  65.3 290.9 %all-reduce.5.cloned.1.call-done = f32[1536,128]{1,0:T(8,128)} async-done(((f32[1536,128]{1,0:T(8,128)}), f32[1536,128]{1,0:T(8,128)}) %all-reduce.5.cloned.1.call-update) | async-done | bytes 786448 | tf_op jit(solution)/shard_map/psum | solution.py:37
  356.2 1.3 convert_subtract_fusion
  357.5 0.8 convolution_convert_fusion.3
  358.4 0.0 collective-permute-done.2
  358.4 0.1 bitcast_select_fusion.2
  358.5 1.3 collective-permute-start.4
  359.8 7.9 collective-permute-start.3
  367.7 3.2 collective-permute-done.4
  370.9 13.7 %collective-permute-done.3 = bf16[1536,128]{1,0:T(8,128)(2,1)S(1)} collective-permute-done((bf16[1536,128]{1,0:T(8,128)(2,1)S(1)}, bf16[1536,128]{1,0:T(8,128)(2,1)S(1)}, u32[]{:S(2)}, u32[]{:S(2)}) %collective-permute-start.3) | collective-permute-done | bytes 393248 | tf_op jit(solution)/shard_map/ppermute | solution.py:14
  384.6 0.1 pad_maximum_fusion.1
  384.7 7.5 gather_fusion.1
  392.2 5.8 fusion.2
  398.0 0.0 all-reduce.7.cloned.1.call-update
  398.0 0.0 all-reduce.9.cloned.1.call-start
  398.1 1.9 collective-permute-start.5
  400.0 290.8 %all-reduce.7.cloned.1.call-done = f32[1536,128]{1,0:T(8,128)} async-done(((f32[1536,128]{1,0:T(8,128)}), f32[1536,128]{1,0:T(8,128)}) %all-reduce.7.cloned.1.call-update) | async-done | bytes 786448 | tf_op jit(solution)/shard_map/psum | solution.py:37
  690.8 1.3 convert_subtract_fusion.1
  692.1 0.8 convolution_convert_fusion.2
  693.0 0.0 collective-permute-done.5
  693.0 0.1 bitcast_select_fusion.1
  693.1 1.3 collective-permute-start.7
  694.4 8.1 collective-permute-start.6
  702.5 3.0 collective-permute-done.7
  705.5 13.7 %collective-permute-done.6 = bf16[1536,128]{1,0:T(8,128)(2,1)S(1)} collective-permute-done((bf16[1536,128]{1,0:T(8,128)(2,1)S(1)}, bf16[1536,128]{1,0:T(8,128)(2,1)S(1)}, u32[]{:S(2)}, u32[]{:S(2)}) %collective-permute-start.6) | collective-permute-done | bytes 393248 | tf_op jit(solution)/shard_map/ppermute | solution.py:14
  719.2 0.1 pad_maximum_fusion.2
  719.3 7.5 gather_fusion.2
  726.8 5.8 fusion.4
  732.6 0.0 all-reduce.9.cloned.1.call-update
  732.6 0.0 all-reduce.11.cloned.1.call-start
  732.7 1.9 collective-permute-start.8
  734.6 290.8 %all-reduce.9.cloned.1.call-done = f32[1536,128]{1,0:T(8,128)} async-done(((f32[1536,128]{1,0:T(8,128)}), f32[1536,128]{1,0:T(8,128)}) %all-reduce.9.cloned.1.call-update) | async-done | bytes 786448 | tf_op jit(solution)/shard_map/psum | solution.py:37
  1025.4 1.3 convert_subtract_fusion.2
  1026.7 0.8 convolution_convert_fusion.1
  1027.5 0.0 collective-permute-done.8
  1027.6 0.1 bitcast_select_fusion
  1027.6 1.3 collective-permute-start.10
  1028.9 7.9 collective-permute-start.9
  1036.9 3.2 collective-permute-done.10
  1040.1 13.7 %collective-permute-done.9 = bf16[1536,128]{1,0:T(8,128)(2,1)S(1)} collective-permute-done((bf16[1536,128]{1,0:T(8,128)(2,1)S(1)}, bf16[1536,128]{1,0:T(8,128)(2,1)S(1)}, u32[]{:S(2)}, u32[]{:S(2)}) %collective-permute-start.9) | collective-permute-done | bytes 393248 | tf_op jit(solution)/shard_map/ppermute | solution.py:14
  1053.8 0.1 pad_maximum_fusion.3
  1053.9 7.5 gather_fusion.3
  1061.4 5.8 fusion.6
  1067.2 0.0 all-reduce.11.cloned.1.call-update
  1067.2 292.0 %all-reduce.11.cloned.1.call-done = f32[1536,128]{1,0:T(8,128)} async-done(((f32[1536,128]{1,0:T(8,128)}), f32[1536,128]{1,0:T(8,128)}) %all-reduce.11.cloned.1.call-update) | async-done | bytes 786448 | tf_op jit(solution)/shard_map/psum | solution.py:37
  1359.2 1.3 convert_subtract_fusion.3
  1360.5 1.6 convolution_convert_fusion
  (4 shorter events, 0.0 us)
Async XLA Ops:
  6.5 351.0 %copy-start = (f32[12,128,128]{2,1,0:T(8,128)S(1)}, f32[12,128,128]{2,1,0:T(8,128)}, u32[]{:S(2)}) copy-start(f32[12,128,128]{2,1,0:T(8,128)} %param.11) | copy-start | bytes 2359300
  6.5 349.7 %all-reduce.5.cloned.1.call-start = ((), (), s32[]{:S(2)}) async-start(), calls=%async_computation | async-start | bytes 1572864 | tf_op jit(solution)/shard_map/psum | solution.py:37
  6.5 18.3 %collective-permute-start.1 = (bf16[1536,128]{1,0:T(8,128)(2,1)}, bf16[1536,128]{1,0:T(8,128)(2,1)S(1)}, u32[]{:S(2)}, u32[]{:S(2)}) collective-permute-start(bf16[1536,128]{1,0:T(8,128)(2,1)} %bitcast.101), channel_id=1, source_target_pairs={{1,0},{2,1},{3,2},{4,3},{5,4},{6,5},{7,6},{8,7},{9,8},{10,9},{11,1... | collective-permute-start | bytes 1179656 | tf_op jit(solution)/shard_map/ppermute | solution.py:15
  8.0 39.3 %collective-permute-start = (bf16[1536,128]{1,0:T(8,128)(2,1)}, bf16[1536,128]{1,0:T(8,128)(2,1)S(1)}, u32[]{:S(2)}, u32[]{:S(2)}) collective-permute-start(bf16[1536,128]{1,0:T(8,128)(2,1)} %bitcast.102), channel_id=1, source_target_pairs={{0,1},{1,2},{2,3},{3,4},{4,5},{5,6},{6,7},{7,8},{8,9},{9,10},{10,1... | collective-permute-start | bytes 1179656 | tf_op jit(solution)/shard_map/ppermute | solution.py:14
  55.9 5.9 copy-start.1
  61.8 629.1 %all-reduce.7.cloned.1.call-start = ((), (), s32[]{:S(2)}) async-start(), calls=%async_computation.1 | async-start | bytes 1572864 | tf_op jit(solution)/shard_map/psum | solution.py:37
  61.8 296.6 %collective-permute-start.2 = (bf16[1536,128]{1,0:T(8,128)(2,1)S(1)}, bf16[1536,128]{1,0:T(8,128)(2,1)S(1)}, u32[]{:S(2)}, u32[]{:S(2)}) collective-permute-start(bf16[1536,128]{1,0:T(8,128)(2,1)S(1)} %bitcast.104), channel_id=1, source_target_pairs={{0,16},{16,32},{32,48},{48,64},{64,80},{80,96},{96,112},{112,128},... | collective-permute-start | bytes 1179656 | tf_op jit(solution)/shard_map/ppermute | solution.py:23
  358.5 12.4 collective-permute-start.4
  359.8 24.8 %collective-permute-start.3 = (bf16[1536,128]{1,0:T(8,128)(2,1)S(1)}, bf16[1536,128]{1,0:T(8,128)(2,1)S(1)}, u32[]{:S(2)}, u32[]{:S(2)}) collective-permute-start(bf16[1536,128]{1,0:T(8,128)(2,1)S(1)} %bitcast_select_fusion.2), channel_id=1, source_target_pairs={{0,1},{1,2},{2,3},{3,4},{4,5},{5,6},{6,7},{7,8},{8,9},{9,10},{10,1... | collective-permute-start | bytes 1179656 | tf_op jit(solution)/shard_map/ppermute | solution.py:14
  398.0 627.4 %all-reduce.9.cloned.1.call-start = ((), (), s32[]{:S(2)}) async-start(), calls=%async_computation.2 | async-start | bytes 1572864 | tf_op jit(solution)/shard_map/psum | solution.py:37
  398.1 294.9 %collective-permute-start.5 = (bf16[1536,128]{1,0:T(8,128)(2,1)S(1)}, bf16[1536,128]{1,0:T(8,128)(2,1)S(1)}, u32[]{:S(2)}, u32[]{:S(2)}) collective-permute-start(bf16[1536,128]{1,0:T(8,128)(2,1)S(1)} %bitcast_select_fusion.2), channel_id=1, source_target_pairs={{0,16},{16,32},{32,48},{48,64},{64,80},{80,96},{96,112},{112,128},... | collective-permute-start | bytes 1179656 | tf_op jit(solution)/shard_map/ppermute | solution.py:23
  693.1 12.4 collective-permute-start.7
  694.4 24.8 %collective-permute-start.6 = (bf16[1536,128]{1,0:T(8,128)(2,1)S(1)}, bf16[1536,128]{1,0:T(8,128)(2,1)S(1)}, u32[]{:S(2)}, u32[]{:S(2)}) collective-permute-start(bf16[1536,128]{1,0:T(8,128)(2,1)S(1)} %bitcast_select_fusion.1), channel_id=1, source_target_pairs={{0,1},{1,2},{2,3},{3,4},{4,5},{5,6},{6,7},{7,8},{8,9},{9,10},{10,1... | collective-permute-start | bytes 1179656 | tf_op jit(solution)/shard_map/ppermute | solution.py:14
  732.6 626.5 %all-reduce.11.cloned.1.call-start = ((), (), s32[]{:S(2)}) async-start(), calls=%async_computation.3 | async-start | bytes 1572864 | tf_op jit(solution)/shard_map/psum | solution.py:37
  732.7 294.9 %collective-permute-start.8 = (bf16[1536,128]{1,0:T(8,128)(2,1)S(1)}, bf16[1536,128]{1,0:T(8,128)(2,1)S(1)}, u32[]{:S(2)}, u32[]{:S(2)}) collective-permute-start(bf16[1536,128]{1,0:T(8,128)(2,1)S(1)} %bitcast_select_fusion.1), channel_id=1, source_target_pairs={{0,16},{16,32},{32,48},{48,64},{64,80},{80,96},{96,112},{112,128},... | collective-permute-start | bytes 1179656 | tf_op jit(solution)/shard_map/ppermute | solution.py:23
  1027.6 12.4 collective-permute-start.10
  1028.9 24.8 %collective-permute-start.9 = (bf16[1536,128]{1,0:T(8,128)(2,1)S(1)}, bf16[1536,128]{1,0:T(8,128)(2,1)S(1)}, u32[]{:S(2)}, u32[]{:S(2)}) collective-permute-start(bf16[1536,128]{1,0:T(8,128)(2,1)S(1)} %bitcast_select_fusion), channel_id=1, source_target_pairs={{0,1},{1,2},{2,3},{3,4},{4,5},{5,6},{6,7},{7,8},{8,9},{9,10},{10,1... | collective-permute-start | bytes 1179656 | tf_op jit(solution)/shard_map/ppermute | solution.py:14
Sparse Core Ops, SparseCore 0:
  61.9 294.2 all-reduce.4
  398.2 292.6 all-reduce.6
  732.8 292.5 all-reduce.8
  1067.3 291.7 all-reduce.10
where the time goes:
time: 1370 us
  waiting for transfers between devices  1240 us (91%)
  starting transfers between devices  48.8 us (4%)
  local copies, waits for them, and re-layouts  30.3 us (2%)
  matrix products  27.5 us (2%)
    psum x4, waiting for transfers between devices, settle(): summed = lax.psum(partial_value, 'lag')  1160 us
    ppermute x4, waiting for transfers between devices, extended(): before = lax.ppermute(last, axis, up)  63.6 us
    ppermute x4, starting transfers between devices, extended(): before = lax.ppermute(last, axis, up)  36.1 us
    gather x4, local copies, waits for them, and re-layouts, per_device(): jnp.take(padded.reshape(3 * blocks, width, waves), local_cols, axis=0)  30 us
  transfers between devices with their start and end apart: 15, of which 12 were waited for; matrix products, arithmetic and copies ran while one was open for 1% of the time, Pallas kernels for 0%

commit v1 on v0

v1 whole, which is shorter than its diff:
```python
import functools

import jax
import jax.numpy as jnp
from jax import lax
from jax.experimental import pallas as pl
from jax.experimental.pallas import tpu as pltpu
from jax.sharding import PartitionSpec as P

CORES, XS = 2, 4
HALF = 64
AXES = ("lag", "row")


def coords(lag):
    return lag // (XS * CORES), lag // CORES % XS, lag % CORES


def lag_of(z, x, core):
    return (z * XS + x) * CORES + core


def pairs(lags, rows, target):
    out = []
    for lag in range(lags):
        for row in range(rows):
            goal = target(lag, row)
            if goal is not None and 0 <= goal[0] < lags and 0 <= goal[1] < rows:
                out.append((lag * rows + row, goal[0] * rows + goal[1]))
    return out


def send(value, target):
    lags, rows = lax.axis_size("lag"), lax.axis_size("row")
    return lax.ppermute(value, AXES, pairs(lags, rows, target))


def along_z(step, when):
    def target(lag, row):
        z, x, core = coords(lag)
        return (lag_of(z + step, x, core), row) if when(z, x) and z + step >= 0 else None
    return target


def along_x(step, when):
    def target(lag, row):
        z, x, core = coords(lag)
        return (lag_of(z, x + step, core), row) if when(z, x) else None
    return target


def other_core(lag, row):
    return lag ^ 1, row


def sparse_row(z_ref, row, tile, cols, count):
    total = None
    for first in range(0, count, 2):
        js = range(first, min(first + 2, count))
        left = [z_ref[row, j] for j in js]
        right = [tile(cols(j)) for j in js]
        if len(left) > 1:
            left, right = [jnp.concatenate(left, axis=1)], [jnp.concatenate(right, axis=0)]
        term = jnp.dot(left[0], right[0], preferred_element_type=jnp.float32)
        total = term if total is None else total + term
    return total


def low_lanes(shape):
    return lax.broadcasted_iota(jnp.int32, shape, len(shape) - 1) < HALF


def pack(first, second):
    low = low_lanes(first.shape)
    return (
        jnp.where(low, first, pltpu.roll(second, HALF, 1)),
        jnp.where(low, pltpu.roll(first, HALF, 1), second),
    )


def history_kernel(count, meta, z_ref, past_ref, keep_ref, send_ref):
    step = pl.program_id(0)
    core = meta[0]
    rows = []
    for part in range(2):
        base = 8 + (2 * step + part) * count
        rows.append(sparse_row(z_ref, part, lambda c: past_ref[c], lambda j: meta[base + j], count))
    low, high = pack(*rows)
    keep_ref[0] = jnp.where(core == 0, low, high)
    send_ref[0] = jnp.where(core == 0, high, low)


def history_partial(meta, zmat, past):
    blocks, count, width, unused = zmat.shape
    half = jax.ShapeDtypeStruct((blocks // 2, width, width), jnp.float32)
    spec = pl.BlockSpec((1, width, width), lambda i, meta: (i, 0, 0))
    return pl.pallas_call(
        functools.partial(history_kernel, count),
        out_shape=(half, half),
        grid_spec=pltpu.PrefetchScalarGridSpec(
            num_scalar_prefetch=1,
            grid=(blocks // 2,),
            in_specs=[
                pl.BlockSpec((2, count, width, width), lambda i, meta: (i, 0, 0, 0)),
                pl.BlockSpec(past.shape, lambda i, meta: (0, 0, 0)),
            ],
            out_specs=(spec, spec),
        ),
        compiler_params=pltpu.CompilerParams(vmem_limit_bytes=32 * 1024 * 1024),
        cost_estimate=pl.CostEstimate(
            flops=2 * blocks * count * width ** 3, bytes_accessed=zmat.size * 2, transcendentals=0
        ),
    )(meta, zmat, past)


def packed_rows(meta, z_ref, now_ref, step, count):
    rows = []
    for part in range(2):
        base = 8 + (2 * step + part) * count

        def tile(col):
            both = now_ref[col // 2]
            mine = low_lanes(both.shape) == (col % 2 == 0)
            return jnp.where(mine, both, jnp.zeros_like(both))

        total = sparse_row(z_ref, part, tile, lambda j: meta[base + j], count)
        rows.append(total + pltpu.roll(total, HALF, 1))
    return jnp.where(low_lanes(rows[0].shape), rows[0], rows[1])


def lag_kernel(count, meta, z_ref, now_ref, *rest):
    out_ref = rest[-1]
    step = pl.program_id(0)

    @pl.when(meta[1] != 0)
    def _():
        total = packed_rows(meta, z_ref, now_ref, step, count)
        if len(rest) == 2:
            total = total + rest[0][0]
        out_ref[0] = total


def lag_product(meta, zmat, now, *more):
    blocks, count, width, unused = zmat.shape
    spec = pl.BlockSpec((1, width, width), lambda i, meta: (i * meta[1], 0, 0))
    return pl.pallas_call(
        functools.partial(lag_kernel, count),
        out_shape=jax.ShapeDtypeStruct((blocks // 2, width, width), jnp.float32),
        grid_spec=pltpu.PrefetchScalarGridSpec(
            num_scalar_prefetch=1,
            grid=(blocks // 2,),
            in_specs=[
                pl.BlockSpec((2, count, width, width), lambda i, meta: (i * meta[1], 0, 0, 0)),
                pl.BlockSpec(now.shape, lambda i, meta: (0, 0, 0)),
            ] + [spec] * len(more),
            out_specs=spec,
        ),
        compiler_params=pltpu.CompilerParams(vmem_limit_bytes=32 * 1024 * 1024),
    )(meta, zmat, now, *more)


def step_kernel(count, product, old, meta, *refs):
    refs = list(refs)
    incident_ref, summed_ref, inverse_ref = refs[:3]
    out_ref = refs[-1]
    step = pl.program_id(0)

    @pl.when(meta[1] != 0)
    def _():
        parts = []
        for part in range(2):
            parts.append(incident_ref[part].astype(jnp.float32))
        low, high = pack(*parts)
        driven = jnp.where(meta[0] == 0, low, high) - summed_ref[0]
        if old:
            driven = driven - refs[-2][0]
        if product:
            driven = driven - packed_rows(meta, refs[3], refs[4], step, count)
        solved = []
        for part in range(2):
            solved.append(
                jnp.dot(
                    inverse_ref[part], driven,
                    precision=lax.Precision.HIGHEST, preferred_element_type=jnp.float32,
                )
            )
        out_ref[0] = jnp.where(low_lanes(driven.shape), solved[0], solved[1]).astype(out_ref.dtype)


def solve_step(meta, incident, summed, inverse, zmat=None, now=None, old=None):
    blocks, width, unused = inverse.shape
    count = 1 if zmat is None else zmat.shape[1]
    spec = pl.BlockSpec((1, width, width), lambda i, meta: (i * meta[1], 0, 0))
    twice = pl.BlockSpec((2, width, width), lambda i, meta: (i * meta[1], 0, 0))
    args, specs = [incident, summed, inverse], [twice, spec, twice]
    if zmat is not None:
        args += [zmat, now]
        specs += [
            pl.BlockSpec((2, count, width, width), lambda i, meta: (i * meta[1], 0, 0, 0)),
            pl.BlockSpec(now.shape, lambda i, meta: (0, 0, 0)),
        ]
    if old is not None:
        args.append(old)
        specs.append(spec)
    return pl.pallas_call(
        functools.partial(step_kernel, count, zmat is not None, old is not None),
        out_shape=jax.ShapeDtypeStruct((blocks // 2, width, width), jnp.bfloat16),
        grid_spec=pltpu.PrefetchScalarGridSpec(
            num_scalar_prefetch=1, grid=(blocks // 2,), in_specs=specs, out_specs=spec
        ),
        compiler_params=pltpu.CompilerParams(vmem_limit_bytes=32 * 1024 * 1024),
    )(meta, *args)


def unpack_kernel(meta, mine_ref, other_ref, out_ref):
    mine, other = mine_ref[0].astype(jnp.float32), other_ref[0].astype(jnp.float32)
    low = jnp.where(meta[0] == 0, mine, other)
    high = jnp.where(meta[0] == 0, other, mine)
    first, second = pack(low, high)
    out_ref[0] = first.astype(out_ref.dtype)
    out_ref[1] = second.astype(out_ref.dtype)


def unpack(meta, mine, other):
    count, width, unused = mine.shape
    spec = pl.BlockSpec((1, width, width), lambda i, meta: (i, 0, 0))
    return pl.pallas_call(
        unpack_kernel,
        out_shape=jax.ShapeDtypeStruct((2 * count, width, width), mine.dtype),
        grid_spec=pltpu.PrefetchScalarGridSpec(
            num_scalar_prefetch=1,
            grid=(count,),
            in_specs=[spec, spec],
            out_specs=pl.BlockSpec((2, width, width), lambda i, meta: (i, 0, 0)),
        ),
    )(meta, mine, other)


def swap_rows(lag, row):
    return lag, row ^ 1


def next_chip(lag, row):
    return lag, (row + 2 if row % 2 == 0 else row - 2)


def on_root(step):
    def target(lag, row):
        return (lag, row + step) if lag < CORES else None
    return target


def reduced(keep, extra):
    total = keep + send(extra, other_core)
    for move in (
        along_x(-1, lambda z, x: x % 2 == 1),
        along_x(-2, lambda z, x: x == 2),
        along_z(-1, lambda z, x: x == 0 and z % 2 == 1),
        along_z(-2, lambda z, x: x == 0 and z == 2),
    ):
        total = total + send(total.astype(jnp.bfloat16), move).astype(jnp.float32)
    return total


def spread(value, z_pos, x_pos):
    for move, got in (
        (along_z(2, lambda z, x: x == 0 and z == 0), (x_pos == 0) & (z_pos == 2)),
        (along_z(1, lambda z, x: x == 0 and z % 2 == 0), (x_pos == 0) & (z_pos % 2 == 1)),
        (along_x(2, lambda z, x: x == 0), x_pos == 2),
        (along_x(1, lambda z, x: x % 2 == 0), x_pos % 2 == 1),
    ):
        value = jnp.where(got, send(value, move), value)
    return value


def per_device(z_blocks, block_cols, history, incident, near_inverse):
    blocks, width, unused = near_inverse.shape
    zmat = z_blocks[0]
    count = zmat.shape[1]
    lag_pos = lax.axis_index("lag")
    row_pos = lax.axis_index("row")
    z_pos, x_pos, core = coords(lag_pos)
    root = (lag_pos < CORES).astype(jnp.int32)
    own = history[0].reshape(blocks, width, width)
    fields = incident.reshape(incident.shape[0], blocks, width, width)

    cols = block_cols[0].reshape(-1) - (row_pos - 1) * blocks
    group, inside = cols // blocks, cols % blocks
    even = row_pos % 2 == 0
    slot = jnp.where(group == 1, 0, jnp.where((group == 2) == even, 1, 2))
    flags = jnp.zeros((8,), jnp.int32).at[0].set(core).at[1].set(root)
    history_meta = jnp.concatenate([flags, slot * blocks + inside])

    def to_root(lag, row):
        return (lag ^ 1, row) if lag < CORES else None

    def third(lag, row):
        return (0, row) if lag == CORES else None

    def shared(lag, row):
        return (1, row) if lag == 0 else None

    def gathered(value):
        swapped = send(value, to_root)
        first = jnp.where(lag_pos == 0, value, swapped)
        second = jnp.where(lag_pos == 0, swapped, value)
        got = send(value, third)
        last = jnp.where(lag_pos == 0, got, send(got, shared))
        return first, second, last

    near = send(own, swap_rows)
    far = send(near, next_chip)
    past = jnp.concatenate([own, near, far], axis=0)

    z_lags = gathered(zmat)
    metas = [jnp.concatenate([flags, c]) for c in gathered(cols)]

    sums = []
    for step in range(4):
        keep, extra = history_partial(history_meta, zmat, past)
        sums.append(reduced(keep, extra))
        if step < 3:
            past = send(past, lambda lag, row: (lag + 1, row))

    def wide(value):
        below = send(value, on_root(1))
        above = send(value, on_root(-1))
        return jnp.concatenate([below, value, above], axis=0)

    c0 = wide(solve_step(metas[0], fields[0], sums[0], near_inverse))
    c1 = wide(solve_step(metas[0], fields[1], sums[1], near_inverse, z_lags[0], c0))
    old = lag_product(metas[1], z_lags[1], c0)
    c2 = wide(solve_step(metas[0], fields[2], sums[2], near_inverse, z_lags[0], c1, old))
    old = lag_product(metas[2], z_lags[2], c0)
    old = lag_product(metas[1], z_lags[1], c1, old)
    c3 = solve_step(metas[0], fields[3], sums[3], near_inverse, z_lags[0], c2, old)
    c3 = spread(c3, z_pos, x_pos)
    out = unpack(history_meta, c3, send(c3, other_core))
    return out.reshape(blocks * width, width)


def solution(mesh):
    return jax.shard_map(
        per_device,
        mesh=mesh,
        in_specs=(
            P("lag", "row", None, None, None),
            P("lag", "row", None),
            P("lag", "row", None),
            P(None, "row", None),
            P("row", None, None),
        ),
        out_specs=P("row", None),
        check_vma=False,
    )
```

time: 1370 us -> 292 us (0.21)
  the two profiles are of different devices: /device:TPU:1 before, /device:TPU:39 now
where the time goes in v1:
time: 292 us; the launch traced here: 290 us
  starting transfers between devices  144 us (49%)
  waiting for transfers between devices  96.5 us (33%)
  Pallas kernels  32.3 us (11%)
  other arithmetic  15.6 us (5%)
    ppermute x42, starting transfers between devices, send(): return lax.ppermute(value, AXES, pairs(lags, rows, target))  144 us
    ppermute x42, waiting for transfers between devices, send(): return lax.ppermute(value, AXES, pairs(lags, rows, target))  96.5 us
    pallas_call x4, Pallas kernels, history_partial(): pl.pallas_call(functools.partial(history_kernel, count), out_shape=(half,...  23 us
  transfers between devices with their start and end apart: 42, of which 11 were waited for; matrix products, arithmetic and copies ran while one was open for 5% of the time, Pallas kernels for 9%

profile of v1, /device:TPU:39, one launch (start us, length us, event | category | flops | bytes accessed | tf_op | source)
XLA Modules:
  0.0 290.0 jit_solution(15951359877096832108)
XLA Ops:
  0.0 10.6 %collective-permute-start.1 = (bf16[12,128,128]{2,1,0:T(8,128)(2,1)}, bf16[12,128,128]{2,1,0:T(8,128)(2,1)S(1)}, u32[]{:S(2)}, u32[]{:S(2)}) collective-permute-start(bf16[12,128,128]{2,1,0:T(8,128)(2,1)} %bitcast.15), channel_id=1, source_target_pairs={{0,1},{1,0},{2,3},{3,2},{4,5},{5,4},{6,7},{7,6},{8,9},{9,8},{10,11... | collective-permute-start | bytes 1179656 | tf_op jit(solution)/shard_map/ppermute | solution.py:35
  10.6 2.7 collective-permute-start.35
  13.3 0.7 broadcast_subtract_fusion
  16.3 3.5 %collective-permute-done.1 = bf16[12,128,128]{2,1,0:T(8,128)(2,1)S(1)} collective-permute-done((bf16[12,128,128]{2,1,0:T(8,128)(2,1)}, bf16[12,128,128]{2,1,0:T(8,128)(2,1)S(1)}, u32[]{:S(2)}, u32[]{:S(2)}) %collective-permute-start.1) | collective-permute-done | bytes 393248 | tf_op jit(solution)/shard_map/ppermute | solution.py:35
  19.8 2.3 collective-permute-start.2
  22.2 10.0 %collective-permute-done.2 = bf16[12,128,128]{2,1,0:T(8,128)(2,1)S(1)} collective-permute-done((bf16[12,128,128]{2,1,0:T(8,128)(2,1)S(1)}, bf16[12,128,128]{2,1,0:T(8,128)(2,1)S(1)}, u32[]{:S(2)}, u32[]{:S(2)}) %collective-permute-start.2) | collective-permute-done | bytes 393248 | tf_op jit(solution)/shard_map/ppermute | solution.py:35
  32.2 1.1 pad_maximum_fusion.past_ref
  33.3 5.7 %shard_map.58 = (f32[6,128,128]{2,1,0:T(8,128)S(1)}, f32[6,128,128]{2,1,0:T(8,128)S(1)}) custom-call(s32[140]{0:T(256)S(1)} %get-tuple-element.65.meta, bf16[12,11,128,128]{3,2,1,0:T(8,128)(2,1)} %bitcast.3.z_ref, bf16[36,128,128]{2,1,0:T(8,128)(2,1)S(1)} %pad_maximum_fusion.past_ref), custom_call_target="tpu_custom_call" | custom-call | flops 553648128 | bytes 4325376 | tf_op jit(solution)/shard_map/pallas_call | solution.py:97
  39.1 4.1 %collective-permute-start.22 = (f32[6,128,128]{2,1,0:T(8,128)S(1)}, f32[6,128,128]{2,1,0:T(8,128)S(1)}, u32[]{:S(2)}, u32[]{:S(2)}) collective-permute-start(f32[6,128,128]{2,1,0:T(8,128)S(1)} %get-tuple-element.44), channel_id=1, source_target_pairs={{0,16},{1,17},{2,18},{3,19},{4,20},{5,21},{6,22},{7,23},{8,24},{9,... | collective-permute-start | bytes 1179656 | tf_op jit(solution)/shard_map/ppermute | solution.py:35
  43.2 11.2 %collective-permute-start.3 = (bf16[36,128,128]{2,1,0:T(8,128)(2,1)S(1)}, bf16[36,128,128]{2,1,0:T(8,128)(2,1)S(1)}, u32[]{:S(2)}, u32[]{:S(2)}) collective-permute-start(bf16[36,128,128]{2,1,0:T(8,128)(2,1)S(1)} %pad_maximum_fusion.past_ref), channel_id=1, source_target_pairs={{0,16},{1,17},{2,18},{3,19},{4,20},{5,21},{6,22},{7,23},{8,24},{9,... | collective-permute-start | bytes 3538952 | tf_op jit(solution)/shard_map/ppermute | solution.py:35
  54.5 1.4 collective-permute-start.23
  56.0 2.6 collective-permute-done.23
  59.3 2.8 collective-permute-start.11
  62.2 0.7 collective-permute-start.25
  62.9 4.7 %collective-permute-done.3.past_ref = bf16[36,128,128]{2,1,0:T(8,128)(2,1)S(1)} collective-permute-done((bf16[36,128,128]{2,1,0:T(8,128)(2,1)S(1)}, bf16[36,128,128]{2,1,0:T(8,128)(2,1)S(1)}, u32[]{:S(2)}, u32[]{:S(2)}) %collective-permute-start.3) | collective-permute-done | bytes 1179680 | tf_op jit(solution)/shard_map/ppermute | solution.py:35
  67.6 5.7 %shard_map.57 = (f32[6,128,128]{2,1,0:T(8,128)S(1)}, f32[6,128,128]{2,1,0:T(8,128)S(1)}) custom-call(s32[140]{0:T(256)S(1)} %get-tuple-element.65.meta, bf16[12,11,128,128]{3,2,1,0:T(8,128)(2,1)} %bitcast.3.z_ref, bf16[36,128,128]{2,1,0:T(8,128)(2,1)S(1)} %collective-permute-done.3.past_ref), custom_call_target="tpu_custom_call" | custom-call | flops 553648128 | bytes 4325376 | tf_op jit(solution)/shard_map/pallas_call | solution.py:97
  73.3 2.1 collective-permute-start.17
  75.4 43.3 %collective-permute-start.4 = (bf16[36,128,128]{2,1,0:T(8,128)(2,1)S(1)}, bf16[36,128,128]{2,1,0:T(8,128)(2,1)S(1)}, u32[]{:S(2)}, u32[]{:S(2)}) collective-permute-start(bf16[36,128,128]{2,1,0:T(8,128)(2,1)S(1)} %collective-permute-done.3.past_ref), channel_id=1, source_target_pairs={{0,16},{1,17},{2,18},{3,19},{4,20},{5,21},{6,22},{7,23},{8,24},{9,... | collective-permute-start | bytes 3538952 | tf_op jit(solution)/shard_map/ppermute | solution.py:35
  118.9 0.7 collective-permute-start.26
  119.7 1.3 collective-permute-start.18
  121.8 0.7 collective-permute-start.28
  122.5 1.1 collective-permute-done.18
  124.3 0.7 collective-permute-start.19
  125.0 7.4 %collective-permute-done.4.past_ref = bf16[36,128,128]{2,1,0:T(8,128)(2,1)S(1)} collective-permute-done((bf16[36,128,128]{2,1,0:T(8,128)(2,1)S(1)}, bf16[36,128,128]{2,1,0:T(8,128)(2,1)S(1)}, u32[]{:S(2)}, u32[]{:S(2)}) %collective-permute-start.4) | collective-permute-done | bytes 1179680 | tf_op jit(solution)/shard_map/ppermute | solution.py:35
  132.4 7.5 %collective-permute-start.5 = (bf16[36,128,128]{2,1,0:T(8,128)(2,1)S(1)}, bf16[36,128,128]{2,1,0:T(8,128)(2,1)S(1)}, u32[]{:S(2)}, u32[]{:S(2)}) collective-permute-start(bf16[36,128,128]{2,1,0:T(8,128)(2,1)S(1)} %collective-permute-done.4.past_ref), channel_id=1, source_target_pairs={{0,16},{1,17},{2,18},{3,19},{4,20},{5,21},{6,22},{7,23},{8,24},{9,... | collective-permute-start | bytes 3538952 | tf_op jit(solution)/shard_map/ppermute | solution.py:35
  139.9 5.7 %shard_map.56 = (f32[6,128,128]{2,1,0:T(8,128)S(1)}, f32[6,128,128]{2,1,0:T(8,128)S(1)}) custom-call(s32[140]{0:T(256)S(1)} %get-tuple-element.65.meta, bf16[12,11,128,128]{3,2,1,0:T(8,128)(2,1)} %bitcast.3.z_ref, bf16[36,128,128]{2,1,0:T(8,128)(2,1)S(1)} %collective-permute-done.4.past_ref), custom_call_target="tpu_custom_call" | custom-call | flops 553648128 | bytes 4325376 | tf_op jit(solution)/shard_map/pallas_call | solution.py:97
  145.7 1.9 collective-permute-start.12
  147.7 2.7 collective-permute-start.36
  150.5 0.7 collective-permute-start.20
  151.3 12.5 %collective-permute-start.13 = (bf16[6,128,128]{2,1,0:T(8,128)(2,1)S(1)}, bf16[6,128,128]{2,1,0:T(8,128)(2,1)S(1)}, u32[]{:S(2)}, u32[]{:S(2)}) collective-permute-start(bf16[6,128,128]{2,1,0:T(8,128)(2,1)S(1)} %get-tuple-element.49), channel_id=1, source_target_pairs={{32,0},{33,1},{34,2},{35,3},{36,4},{37,5},{38,6},{39,7},{40,8},{41... | collective-permute-start | bytes 589832 | tf_op jit(solution)/shard_map/ppermute | solution.py:35
  164.6 3.5 %collective-permute-done.13 = bf16[6,128,128]{2,1,0:T(8,128)(2,1)S(1)} collective-permute-done((bf16[6,128,128]{2,1,0:T(8,128)(2,1)S(1)}, bf16[6,128,128]{2,1,0:T(8,128)(2,1)S(1)}, u32[]{:S(2)}, u32[]{:S(2)}) %collective-permute-start.13) | collective-permute-done | bytes 196640 | tf_op jit(solution)/shard_map/ppermute | solution.py:35
  168.1 0.7 collective-permute-start.14
  168.8 5.7 %shard_map.55 = (f32[6,128,128]{2,1,0:T(8,128)S(1)}, f32[6,128,128]{2,1,0:T(8,128)S(1)}) custom-call(s32[140]{0:T(256)S(1)} %get-tuple-element.65.meta, bf16[12,11,128,128]{3,2,1,0:T(8,128)(2,1)} %bitcast.3.z_ref, bf16[36,128,128]{2,1,0:T(8,128)(2,1)S(1)} %collective-permute-done.5.past_ref), custom_call_target="tpu_custom_call" | custom-call | flops 553648128 | bytes 4325376 | tf_op jit(solution)/shard_map/pallas_call | solution.py:97
  174.6 2.7 collective-permute-start.6
  177.5 0.7 collective-permute-start.15
  178.7 6.1 %collective-permute-start.7 = (bf16[6,128,128]{2,1,0:T(8,128)(2,1)S(1)}, bf16[6,128,128]{2,1,0:T(8,128)(2,1)S(1)}, u32[]{:S(2)}, u32[]{:S(2)}) collective-permute-start(bf16[6,128,128]{2,1,0:T(8,128)(2,1)S(1)} %get-tuple-element.51), channel_id=1, source_target_pairs={{32,0},{33,1},{34,2},{35,3},{36,4},{37,5},{38,6},{39,7},{40,8},{41... | collective-permute-start | bytes 589832 | tf_op jit(solution)/shard_map/ppermute | solution.py:35
  184.8 0.8 fusion.3
  185.6 1.3 collective-permute-start.16
  186.9 1.8 collective-permute-done.7
  188.7 0.7 fusion
  189.4 1.3 collective-permute-start.8
  190.7 4.1 %broadcast_select_fusion.1 = (bf16[12,11,128,128]{3,2,1,0:T(8,128)(2,1)S(1)}, bf16[12,11,128,128]{3,2,1,0:T(8,128)(2,1)S(1)}) fusion(bf16[12,11,128,128]{3,2,1,0:T(8,128)(2,1)} %collective-permute-done.11, pred[]{:T(512)S(6)} %eq.62, bf16[1,12,11,128,128]{4,3,2,1,0:T(8,128)(2,1)} %param.9), kind=kLoop, calls=%fused_computation.1 | loop fusion | flops 4325376 | bytes 17301504 | tf_op jit(solution)/shard_map/jit(_where)/select_n | solution.py:306
  195.5 0.8 collective-permute-start.30
  196.3 0.7 collective-permute-start.29
  197.7 1.0 fusion.10
  198.7 0.7 collective-permute-start.9
  199.4 1.0 convert_add_fusion.8.refs_1_
  200.5 0.7 shard_map.62
  201.2 0.7 collective-permute-start.32
  201.9 0.7 collective-permute-start.31
  202.6 1.0 fusion.1
  203.6 0.7 collective-permute-start.10
  204.4 1.0 convert_add_fusion.12.refs_1_
  205.5 2.7 broadcast_select_fusion.z_ref
  209.5 0.7 shard_map.65
  210.2 0.7 collective-permute-start.37
  210.9 0.7 collective-permute-start.38
  211.7 0.7 collective-permute-start.39
  212.4 1.3 collective-permute-start.40
  213.7 60.3 %collective-permute-done.40 = bf16[6,128,128]{2,1,0:T(8,128)(2,1)S(1)} collective-permute-done((bf16[6,128,128]{2,1,0:T(8,128)(2,1)S(1)}, bf16[6,128,128]{2,1,0:T(8,128)(2,1)S(1)}, u32[]{:S(2)}, u32[]{:S(2)}) %collective-permute-start.40) | collective-permute-done | bytes 196640 | tf_op jit(solution)/shard_map/ppermute | solution.py:35
  274.1 9.5 %collective-permute-start.41 = (bf16[6,128,128]{2,1,0:T(8,128)(2,1)S(1)}, bf16[6,128,128]{2,1,0:T(8,128)(2,1)S(1)}, u32[]{:S(2)}, u32[]{:S(2)}) collective-permute-start(bf16[6,128,128]{2,1,0:T(8,128)(2,1)S(1)} %broadcast_select_fusion.6.mine_ref), channel_id=1, source_target_pairs={{0,16},{1,17},{2,18},{3,19},{4,20},{5,21},{6,22},{7,23},{8,24},{9,... | collective-permute-start | bytes 589832 | tf_op jit(solution)/shard_map/ppermute | solution.py:35
  283.6 1.0 collective-permute-done.41.other_ref
  284.7 0.7 copy-done.6
  285.4 4.6 %shard_map.66 = bf16[12,128,128]{2,1,0:T(8,128)(2,1)} custom-call(s32[140]{0:T(256)} %copy-done.1, bf16[6,128,128]{2,1,0:T(8,128)(2,1)} %copy-done.5, bf16[6,128,128]{2,1,0:T(8,128)(2,1)} %copy-done.6), custom_call_target="tpu_custom_call" | custom-call | tf_op jit(solution)/shard_map/pallas_call | solution.py:227
  (85 shorter events, 9.6 us)
Async XLA Ops:
  0.0 19.8 %collective-permute-start.1 = (bf16[12,128,128]{2,1,0:T(8,128)(2,1)}, bf16[12,128,128]{2,1,0:T(8,128)(2,1)S(1)}, u32[]{:S(2)}, u32[]{:S(2)}) collective-permute-start(bf16[12,128,128]{2,1,0:T(8,128)(2,1)} %bitcast.15), channel_id=1, source_target_pairs={{0,1},{1,0},{2,3},{3,2},{4,5},{5,4},{6,7},{7,6},{8,9},{9,8},{10,11... | collective-permute-start | bytes 1179656 | tf_op jit(solution)/shard_map/ppermute | solution.py:35
  10.6 137.1 %collective-permute-start.35 = (bf16[12,11,128,128]{3,2,1,0:T(8,128)(2,1)}, bf16[12,11,128,128]{3,2,1,0:T(8,128)(2,1)}, u32[]{:S(2)}, u32[]{:S(2)}) collective-permute-start(bf16[12,11,128,128]{3,2,1,0:T(8,128)(2,1)} %bitcast.3.z_ref), channel_id=1, source_target_pairs={{32,0},{33,1},{34,2},{35,3},{36,4},{37,5},{38,6},{39,7},{40,8},{41... | collective-permute-start | bytes 12976136 | tf_op jit(solution)/shard_map/ppermute | solution.py:35
  14.2 7.9 %collective-permute-start = (s32[132]{0:T(256)S(1)}, s32[132]{0:T(256)S(1)}, u32[]{:S(2)}, u32[]{:S(2)}) collective-permute-start(s32[132]{0:T(256)S(1)} %sub.28), channel_id=1, source_target_pairs={{0,16},{1,17},{2,18},{3,19},{4,20},{5,21},{6,22},{7,23},{8,24},{9,... | collective-permute-start | bytes 1592 | tf_op jit(solution)/shard_map/ppermute | solution.py:35
  14.9 0.7 collective-permute-start.33
  15.6 6.5 %collective-permute-start.34 = (s32[132]{0:T(256)S(1)}, s32[132]{0:T(256)S(1)}, u32[]{:S(2)}, u32[]{:S(2)}) collective-permute-start(s32[132]{0:T(256)S(1)} %collective-permute-done.33), channel_id=1, source_target_pairs={{0,16},{1,17},{2,18},{3,19},{4,20},{5,21},{6,22},{7,23},{8,24},{9,... | collective-permute-start | bytes 1592 | tf_op jit(solution)/shard_map/ppermute | solution.py:35
  19.8 12.4 %collective-permute-start.2 = (bf16[12,128,128]{2,1,0:T(8,128)(2,1)S(1)}, bf16[12,128,128]{2,1,0:T(8,128)(2,1)S(1)}, u32[]{:S(2)}, u32[]{:S(2)}) collective-permute-start(bf16[12,128,128]{2,1,0:T(8,128)(2,1)S(1)} %collective-permute-done.1), channel_id=1, source_target_pairs={{0,2},{2,4},{3,1},{4,6},{5,3},{6,8},{7,5},{8,10},{9,7},{10,12},{11... | collective-permute-start | bytes 1179656 | tf_op jit(solution)/shard_map/ppermute | solution.py:35
  22.2 146.6 %copy-start.1 = (s32[140]{0:T(256)}, s32[140]{0:T(256)S(1)}, u32[]{:S(2)}) copy-start(s32[140]{0:T(256)S(1)} %get-tuple-element.65.meta) | copy-start | bytes 1684
  39.1 15.4 %collective-permute-start.22 = (f32[6,128,128]{2,1,0:T(8,128)S(1)}, f32[6,128,128]{2,1,0:T(8,128)S(1)}, u32[]{:S(2)}, u32[]{:S(2)}) collective-permute-start(f32[6,128,128]{2,1,0:T(8,128)S(1)} %get-tuple-element.44), channel_id=1, source_target_pairs={{0,16},{1,17},{2,18},{3,19},{4,20},{5,21},{6,22},{7,23},{8,24},{9,... | collective-permute-start | bytes 1179656 | tf_op jit(solution)/shard_map/ppermute | solution.py:35
  43.2 24.4 %collective-permute-start.3 = (bf16[36,128,128]{2,1,0:T(8,128)(2,1)S(1)}, bf16[36,128,128]{2,1,0:T(8,128)(2,1)S(1)}, u32[]{:S(2)}, u32[]{:S(2)}) collective-permute-start(bf16[36,128,128]{2,1,0:T(8,128)(2,1)S(1)} %pad_maximum_fusion.past_ref), channel_id=1, source_target_pairs={{0,16},{1,17},{2,18},{3,19},{4,20},{5,21},{6,22},{7,23},{8,24},{9,... | collective-permute-start | bytes 3538952 | tf_op jit(solution)/shard_map/ppermute | solution.py:35
  54.5 64.2 %copy-start.2 = (bf16[4,1536,128]{2,1,0:T(8,128)(2,1)S(1)}, bf16[4,1536,128]{2,1,0:T(8,128)(2,1)}, u32[]{:S(2)}) copy-start(bf16[4,1536,128]{2,1,0:T(8,128)(2,1)} %param.12) | copy-start | bytes 4718596
  54.5 4.0 %collective-permute-start.23 = (bf16[6,128,128]{2,1,0:T(8,128)(2,1)S(1)}, bf16[6,128,128]{2,1,0:T(8,128)(2,1)S(1)}, u32[]{:S(2)}, u32[]{:S(2)}) collective-permute-start(bf16[6,128,128]{2,1,0:T(8,128)(2,1)S(1)} %get-tuple-element.45), channel_id=1, source_target_pairs={{32,0},{33,1},{34,2},{35,3},{36,4},{37,5},{38,6},{39,7},{40,8},{41... | collective-permute-start | bytes 589832 | tf_op jit(solution)/shard_map/ppermute | solution.py:35
  58.6 3.5 %collective-permute-start.24 = (bf16[6,128,128]{2,1,0:T(8,128)(2,1)S(1)}, bf16[6,128,128]{2,1,0:T(8,128)(2,1)S(1)}, u32[]{:S(2)}, u32[]{:S(2)}) collective-permute-start(bf16[6,128,128]{2,1,0:T(8,128)(2,1)S(1)} %fusion.6), channel_id=1, source_target_pairs={{64,0},{65,1},{66,2},{67,3},{68,4},{69,5},{70,6},{71,7},{72,8},{73... | collective-permute-start | bytes 589832 | tf_op jit(solution)/shard_map/ppermute | solution.py:35
  59.3 131.4 %collective-permute-start.11 = (bf16[12,11,128,128]{3,2,1,0:T(8,128)(2,1)}, bf16[12,11,128,128]{3,2,1,0:T(8,128)(2,1)}, u32[]{:S(2)}, u32[]{:S(2)}) collective-permute-start(bf16[12,11,128,128]{3,2,1,0:T(8,128)(2,1)} %bitcast.3.z_ref), channel_id=1, source_target_pairs={{0,16},{1,17},{2,18},{3,19},{4,20},{5,21},{6,22},{7,23},{8,24},{9,... | collective-permute-start | bytes 12976136 | tf_op jit(solution)/shard_map/ppermute | solution.py:35
  62.2 56.6 %collective-permute-start.25 = (bf16[6,128,128]{2,1,0:T(8,128)(2,1)S(1)}, bf16[6,128,128]{2,1,0:T(8,128)(2,1)S(1)}, u32[]{:S(2)}, u32[]{:S(2)}) collective-permute-start(bf16[6,128,128]{2,1,0:T(8,128)(2,1)S(1)} %fusion.13), channel_id=1, source_target_pairs={{128,0},{129,1},{130,2},{131,3},{132,4},{133,5},{134,6},{135,7},{1... | collective-permute-start | bytes 589832 | tf_op jit(solution)/shard_map/ppermute | solution.py:35
  73.3 47.8 %copy-start = (f32[12,128,128]{2,1,0:T(8,128)S(1)}, f32[12,128,128]{2,1,0:T(8,128)}, u32[]{:S(2)}) copy-start(f32[12,128,128]{2,1,0:T(8,128)} %refs_2_.7) | copy-start | bytes 2359300
  73.3 46.3 %collective-permute-start.17 = (f32[6,128,128]{2,1,0:T(8,128)S(1)}, f32[6,128,128]{2,1,0:T(8,128)S(1)}, u32[]{:S(2)}, u32[]{:S(2)}) collective-permute-start(f32[6,128,128]{2,1,0:T(8,128)S(1)} %get-tuple-element.42), channel_id=1, source_target_pairs={{0,16},{1,17},{2,18},{3,19},{4,20},{5,21},{6,22},{7,23},{8,24},{9,... | collective-permute-start | bytes 1179656 | tf_op jit(solution)/shard_map/ppermute | solution.py:35
  75.4 57.0 %collective-permute-start.4 = (bf16[36,128,128]{2,1,0:T(8,128)(2,1)S(1)}, bf16[36,128,128]{2,1,0:T(8,128)(2,1)S(1)}, u32[]{:S(2)}, u32[]{:S(2)}) collective-permute-start(bf16[36,128,128]{2,1,0:T(8,128)(2,1)S(1)} %collective-permute-done.3.past_ref), channel_id=1, source_target_pairs={{0,16},{1,17},{2,18},{3,19},{4,20},{5,21},{6,22},{7,23},{8,24},{9,... | collective-permute-start | bytes 3538952 | tf_op jit(solution)/shard_map/ppermute | solution.py:35
  118.9 2.1 collective-permute-start.26
  119.7 3.9 %collective-permute-start.18 = (bf16[6,128,128]{2,1,0:T(8,128)(2,1)S(1)}, bf16[6,128,128]{2,1,0:T(8,128)(2,1)S(1)}, u32[]{:S(2)}, u32[]{:S(2)}) collective-permute-start(bf16[6,128,128]{2,1,0:T(8,128)(2,1)S(1)} %get-tuple-element.47), channel_id=1, source_target_pairs={{32,0},{33,1},{34,2},{35,3},{36,4},{37,5},{38,6},{39,7},{40,8},{41... | collective-permute-start | bytes 589832 | tf_op jit(solution)/shard_map/ppermute | solution.py:35
  121.8 2.5 collective-permute-start.28
  123.6 22.1 %collective-permute-start.27 = (bf16[6,128,128]{2,1,0:T(8,128)(2,1)S(1)}, bf16[6,128,128]{2,1,0:T(8,128)(2,1)S(1)}, u32[]{:S(2)}, u32[]{:S(2)}) collective-permute-start(bf16[6,128,128]{2,1,0:T(8,128)(2,1)S(1)} %shard_map.59), channel_id=1, source_target_pairs={{0,1},{1,2},{2,3},{3,4},{4,5},{5,6},{6,7},{7,8},{8,9},{9,10},{10,1... | collective-permute-start | bytes 589832 | tf_op jit(solution)/shard_map/ppermute | solution.py:35
  124.3 26.1 %collective-permute-start.19 = (bf16[6,128,128]{2,1,0:T(8,128)(2,1)S(1)}, bf16[6,128,128]{2,1,0:T(8,128)(2,1)S(1)}, u32[]{:S(2)}, u32[]{:S(2)}) collective-permute-start(bf16[6,128,128]{2,1,0:T(8,128)(2,1)S(1)} %fusion.4), channel_id=1, source_target_pairs={{64,0},{65,1},{66,2},{67,3},{68,4},{69,5},{70,6},{71,7},{72,8},{73... | collective-permute-start | bytes 589832 | tf_op jit(solution)/shard_map/ppermute | solution.py:35
  132.4 36.4 %collective-permute-start.5 = (bf16[36,128,128]{2,1,0:T(8,128)(2,1)S(1)}, bf16[36,128,128]{2,1,0:T(8,128)(2,1)S(1)}, u32[]{:S(2)}, u32[]{:S(2)}) collective-permute-start(bf16[36,128,128]{2,1,0:T(8,128)(2,1)S(1)} %collective-permute-done.4.past_ref), channel_id=1, source_target_pairs={{0,16},{1,17},{2,18},{3,19},{4,20},{5,21},{6,22},{7,23},{8,24},{9,... | collective-permute-start | bytes 3538952 | tf_op jit(solution)/shard_map/ppermute | solution.py:35
  145.7 5.5 %collective-permute-start.12 = (f32[6,128,128]{2,1,0:T(8,128)S(1)}, f32[6,128,128]{2,1,0:T(8,128)S(1)}, u32[]{:S(2)}, u32[]{:S(2)}) collective-permute-start(f32[6,128,128]{2,1,0:T(8,128)S(1)} %get-tuple-element.40), channel_id=1, source_target_pairs={{0,16},{1,17},{2,18},{3,19},{4,20},{5,21},{6,22},{7,23},{8,24},{9,... | collective-permute-start | bytes 1179656 | tf_op jit(solution)/shard_map/ppermute | solution.py:35
  147.7 57.7 %collective-permute-start.36 = (bf16[12,11,128,128]{3,2,1,0:T(8,128)(2,1)}, bf16[12,11,128,128]{3,2,1,0:T(8,128)(2,1)}, u32[]{:S(2)}, u32[]{:S(2)}) collective-permute-start(bf16[12,11,128,128]{3,2,1,0:T(8,128)(2,1)} %collective-permute-done.35), channel_id=1, source_target_pairs={{0,16},{1,17},{2,18},{3,19},{4,20},{5,21},{6,22},{7,23},{8,24},{9,... | collective-permute-start | bytes 12976136 | tf_op jit(solution)/shard_map/ppermute | solution.py:35
  150.5 13.2 %collective-permute-start.20 = (bf16[6,128,128]{2,1,0:T(8,128)(2,1)S(1)}, bf16[6,128,128]{2,1,0:T(8,128)(2,1)S(1)}, u32[]{:S(2)}, u32[]{:S(2)}) collective-permute-start(bf16[6,128,128]{2,1,0:T(8,128)(2,1)S(1)} %fusion.12), channel_id=1, source_target_pairs={{128,0},{129,1},{130,2},{131,3},{132,4},{133,5},{134,6},{135,7},{1... | collective-permute-start | bytes 589832 | tf_op jit(solution)/shard_map/ppermute | solution.py:35
  151.3 16.8 %collective-permute-start.13 = (bf16[6,128,128]{2,1,0:T(8,128)(2,1)S(1)}, bf16[6,128,128]{2,1,0:T(8,128)(2,1)S(1)}, u32[]{:S(2)}, u32[]{:S(2)}) collective-permute-start(bf16[6,128,128]{2,1,0:T(8,128)(2,1)S(1)} %get-tuple-element.49), channel_id=1, source_target_pairs={{32,0},{33,1},{34,2},{35,3},{36,4},{37,5},{38,6},{39,7},{40,8},{41... | collective-permute-start | bytes 589832 | tf_op jit(solution)/shard_map/ppermute | solution.py:35
  163.9 13.4 %collective-permute-start.21 = (bf16[6,128,128]{2,1,0:T(8,128)(2,1)S(1)}, bf16[6,128,128]{2,1,0:T(8,128)(2,1)S(1)}, u32[]{:S(2)}, u32[]{:S(2)}) collective-permute-start(bf16[6,128,128]{2,1,0:T(8,128)(2,1)S(1)} %fusion.5), channel_id=1, source_target_pairs={{256,0},{257,1},{258,2},{259,3},{260,4},{261,5},{262,6},{263,7},{2... | collective-permute-start | bytes 589832 | tf_op jit(solution)/shard_map/ppermute | solution.py:35
  168.1 9.3 %collective-permute-start.14 = (bf16[6,128,128]{2,1,0:T(8,128)(2,1)S(1)}, bf16[6,128,128]{2,1,0:T(8,128)(2,1)S(1)}, u32[]{:S(2)}, u32[]{:S(2)}) collective-permute-start(bf16[6,128,128]{2,1,0:T(8,128)(2,1)S(1)} %fusion.2), channel_id=1, source_target_pairs={{64,0},{65,1},{66,2},{67,3},{68,4},{69,5},{70,6},{71,7},{72,8},{73... | collective-permute-start | bytes 589832 | tf_op jit(solution)/shard_map/ppermute | solution.py:35
  174.6 4.0 %collective-permute-start.6 = (f32[6,128,128]{2,1,0:T(8,128)S(1)}, f32[6,128,128]{2,1,0:T(8,128)S(1)}, u32[]{:S(2)}, u32[]{:S(2)}) collective-permute-start(f32[6,128,128]{2,1,0:T(8,128)S(1)} %get-tuple-element.38), channel_id=1, source_target_pairs={{0,16},{1,17},{2,18},{3,19},{4,20},{5,21},{6,22},{7,23},{8,24},{9,... | collective-permute-start | bytes 1179656 | tf_op jit(solution)/shard_map/ppermute | solution.py:35
  177.5 7.3 %collective-permute-start.15 = (bf16[6,128,128]{2,1,0:T(8,128)(2,1)S(1)}, bf16[6,128,128]{2,1,0:T(8,128)(2,1)S(1)}, u32[]{:S(2)}, u32[]{:S(2)}) collective-permute-start(bf16[6,128,128]{2,1,0:T(8,128)(2,1)S(1)} %fusion.11), channel_id=1, source_target_pairs={{128,0},{129,1},{130,2},{131,3},{132,4},{133,5},{134,6},{135,7},{1... | collective-permute-start | bytes 589832 | tf_op jit(solution)/shard_map/ppermute | solution.py:35
  178.7 10.0 %collective-permute-start.7 = (bf16[6,128,128]{2,1,0:T(8,128)(2,1)S(1)}, bf16[6,128,128]{2,1,0:T(8,128)(2,1)S(1)}, u32[]{:S(2)}, u32[]{:S(2)}) collective-permute-start(bf16[6,128,128]{2,1,0:T(8,128)(2,1)S(1)} %get-tuple-element.51), channel_id=1, source_target_pairs={{32,0},{33,1},{34,2},{35,3},{36,4},{37,5},{38,6},{39,7},{40,8},{41... | collective-permute-start | bytes 589832 | tf_op jit(solution)/shard_map/ppermute | solution.py:35
  184.8 5.9 %copy-start.3 = (bf16[6,128,128]{2,1,0:T(8,128)(2,1)}, bf16[6,128,128]{2,1,0:T(8,128)(2,1)S(1)}, u32[]{:S(2)}) copy-start(bf16[6,128,128]{2,1,0:T(8,128)(2,1)S(1)} %collective-permute-done.15) | copy-start | bytes 589828
  185.6 13.8 %collective-permute-start.16 = (bf16[6,128,128]{2,1,0:T(8,128)(2,1)}, bf16[6,128,128]{2,1,0:T(8,128)(2,1)}, u32[]{:S(2)}, u32[]{:S(2)}) collective-permute-start(bf16[6,128,128]{2,1,0:T(8,128)(2,1)} %fusion.3), channel_id=1, source_target_pairs={{256,0},{257,1},{258,2},{259,3},{260,4},{261,5},{262,6},{263,7},{2... | collective-permute-start | bytes 589832 | tf_op jit(solution)/shard_map/ppermute | solution.py:35
  189.4 8.3 %collective-permute-start.8 = (bf16[6,128,128]{2,1,0:T(8,128)(2,1)}, bf16[6,128,128]{2,1,0:T(8,128)(2,1)}, u32[]{:S(2)}, u32[]{:S(2)}) collective-permute-start(bf16[6,128,128]{2,1,0:T(8,128)(2,1)} %fusion), channel_id=1, source_target_pairs={{64,0},{65,1},{66,2},{67,3},{68,4},{69,5},{70,6},{71,7},{72,8},{73... | collective-permute-start | bytes 589832 | tf_op jit(solution)/shard_map/ppermute | solution.py:35
  195.5 3.9 %copy-start.4 = (bf16[6,128,128]{2,1,0:T(8,128)(2,1)S(1)}, bf16[6,128,128]{2,1,0:T(8,128)(2,1)}, u32[]{:S(2)}) copy-start(bf16[6,128,128]{2,1,0:T(8,128)(2,1)} %copy-done.3) | copy-start | bytes 589828
  195.5 4.9 %collective-permute-start.30 = (bf16[6,128,128]{2,1,0:T(8,128)(2,1)S(1)}, bf16[6,128,128]{2,1,0:T(8,128)(2,1)S(1)}, u32[]{:S(2)}, u32[]{:S(2)}) collective-permute-start(bf16[6,128,128]{2,1,0:T(8,128)(2,1)S(1)} %shard_map.60), channel_id=1, source_target_pairs={{1,0},{2,1},{3,2},{4,3},{5,4},{6,5},{7,6},{8,7},{9,8},{10,9},{11,1... | collective-permute-start | bytes 589832 | tf_op jit(solution)/shard_map/ppermute | solution.py:35
  196.3 4.1 %collective-permute-start.29 = (bf16[6,128,128]{2,1,0:T(8,128)(2,1)S(1)}, bf16[6,128,128]{2,1,0:T(8,128)(2,1)S(1)}, u32[]{:S(2)}, u32[]{:S(2)}) collective-permute-start(bf16[6,128,128]{2,1,0:T(8,128)(2,1)S(1)} %shard_map.60), channel_id=1, source_target_pairs={{0,1},{1,2},{2,3},{3,4},{4,5},{5,6},{6,7},{7,8},{8,9},{9,10},{10,1... | collective-permute-start | bytes 589832 | tf_op jit(solution)/shard_map/ppermute | solution.py:35
  198.7 3.9 %collective-permute-start.9 = (bf16[6,128,128]{2,1,0:T(8,128)(2,1)S(1)}, bf16[6,128,128]{2,1,0:T(8,128)(2,1)S(1)}, u32[]{:S(2)}, u32[]{:S(2)}) collective-permute-start(bf16[6,128,128]{2,1,0:T(8,128)(2,1)S(1)} %fusion.10), channel_id=1, source_target_pairs={{128,0},{129,1},{130,2},{131,3},{132,4},{133,5},{134,6},{135,7},{1... | collective-permute-start | bytes 589832 | tf_op jit(solution)/shard_map/ppermute | solution.py:35
  201.2 3.1 %collective-permute-start.32 = (bf16[6,128,128]{2,1,0:T(8,128)(2,1)S(1)}, bf16[6,128,128]{2,1,0:T(8,128)(2,1)S(1)}, u32[]{:S(2)}, u32[]{:S(2)}) collective-permute-start(bf16[6,128,128]{2,1,0:T(8,128)(2,1)S(1)} %shard_map.62), channel_id=1, source_target_pairs={{1,0},{2,1},{3,2},{4,3},{5,4},{6,5},{7,6},{8,7},{9,8},{10,9},{11,1... | collective-permute-start | bytes 589832 | tf_op jit(solution)/shard_map/ppermute | solution.py:35
  201.9 2.4 collective-permute-start.31
  203.6 0.8 collective-permute-start.10
  210.2 0.7 collective-permute-start.37
  210.9 0.7 collective-permute-start.38
  211.7 0.7 collective-permute-start.39
  212.4 61.7 %collective-permute-start.40 = (bf16[6,128,128]{2,1,0:T(8,128)(2,1)S(1)}, bf16[6,128,128]{2,1,0:T(8,128)(2,1)S(1)}, u32[]{:S(2)}, u32[]{:S(2)}) collective-permute-start(bf16[6,128,128]{2,1,0:T(8,128)(2,1)S(1)} %broadcast_select_fusion.5), channel_id=1, source_target_pairs={{0,32},{1,33},{2,34},{3,35},{4,36},{5,37},{6,38},{7,39},{8,40},{9,... | collective-permute-start | bytes 589832 | tf_op jit(solution)/shard_map/ppermute | solution.py:35
  274.1 10.6 %copy-start.5 = (bf16[6,128,128]{2,1,0:T(8,128)(2,1)}, bf16[6,128,128]{2,1,0:T(8,128)(2,1)S(1)}, u32[]{:S(2)}) copy-start(bf16[6,128,128]{2,1,0:T(8,128)(2,1)S(1)} %broadcast_select_fusion.6.mine_ref) | copy-start | bytes 589828
  274.1 10.6 %collective-permute-start.41 = (bf16[6,128,128]{2,1,0:T(8,128)(2,1)S(1)}, bf16[6,128,128]{2,1,0:T(8,128)(2,1)S(1)}, u32[]{:S(2)}, u32[]{:S(2)}) collective-permute-start(bf16[6,128,128]{2,1,0:T(8,128)(2,1)S(1)} %broadcast_select_fusion.6.mine_ref), channel_id=1, source_target_pairs={{0,16},{1,17},{2,18},{3,19},{4,20},{5,21},{6,22},{7,23},{8,24},{9,... | collective-permute-start | bytes 589832 | tf_op jit(solution)/shard_map/ppermute | solution.py:35
  284.7 0.7 copy-start.6

commit v2 on v1

v2 whole, which is shorter than its diff:
```python
import functools

import jax
import jax.numpy as jnp
from jax import lax
from jax.experimental import pallas as pl
from jax.experimental.pallas import tpu as pltpu
from jax.sharding import PartitionSpec as P

CORES, XS = 2, 4
HALF = 64
AXES = ("lag", "row")


def coords(lag):
    return lag // (XS * CORES), lag // CORES % XS, lag % CORES


def lag_of(z, x, core):
    return (z * XS + x) * CORES + core


def pairs(lags, rows, target):
    out = []
    for lag in range(lags):
        for row in range(rows):
            goal = target(lag, row)
            if goal is not None and 0 <= goal[0] < lags and 0 <= goal[1] < rows:
                out.append((lag * rows + row, goal[0] * rows + goal[1]))
    return out


def send(value, target):
    lags, rows = lax.axis_size("lag"), lax.axis_size("row")
    return lax.ppermute(value, AXES, pairs(lags, rows, target))


def along_z(step, when):
    def target(lag, row):
        z, x, core = coords(lag)
        return (lag_of(z + step, x, core), row) if when(z, x) and z + step >= 0 else None
    return target


def along_x(step, when):
    def target(lag, row):
        z, x, core = coords(lag)
        return (lag_of(z, x + step, core), row) if when(z, x) else None
    return target


def other_core(lag, row):
    return lag ^ 1, row


def sparse_row(z_ref, row, tile, cols, count):
    left = jnp.concatenate([z_ref[row, j] for j in range(count)], axis=1)
    right = jnp.concatenate([tile(cols(j)) for j in range(count)], axis=0)
    return jnp.dot(left, right, preferred_element_type=jnp.float32)


def low_lanes(shape):
    return lax.broadcasted_iota(jnp.int32, shape, len(shape) - 1) < HALF


def pack(first, second):
    low = low_lanes(first.shape)
    return (
        jnp.where(low, first, pltpu.roll(second, HALF, 1)),
        jnp.where(low, pltpu.roll(first, HALF, 1), second),
    )


VMEM = pl.BlockSpec(memory_space=pltpu.VMEM)
SMEM = pl.BlockSpec(memory_space=pltpu.SMEM)
HBM = pl.BlockSpec(memory_space=pl.ANY)
CHUNKS = 3
CORE, ROOT, NEXT, HEAD = 0, 1, 2, 8


def chunk_copies(source, buffer, sems):
    size = source.shape[0] // CHUNKS
    return [
        pltpu.make_async_copy(
            source.at[pl.ds(c * size, size)], buffer.at[pl.ds(c * size, size)], sems.at[c]
        )
        for c in range(CHUNKS)
    ]


def z_scratch(zmat):
    return [pltpu.VMEM(zmat.shape, zmat.dtype), pltpu.SemaphoreType.DMA((CHUNKS,))]


def call(kernel, out_shape, in_specs, scratch, flops, *args):
    outs = len(out_shape) if isinstance(out_shape, tuple) else 0
    return pl.pallas_call(
        kernel,
        out_shape=out_shape,
        in_specs=in_specs,
        out_specs=(VMEM,) * outs if outs else VMEM,
        scratch_shapes=scratch,
        compiler_params=pltpu.CompilerParams(vmem_limit_bytes=40 * 1024 * 1024),
        cost_estimate=pl.CostEstimate(flops=flops, bytes_accessed=5 * 10 ** 6, transcendentals=0),
    )(*args)


def history_kernel(meta, z_ref, past_ref, keep_ref, send_ref, buffer, sems):
    count = z_ref.shape[1]
    copies = chunk_copies(z_ref, buffer, sems)
    for copy in copies:
        copy.start()
    groups = z_ref.shape[0] // CHUNKS
    for pair in range(z_ref.shape[0] // 2):
        if 2 * pair % groups == 0:
            copies[2 * pair // groups].wait()
        rows = []
        for row in (2 * pair, 2 * pair + 1):
            base = HEAD + row * count
            rows.append(
                sparse_row(buffer, row, lambda c: past_ref[c], lambda j: meta[base + j], count)
            )
        low, high = pack(*rows)
        keep_ref[pair] = jnp.where(meta[CORE] == 0, low, high)
        send_ref[pair] = jnp.where(meta[CORE] == 0, high, low)


def history_partial(meta, zmat, past):
    blocks, count, width, unused = zmat.shape
    half = jax.ShapeDtypeStruct((blocks // 2, width, width), jnp.float32)
    return call(
        history_kernel, (half, half), [SMEM, HBM, VMEM], z_scratch(zmat),
        2 * blocks * count * width ** 3, meta, zmat, past,
    )


def load_lag(first, meta, mine_ref, swapped_ref, buffer, sems):
    mine = chunk_copies(mine_ref, buffer, sems)
    swapped = chunk_copies(swapped_ref, buffer, sems)
    direct = (meta[CORE] == 0) == first

    @pl.when(direct)
    def _():
        for copy in mine:
            copy.start()

    @pl.when(jnp.logical_not(direct))
    def _():
        for copy in swapped:
            copy.start()

    return mine


def packed_rows(meta, buffer, now_ref, pair, count):
    rows = []
    for row in (2 * pair, 2 * pair + 1):
        base = HEAD + row * count

        def tile(col):
            both = now_ref[col // 2]
            mine = low_lanes(both.shape) == (col % 2 == 0)
            return jnp.where(mine, both, jnp.zeros_like(both))

        total = sparse_row(buffer, row, tile, lambda j: meta[base + j], count)
        rows.append(total + pltpu.roll(total, HALF, 1))
    return jnp.where(low_lanes(rows[0].shape), rows[0], rows[1])


def lag_kernel(first, flag, meta, mine_ref, swapped_ref, now_ref, *rest):
    more, (out_ref, buffer, sems) = rest[:-3], rest[-3:]
    blocks, count = mine_ref.shape[0], mine_ref.shape[1]

    @pl.when(meta[flag] != 0)
    def _():
        copies = load_lag(first, meta, mine_ref, swapped_ref, buffer, sems)
        for copy in copies:
            copy.wait()
        for pair in range(blocks // 2):
            total = packed_rows(meta, buffer, now_ref, pair, count)
            for ref in more:
                total = total + ref[pair].astype(jnp.float32)
            out_ref[pair] = total.astype(out_ref.dtype)


def lag_product(first, flag, dtype, meta, mine, swapped, now, *more):
    blocks, count, width, unused = mine.shape
    return call(
        functools.partial(lag_kernel, first, flag),
        jax.ShapeDtypeStruct((blocks // 2, width, width), dtype),
        [SMEM, HBM, HBM, VMEM] + [VMEM] * len(more), z_scratch(mine),
        2 * blocks * count * width ** 3, meta, mine, swapped, now, *more,
    )


def step_kernel(product, old, meta, incident_ref, summed_ref, inverse_ref, *refs):
    refs = list(refs)
    if product:
        buffer, sems = refs[-2:]
        refs = refs[:-2]
    out_ref = refs.pop()

    @pl.when(meta[ROOT] != 0)
    def _():
        if product:
            copies = load_lag(True, meta, refs[0], refs[1], buffer, sems)
            groups = buffer.shape[0] // CHUNKS
        for pair in range(summed_ref.shape[0]):
            low, high = pack(*(incident_ref[2 * pair + p].astype(jnp.float32) for p in range(2)))
            driven = jnp.where(meta[CORE] == 0, low, high) - summed_ref[pair]
            if old:
                driven = driven - refs[-1][pair]
            if product:
                if 2 * pair % groups == 0:
                    copies[2 * pair // groups].wait()
                driven = driven - packed_rows(meta, buffer, refs[2], pair, buffer.shape[1])
            solved = [
                jnp.dot(
                    inverse_ref[2 * pair + p], driven,
                    precision=lax.Precision.HIGHEST, preferred_element_type=jnp.float32,
                )
                for p in range(2)
            ]
            out_ref[pair] = jnp.where(low_lanes(driven.shape), *solved).astype(out_ref.dtype)


def solve_step(meta, incident, summed, inverse, mine=None, swapped=None, now=None, old=None):
    blocks, width, unused = inverse.shape
    args, specs, scratch = [meta, incident, summed, inverse], [SMEM, VMEM, VMEM, VMEM], []
    if mine is not None:
        args += [mine, swapped, now]
        specs += [HBM, HBM, VMEM]
        scratch = z_scratch(mine)
    if old is not None:
        args.append(old)
        specs.append(VMEM)
    return call(
        functools.partial(step_kernel, mine is not None, old is not None),
        jax.ShapeDtypeStruct((blocks // 2, width, width), jnp.bfloat16),
        specs, scratch, 10 ** 9, *args,
    )


def unpack_kernel(meta, mine_ref, other_ref, out_ref):
    for pair in range(mine_ref.shape[0]):
        mine, other = mine_ref[pair].astype(jnp.float32), other_ref[pair].astype(jnp.float32)
        low = jnp.where(meta[CORE] == 0, mine, other)
        high = jnp.where(meta[CORE] == 0, other, mine)
        first, second = pack(low, high)
        out_ref[2 * pair] = first.astype(out_ref.dtype)
        out_ref[2 * pair + 1] = second.astype(out_ref.dtype)


def unpack(meta, mine, other):
    count, width, unused = mine.shape
    return call(
        unpack_kernel, jax.ShapeDtypeStruct((2 * count, width, width), mine.dtype),
        [SMEM, VMEM, VMEM], [], 10 ** 6, meta, mine, other,
    )


def swap_rows(lag, row):
    return lag, row ^ 1


def next_chip(lag, row):
    return lag, (row + 2 if row % 2 == 0 else row - 2)


def on_root(step):
    def target(lag, row):
        return (lag, row + step) if lag < CORES else None
    return target


def reduced(keep, extra):
    total = keep + send(extra, other_core)
    for move in (
        along_x(-1, lambda z, x: x % 2 == 1),
        along_x(-2, lambda z, x: x == 2),
        along_z(-1, lambda z, x: x == 0 and z % 2 == 1),
        along_z(-2, lambda z, x: x == 0 and z == 2),
    ):
        total = total + send(total.astype(jnp.bfloat16), move).astype(jnp.float32)
    return total


def spread(value, z_pos, x_pos):
    for move, got in (
        (along_z(2, lambda z, x: x == 0 and z == 0), (x_pos == 0) & (z_pos == 2)),
        (along_z(1, lambda z, x: x == 0 and z % 2 == 0), (x_pos == 0) & (z_pos % 2 == 1)),
        (along_x(2, lambda z, x: x == 0), x_pos == 2),
        (along_x(1, lambda z, x: x % 2 == 0), x_pos % 2 == 1),
    ):
        value = jnp.where(got, send(value, move), value)
    return value


def per_device(z_blocks, block_cols, history, incident, near_inverse):
    blocks, width, unused = near_inverse.shape
    zmat = z_blocks[0]
    lag_pos = lax.axis_index("lag")
    row_pos = lax.axis_index("row")
    z_pos, x_pos, core = coords(lag_pos)
    own = history[0].reshape(blocks, width, width)
    fields = [f.reshape(blocks, width, width) for f in incident]

    cols = block_cols[0].reshape(-1) - (row_pos - 1) * blocks
    group, inside = cols // blocks, cols % blocks
    even = row_pos % 2 == 0
    slot = jnp.where(group == 1, 0, jnp.where((group == 2) == even, 1, 2))
    chip = lag_pos // CORES
    flags = jnp.stack([core, chip == 0, chip == 1] + [0] * (HEAD - 3)).astype(jnp.int32)
    history_meta = jnp.concatenate([flags, slot * blocks + inside])

    def first_chips(lag, row):
        return (lag ^ 1, row) if lag < 2 * CORES else None

    near = send(own, swap_rows)
    swapped_cols = send(cols, first_chips)
    swapped = send(zmat, first_chips)
    far = send(near, next_chip)
    past = jnp.concatenate([own, near, far], axis=0)
    first_meta = jnp.concatenate([flags, jnp.where(core == 0, cols, swapped_cols)])
    second_meta = jnp.concatenate([flags, jnp.where(core == 0, swapped_cols, cols)])

    sums = []
    for step in range(4):
        keep, extra = history_partial(history_meta, zmat, past)
        sums.append(reduced(keep, extra))
        if step < 3:
            past = send(past, lambda lag, row: (lag + 1, row))

    def wide(value):
        below = send(value, on_root(1))
        above = send(value, on_root(-1))
        return jnp.concatenate([below, value, above], axis=0)

    lags = (zmat, swapped)
    c0 = wide(solve_step(first_meta, fields[0], sums[0], near_inverse))
    third = send(c0, along_x(1, lambda z, x: z == 0 and x == 0))
    third = lag_product(True, NEXT, jnp.bfloat16, first_meta, *lags, third)
    third = send(third, along_x(-1, lambda z, x: z == 0 and x == 1))
    c1 = wide(solve_step(first_meta, fields[1], sums[1], near_inverse, *lags, c0))
    old = lag_product(False, ROOT, jnp.float32, second_meta, *lags, c0)
    c2 = wide(solve_step(first_meta, fields[2], sums[2], near_inverse, *lags, c1, old))
    old = lag_product(False, ROOT, jnp.float32, second_meta, *lags, c1, third)
    c3 = solve_step(first_meta, fields[3], sums[3], near_inverse, *lags, c2, old)
    c3 = spread(c3, z_pos, x_pos)
    out = unpack(history_meta, c3, send(c3, other_core))
    return out.reshape(blocks * width, width)


def solution(mesh):
    return jax.shard_map(
        per_device,
        mesh=mesh,
        in_specs=(
            P("lag", "row", None, None, None),
            P("lag", "row", None),
            P("lag", "row", None),
            P(None, "row", None),
            P("row", None, None),
        ),
        out_specs=P("row", None),
        check_vma=False,
    )
```

time: 292 us -> 263 us (0.901)
  starting transfers between devices: 144 us -> 117 us
  Pallas kernels: 32.3 us -> 23.9 us
  waiting for transfers between devices: 96.5 us -> 104 us
    ppermute x42 -> x40, starting transfers between devices: 144 us -> 117 us  [send(): return lax.ppermute(value, AXES, pairs(lags, rows, target))]
    pallas_call x12, Pallas kernels: 32.3 us -> 23.9 us  [call(): pl.pallas_call(kernel, out_shape=out_shape, in_specs=in_specs, out_specs=...]
    ppermute x42 -> x40, waiting for transfers between devices: 96.5 us -> 104 us  [send(): return lax.ppermute(value, AXES, pairs(lags, rows, target))]
    select_n x4 -> x1, other arithmetic: 6.82 us -> 0.58 us  [per_device(): jnp.where(core == 0, swapped_cols, cols)]
    convert_element_type x16, other arithmetic: 4.28 us -> 7.37 us  [reduced(): total = total + send(total.astype(jnp.bfloat16), move).astype(jnp.float32)]
  transfers between devices with their start and end apart: 42 -> 40, of which waited for: 11 -> 7; matrix products, arithmetic and copies ran while one was open for 5% -> 5% of each run, Pallas kernels for 9% -> 7%
where the time goes in v2:
time: 263 us; the launch traced here: 262 us
  starting transfers between devices  117 us (44%)
  waiting for transfers between devices  104 us (40%)
  Pallas kernels  23.9 us (9%)
  other arithmetic  13.9 us (5%)
    ppermute x40, starting transfers between devices, send(): return lax.ppermute(value, AXES, pairs(lags, rows, target))  117 us
    ppermute x40, waiting for transfers between devices, send(): return lax.ppermute(value, AXES, pairs(lags, rows, target))  104 us
    pallas_call x12, Pallas kernels, call(): pl.pallas_call(kernel, out_shape=out_shape, in_specs=in_specs, out_specs=...  23.9 us
    convert_element_type x16, other arithmetic, reduced(): total = total + send(total.astype(jnp.bfloat16), move).astype(jnp.float32)  7.37 us
  transfers between devices with their start and end apart: 40, of which 7 were waited for; matrix products, arithmetic and copies ran while one was open for 5% of the time, Pallas kernels for 7%

profile of v2, /device:TPU:39, one launch (start us, length us, event | category | flops | bytes accessed | tf_op | source)
XLA Modules:
  0.0 262.0 jit_solution(6374792004329700331)
XLA Ops:
  0.0 10.6 %collective-permute-start.1 = (bf16[12,128,128]{2,1,0:T(8,128)(2,1)}, bf16[12,128,128]{2,1,0:T(8,128)(2,1)S(1)}, u32[]{:S(2)}, u32[]{:S(2)}) collective-permute-start(bf16[12,128,128]{2,1,0:T(8,128)(2,1)} %bitcast.14), channel_id=1, source_target_pairs={{0,1},{1,0},{2,3},{3,2},{4,5},{5,4},{6,7},{7,6},{8,9},{9,8},{10,11... | collective-permute-start | bytes 1179656 | tf_op jit(solution)/shard_map/ppermute | solution.py:35
  10.6 9.1 %collective-permute-done.1 = bf16[12,128,128]{2,1,0:T(8,128)(2,1)S(1)} collective-permute-done((bf16[12,128,128]{2,1,0:T(8,128)(2,1)}, bf16[12,128,128]{2,1,0:T(8,128)(2,1)S(1)}, u32[]{:S(2)}, u32[]{:S(2)}) %collective-permute-start.1) | collective-permute-done | bytes 393248 | tf_op jit(solution)/shard_map/ppermute | solution.py:35
  19.8 2.3 collective-permute-start.2
  22.1 0.7 broadcast_subtract_fusion
  24.3 7.9 %collective-permute-done.2 = bf16[12,128,128]{2,1,0:T(8,128)(2,1)S(1)} collective-permute-done((bf16[12,128,128]{2,1,0:T(8,128)(2,1)S(1)}, bf16[12,128,128]{2,1,0:T(8,128)(2,1)S(1)}, u32[]{:S(2)}, u32[]{:S(2)}) %collective-permute-start.2) | collective-permute-done | bytes 393248 | tf_op jit(solution)/shard_map/ppermute | solution.py:35
  32.2 1.1 pad_maximum_fusion.past_ref
  33.3 3.8 %shard_map.58 = (f32[6,128,128]{2,1,0:T(8,128)S(1)}, f32[6,128,128]{2,1,0:T(8,128)S(1)}) custom-call(s32[140]{0:T(256)S(1)} %concatenate.24.meta, bf16[12,11,128,128]{3,2,1,0:T(8,128)(2,1)} %bitcast.4.z_ref.refs_0_.mine_ref, bf16[36,128,128]{2,1,0:T(8,128)(2,1)S(1)} %pad_maximum_fusion.past_ref), custom_call_target="tpu_custom_call" | custom-call | flops 553648128 | bytes 5000000 | tf_op jit(solution)/shard_map/pallas_call | solution.py:97
  37.1 4.1 %collective-permute-start.22 = (f32[6,128,128]{2,1,0:T(8,128)S(1)}, f32[6,128,128]{2,1,0:T(8,128)S(1)}, u32[]{:S(2)}, u32[]{:S(2)}) collective-permute-start(f32[6,128,128]{2,1,0:T(8,128)S(1)} %get-tuple-element.20), channel_id=1, source_target_pairs={{0,16},{1,17},{2,18},{3,19},{4,20},{5,21},{6,22},{7,23},{8,24},{9,... | collective-permute-start | bytes 1179656 | tf_op jit(solution)/shard_map/ppermute | solution.py:35
  41.2 1.3 collective-permute-done.22
  42.6 2.5 collective-permute-start.23
  45.1 10.4 %collective-permute-start.3 = (bf16[36,128,128]{2,1,0:T(8,128)(2,1)S(1)}, bf16[36,128,128]{2,1,0:T(8,128)(2,1)}, u32[]{:S(2)}, u32[]{:S(2)}) collective-permute-start(bf16[36,128,128]{2,1,0:T(8,128)(2,1)S(1)} %pad_maximum_fusion.past_ref), channel_id=1, source_target_pairs={{0,16},{1,17},{2,18},{3,19},{4,20},{5,21},{6,22},{7,23},{8,24},{9,... | collective-permute-start | bytes 3538952 | tf_op jit(solution)/shard_map/ppermute | solution.py:35
  55.6 0.7 collective-permute-start.24
  56.3 2.7 %collective-permute-start.11 = (bf16[12,11,128,128]{3,2,1,0:T(8,128)(2,1)}, bf16[12,11,128,128]{3,2,1,0:T(8,128)(2,1)}, u32[]{:S(2)}, u32[]{:S(2)}) collective-permute-start(bf16[12,11,128,128]{3,2,1,0:T(8,128)(2,1)} %bitcast.4.z_ref.refs_0_.mine_ref), channel_id=1, source_target_pairs={{0,16},{1,17},{2,18},{3,19},{4,20},{5,21},{6,22},{7,23},{8,24},{9,... | collective-permute-start | bytes 12976136 | tf_op jit(solution)/shard_map/ppermute | solution.py:35
  60.4 0.8 fusion.7
  61.2 1.5 collective-permute-start.26
  62.7 8.0 %collective-permute-done.3.past_ref = bf16[36,128,128]{2,1,0:T(8,128)(2,1)} collective-permute-done((bf16[36,128,128]{2,1,0:T(8,128)(2,1)S(1)}, bf16[36,128,128]{2,1,0:T(8,128)(2,1)}, u32[]{:S(2)}, u32[]{:S(2)}) %collective-permute-start.3) | collective-permute-done | bytes 1179680 | tf_op jit(solution)/shard_map/ppermute | solution.py:35
  70.7 12.0 %collective-permute-start.4 = (bf16[36,128,128]{2,1,0:T(8,128)(2,1)}, bf16[36,128,128]{2,1,0:T(8,128)(2,1)S(1)}, u32[]{:S(2)}, u32[]{:S(2)}) collective-permute-start(bf16[36,128,128]{2,1,0:T(8,128)(2,1)} %collective-permute-done.3.past_ref), channel_id=1, source_target_pairs={{0,16},{1,17},{2,18},{3,19},{4,20},{5,21},{6,22},{7,23},{8,24},{9,... | collective-permute-start | bytes 3538952 | tf_op jit(solution)/shard_map/ppermute | solution.py:35
  82.7 5.2 %shard_map.57 = (f32[6,128,128]{2,1,0:T(8,128)S(1)}, f32[6,128,128]{2,1,0:T(8,128)}) custom-call(s32[140]{0:T(256)S(1)} %concatenate.24.meta, bf16[12,11,128,128]{3,2,1,0:T(8,128)(2,1)} %bitcast.4.z_ref.refs_0_.mine_ref, bf16[36,128,128]{2,1,0:T(8,128)(2,1)} %collective-permute-done.3.past_ref), custom_call_target="tpu_custom_call" | custom-call | flops 553648128 | bytes 5000000 | tf_op jit(solution)/shard_map/pallas_call | solution.py:97
  88.0 1.9 collective-permute-start.17
  90.1 1.4 convert_add_fusion.summed_ref
  91.6 1.2 shard_map.59
  92.8 1.3 collective-permute-start.28
  94.2 1.3 collective-permute-start.27
  95.5 1.9 fusion.15
  97.4 2.0 collective-permute-start.18
  99.4 4.5 %shard_map.56 = (f32[6,128,128]{2,1,0:T(8,128)S(1)}, f32[6,128,128]{2,1,0:T(8,128)}) custom-call(s32[140]{0:T(256)S(1)} %concatenate.24.meta, bf16[12,11,128,128]{3,2,1,0:T(8,128)(2,1)} %bitcast.4.z_ref.refs_0_.mine_ref, bf16[36,128,128]{2,1,0:T(8,128)(2,1)S(1)} %collective-permute-done.4.past_ref), custom_call_target="tpu_custom_call" | custom-call | flops 553648128 | bytes 5000000 | tf_op jit(solution)/shard_map/pallas_call | solution.py:97
  103.9 2.4 collective-permute-start.12
  106.3 0.7 concatenate.29.meta
  107.1 1.2 pad_maximum_fusion.1.refs_2_.now_ref
  108.3 0.7 collective-permute-start.33
  109.0 1.0 fusion.4
  110.0 0.7 collective-permute-start.19
  110.7 6.8 %collective-permute-start.5 = (bf16[36,128,128]{2,1,0:T(8,128)(2,1)S(1)}, bf16[36,128,128]{2,1,0:T(8,128)(2,1)S(1)}, u32[]{:S(2)}, u32[]{:S(2)}) collective-permute-start(bf16[36,128,128]{2,1,0:T(8,128)(2,1)S(1)} %collective-permute-done.4.past_ref), channel_id=1, source_target_pairs={{0,16},{1,17},{2,18},{3,19},{4,20},{5,21},{6,22},{7,23},{8,24},{9,... | collective-permute-start | bytes 3538952 | tf_op jit(solution)/shard_map/ppermute | solution.py:35
  117.5 1.1 fusion.16
  118.5 15.8 %collective-permute-start.13 = (bf16[6,128,128]{2,1,0:T(8,128)(2,1)S(1)}, bf16[6,128,128]{2,1,0:T(8,128)(2,1)S(1)}, u32[]{:S(2)}, u32[]{:S(2)}) collective-permute-start(bf16[6,128,128]{2,1,0:T(8,128)(2,1)S(1)} %get-tuple-element.25), channel_id=1, source_target_pairs={{32,0},{33,1},{34,2},{35,3},{36,4},{37,5},{38,6},{39,7},{40,8},{41... | collective-permute-start | bytes 589832 | tf_op jit(solution)/shard_map/ppermute | solution.py:35
  134.3 1.0 fusion.12
  135.3 0.7 collective-permute-start.20
  136.0 2.0 collective-permute-done.13
  138.0 0.7 collective-permute-start.14
  138.7 1.0 fusion.5
  139.7 0.7 collective-permute-start.21
  140.5 0.7 collective-permute-start.15
  141.2 3.8 %shard_map.55 = (f32[6,128,128]{2,1,0:T(8,128)S(1)}, f32[6,128,128]{2,1,0:T(8,128)S(1)}) custom-call(s32[140]{0:T(256)S(1)} %concatenate.24.meta, bf16[12,11,128,128]{3,2,1,0:T(8,128)(2,1)} %bitcast.4.z_ref.refs_0_.mine_ref, bf16[36,128,128]{2,1,0:T(8,128)(2,1)S(1)} %collective-permute-done.5.past_ref), custom_call_target="tpu_custom_call" | custom-call | flops 553648128 | bytes 5000000 | tf_op jit(solution)/shard_map/pallas_call | solution.py:97
  145.0 10.7 %collective-permute-start.6 = (f32[6,128,128]{2,1,0:T(8,128)S(1)}, f32[6,128,128]{2,1,0:T(8,128)S(1)}, u32[]{:S(2)}, u32[]{:S(2)}) collective-permute-start(f32[6,128,128]{2,1,0:T(8,128)S(1)} %get-tuple-element.14), channel_id=1, source_target_pairs={{0,16},{1,17},{2,18},{3,19},{4,20},{5,21},{6,22},{7,23},{8,24},{9,... | collective-permute-start | bytes 1179656 | tf_op jit(solution)/shard_map/ppermute | solution.py:35
  155.6 1.0 convert_add_fusion.4.summed_ref
  156.8 0.7 collective-permute-start.16
  157.6 3.7 %collective-permute-start.7 = (bf16[6,128,128]{2,1,0:T(8,128)(2,1)S(1)}, bf16[6,128,128]{2,1,0:T(8,128)(2,1)S(1)}, u32[]{:S(2)}, u32[]{:S(2)}) collective-permute-start(bf16[6,128,128]{2,1,0:T(8,128)(2,1)S(1)} %get-tuple-element.27), channel_id=1, source_target_pairs={{32,0},{33,1},{34,2},{35,3},{36,4},{37,5},{38,6},{39,7},{40,8},{41... | collective-permute-start | bytes 589832 | tf_op jit(solution)/shard_map/ppermute | solution.py:35
  161.2 0.8 shard_map.60
  162.0 0.7 collective-permute-start.30
  162.7 0.7 collective-permute-start.29
  164.0 0.7 collective-permute-start.34
  165.3 0.7 collective-permute-start.8
  166.2 0.7 collective-permute-start.9
  167.6 0.7 collective-permute-start.32
  168.3 0.7 collective-permute-start.31
  169.8 0.8 shard_map.64.refs_3_
  171.4 0.7 collective-permute-start.35
  172.2 0.7 collective-permute-start.36
  172.9 0.7 collective-permute-start.37
  173.6 1.3 collective-permute-start.38
  175.0 75.0 %collective-permute-done.38 = bf16[6,128,128]{2,1,0:T(8,128)(2,1)S(1)} collective-permute-done((bf16[6,128,128]{2,1,0:T(8,128)(2,1)S(1)}, bf16[6,128,128]{2,1,0:T(8,128)(2,1)S(1)}, u32[]{:S(2)}, u32[]{:S(2)}) %collective-permute-start.38) | collective-permute-done | bytes 196640 | tf_op jit(solution)/shard_map/ppermute | solution.py:35
  250.0 9.5 %collective-permute-start.39 = (bf16[6,128,128]{2,1,0:T(8,128)(2,1)S(1)}, bf16[6,128,128]{2,1,0:T(8,128)(2,1)S(1)}, u32[]{:S(2)}, u32[]{:S(2)}) collective-permute-start(bf16[6,128,128]{2,1,0:T(8,128)(2,1)S(1)} %broadcast_select_fusion.3.mine_ref), channel_id=1, source_target_pairs={{0,16},{1,17},{2,18},{3,19},{4,20},{5,21},{6,22},{7,23},{8,24},{9,... | collective-permute-start | bytes 589832 | tf_op jit(solution)/shard_map/ppermute | solution.py:35
  259.5 1.0 collective-permute-done.39.other_ref
  260.5 1.5 shard_map.66
  (83 shorter events, 7.3 us)
Async XLA Ops:
  0.0 19.8 %collective-permute-start.1 = (bf16[12,128,128]{2,1,0:T(8,128)(2,1)}, bf16[12,128,128]{2,1,0:T(8,128)(2,1)S(1)}, u32[]{:S(2)}, u32[]{:S(2)}) collective-permute-start(bf16[12,128,128]{2,1,0:T(8,128)(2,1)} %bitcast.14), channel_id=1, source_target_pairs={{0,1},{1,0},{2,3},{3,2},{4,5},{5,4},{6,7},{7,6},{8,9},{9,8},{10,11... | collective-permute-start | bytes 1179656 | tf_op jit(solution)/shard_map/ppermute | solution.py:35
  19.8 12.4 %collective-permute-start.2 = (bf16[12,128,128]{2,1,0:T(8,128)(2,1)S(1)}, bf16[12,128,128]{2,1,0:T(8,128)(2,1)S(1)}, u32[]{:S(2)}, u32[]{:S(2)}) collective-permute-start(bf16[12,128,128]{2,1,0:T(8,128)(2,1)S(1)} %collective-permute-done.1), channel_id=1, source_target_pairs={{0,2},{2,4},{3,1},{4,6},{5,3},{6,8},{7,5},{8,10},{9,7},{10,12},{11... | collective-permute-start | bytes 1179656 | tf_op jit(solution)/shard_map/ppermute | solution.py:35
  23.0 0.7 collective-permute-start
  37.1 5.4 %collective-permute-start.22 = (f32[6,128,128]{2,1,0:T(8,128)S(1)}, f32[6,128,128]{2,1,0:T(8,128)S(1)}, u32[]{:S(2)}, u32[]{:S(2)}) collective-permute-start(f32[6,128,128]{2,1,0:T(8,128)S(1)} %get-tuple-element.20), channel_id=1, source_target_pairs={{0,16},{1,17},{2,18},{3,19},{4,20},{5,21},{6,22},{7,23},{8,24},{9,... | collective-permute-start | bytes 1179656 | tf_op jit(solution)/shard_map/ppermute | solution.py:35
  42.6 18.6 %copy-start.4 = (f32[6,128,128]{2,1,0:T(8,128)}, f32[6,128,128]{2,1,0:T(8,128)S(1)}, u32[]{:S(2)}) copy-start(f32[6,128,128]{2,1,0:T(8,128)S(1)} %get-tuple-element.22) | copy-start | bytes 1179652
  42.6 12.9 %collective-permute-start.23 = (bf16[6,128,128]{2,1,0:T(8,128)(2,1)S(1)}, bf16[6,128,128]{2,1,0:T(8,128)(2,1)S(1)}, u32[]{:S(2)}, u32[]{:S(2)}) collective-permute-start(bf16[6,128,128]{2,1,0:T(8,128)(2,1)S(1)} %get-tuple-element.21), channel_id=1, source_target_pairs={{32,0},{33,1},{34,2},{35,3},{36,4},{37,5},{38,6},{39,7},{40,8},{41... | collective-permute-start | bytes 589832 | tf_op jit(solution)/shard_map/ppermute | solution.py:35
  45.1 25.6 %collective-permute-start.3 = (bf16[36,128,128]{2,1,0:T(8,128)(2,1)S(1)}, bf16[36,128,128]{2,1,0:T(8,128)(2,1)}, u32[]{:S(2)}, u32[]{:S(2)}) collective-permute-start(bf16[36,128,128]{2,1,0:T(8,128)(2,1)S(1)} %pad_maximum_fusion.past_ref), channel_id=1, source_target_pairs={{0,16},{1,17},{2,18},{3,19},{4,20},{5,21},{6,22},{7,23},{8,24},{9,... | collective-permute-start | bytes 3538952 | tf_op jit(solution)/shard_map/ppermute | solution.py:35
  55.5 5.7 %copy-start.5 = (bf16[6,128,128]{2,1,0:T(8,128)(2,1)}, bf16[6,128,128]{2,1,0:T(8,128)(2,1)S(1)}, u32[]{:S(2)}) copy-start(bf16[6,128,128]{2,1,0:T(8,128)(2,1)S(1)} %collective-permute-done.23) | copy-start | bytes 589828
  55.6 3.4 %collective-permute-start.24 = (bf16[6,128,128]{2,1,0:T(8,128)(2,1)S(1)}, bf16[6,128,128]{2,1,0:T(8,128)(2,1)S(1)}, u32[]{:S(2)}, u32[]{:S(2)}) collective-permute-start(bf16[6,128,128]{2,1,0:T(8,128)(2,1)S(1)} %fusion.6), channel_id=1, source_target_pairs={{64,0},{65,1},{66,2},{67,3},{68,4},{69,5},{70,6},{71,7},{72,8},{73... | collective-permute-start | bytes 589832 | tf_op jit(solution)/shard_map/ppermute | solution.py:35
  56.3 105.0 %collective-permute-start.11 = (bf16[12,11,128,128]{3,2,1,0:T(8,128)(2,1)}, bf16[12,11,128,128]{3,2,1,0:T(8,128)(2,1)}, u32[]{:S(2)}, u32[]{:S(2)}) collective-permute-start(bf16[12,11,128,128]{3,2,1,0:T(8,128)(2,1)} %bitcast.4.z_ref.refs_0_.mine_ref), channel_id=1, source_target_pairs={{0,16},{1,17},{2,18},{3,19},{4,20},{5,21},{6,22},{7,23},{8,24},{9,... | collective-permute-start | bytes 12976136 | tf_op jit(solution)/shard_map/ppermute | solution.py:35
  59.0 11.7 %copy-start.6 = (bf16[6,128,128]{2,1,0:T(8,128)(2,1)}, bf16[6,128,128]{2,1,0:T(8,128)(2,1)S(1)}, u32[]{:S(2)}) copy-start(bf16[6,128,128]{2,1,0:T(8,128)(2,1)S(1)} %collective-permute-done.24) | copy-start | bytes 589828
  59.0 0.7 collective-permute-start.25
  59.7 0.7 copy-start.8
  61.2 28.7 %copy-start.7 = (bf16[4,1536,128]{2,1,0:T(8,128)(2,1)S(1)}, bf16[4,1536,128]{2,1,0:T(8,128)(2,1)}, u32[]{:S(2)}) copy-start(bf16[4,1536,128]{2,1,0:T(8,128)(2,1)} %param.8) | copy-start | bytes 4718596
  61.2 28.9 %collective-permute-start.26 = (bf16[6,128,128]{2,1,0:T(8,128)(2,1)}, bf16[6,128,128]{2,1,0:T(8,128)(2,1)}, u32[]{:S(2)}, u32[]{:S(2)}) collective-permute-start(bf16[6,128,128]{2,1,0:T(8,128)(2,1)} %fusion.7), channel_id=1, source_target_pairs={{256,0},{257,1},{258,2},{259,3},{260,4},{261,5},{262,6},{263,7},{2... | collective-permute-start | bytes 589832 | tf_op jit(solution)/shard_map/ppermute | solution.py:35
  70.7 28.7 %collective-permute-start.4 = (bf16[36,128,128]{2,1,0:T(8,128)(2,1)}, bf16[36,128,128]{2,1,0:T(8,128)(2,1)S(1)}, u32[]{:S(2)}, u32[]{:S(2)}) collective-permute-start(bf16[36,128,128]{2,1,0:T(8,128)(2,1)} %collective-permute-done.3.past_ref), channel_id=1, source_target_pairs={{0,16},{1,17},{2,18},{3,19},{4,20},{5,21},{6,22},{7,23},{8,24},{9,... | collective-permute-start | bytes 3538952 | tf_op jit(solution)/shard_map/ppermute | solution.py:35
  88.0 2.1 copy-start.1
  88.0 7.5 %collective-permute-start.17 = (f32[6,128,128]{2,1,0:T(8,128)}, f32[6,128,128]{2,1,0:T(8,128)}, u32[]{:S(2)}, u32[]{:S(2)}) collective-permute-start(f32[6,128,128]{2,1,0:T(8,128)} %get-tuple-element.18), channel_id=1, source_target_pairs={{0,16},{1,17},{2,18},{3,19},{4,20},{5,21},{6,22},{7,23},{8,24},{9,... | collective-permute-start | bytes 1179656 | tf_op jit(solution)/shard_map/ppermute | solution.py:35
  90.0 1.5 copy-start
  91.6 3.9 %copy-start.2 = (f32[6,128,128]{2,1,0:T(8,128)S(1)}, f32[6,128,128]{2,1,0:T(8,128)}, u32[]{:S(2)}) copy-start(f32[6,128,128]{2,1,0:T(8,128)} %copy-done.1) | copy-start | bytes 1179652
  92.8 14.2 %collective-permute-start.28 = (bf16[6,128,128]{2,1,0:T(8,128)(2,1)}, bf16[6,128,128]{2,1,0:T(8,128)(2,1)}, u32[]{:S(2)}, u32[]{:S(2)}) collective-permute-start(bf16[6,128,128]{2,1,0:T(8,128)(2,1)} %shard_map.59), channel_id=1, source_target_pairs={{1,0},{2,1},{3,2},{4,3},{5,4},{6,5},{7,6},{8,7},{9,8},{10,9},{11,1... | collective-permute-start | bytes 589832 | tf_op jit(solution)/shard_map/ppermute | solution.py:35
  94.2 12.9 %collective-permute-start.27 = (bf16[6,128,128]{2,1,0:T(8,128)(2,1)}, bf16[6,128,128]{2,1,0:T(8,128)(2,1)}, u32[]{:S(2)}, u32[]{:S(2)}) collective-permute-start(bf16[6,128,128]{2,1,0:T(8,128)(2,1)} %shard_map.59), channel_id=1, source_target_pairs={{0,1},{1,2},{2,3},{3,4},{4,5},{5,6},{6,7},{7,8},{8,9},{9,10},{10,1... | collective-permute-start | bytes 589832 | tf_op jit(solution)/shard_map/ppermute | solution.py:35
  97.4 11.6 %collective-permute-start.18 = (bf16[6,128,128]{2,1,0:T(8,128)(2,1)}, bf16[6,128,128]{2,1,0:T(8,128)(2,1)}, u32[]{:S(2)}, u32[]{:S(2)}) collective-permute-start(bf16[6,128,128]{2,1,0:T(8,128)(2,1)} %get-tuple-element.23), channel_id=1, source_target_pairs={{32,0},{33,1},{34,2},{35,3},{36,4},{37,5},{38,6},{39,7},{40,8},{41... | collective-permute-start | bytes 589832 | tf_op jit(solution)/shard_map/ppermute | solution.py:35
  103.9 13.6 %collective-permute-start.12 = (f32[6,128,128]{2,1,0:T(8,128)}, f32[6,128,128]{2,1,0:T(8,128)}, u32[]{:S(2)}, u32[]{:S(2)}) collective-permute-start(f32[6,128,128]{2,1,0:T(8,128)} %get-tuple-element.16), channel_id=1, source_target_pairs={{0,16},{1,17},{2,18},{3,19},{4,20},{5,21},{6,22},{7,23},{8,24},{9,... | collective-permute-start | bytes 1179656 | tf_op jit(solution)/shard_map/ppermute | solution.py:35
  107.0 2.0 copy-start.3
  108.3 55.1 %collective-permute-start.33 = (bf16[18,128,128]{2,1,0:T(8,128)(2,1)S(1)}, bf16[18,128,128]{2,1,0:T(8,128)(2,1)S(1)}, u32[]{:S(2)}, u32[]{:S(2)}) collective-permute-start(bf16[18,128,128]{2,1,0:T(8,128)(2,1)S(1)} %pad_maximum_fusion.1.refs_2_.now_ref), channel_id=1, source_target_pairs={{0,32},{1,33},{2,34},{3,35},{4,36},{5,37},{6,38},{7,39},{8,40},{9,... | collective-permute-start | bytes 1769480 | tf_op jit(solution)/shard_map/ppermute | solution.py:35
  110.0 24.3 %collective-permute-start.19 = (bf16[6,128,128]{2,1,0:T(8,128)(2,1)S(1)}, bf16[6,128,128]{2,1,0:T(8,128)(2,1)S(1)}, u32[]{:S(2)}, u32[]{:S(2)}) collective-permute-start(bf16[6,128,128]{2,1,0:T(8,128)(2,1)S(1)} %fusion.4), channel_id=1, source_target_pairs={{64,0},{65,1},{66,2},{67,3},{68,4},{69,5},{70,6},{71,7},{72,8},{73... | collective-permute-start | bytes 589832 | tf_op jit(solution)/shard_map/ppermute | solution.py:35
  110.7 30.5 %collective-permute-start.5 = (bf16[36,128,128]{2,1,0:T(8,128)(2,1)S(1)}, bf16[36,128,128]{2,1,0:T(8,128)(2,1)S(1)}, u32[]{:S(2)}, u32[]{:S(2)}) collective-permute-start(bf16[36,128,128]{2,1,0:T(8,128)(2,1)S(1)} %collective-permute-done.4.past_ref), channel_id=1, source_target_pairs={{0,16},{1,17},{2,18},{3,19},{4,20},{5,21},{6,22},{7,23},{8,24},{9,... | collective-permute-start | bytes 3538952 | tf_op jit(solution)/shard_map/ppermute | solution.py:35
  118.5 19.4 %collective-permute-start.13 = (bf16[6,128,128]{2,1,0:T(8,128)(2,1)S(1)}, bf16[6,128,128]{2,1,0:T(8,128)(2,1)S(1)}, u32[]{:S(2)}, u32[]{:S(2)}) collective-permute-start(bf16[6,128,128]{2,1,0:T(8,128)(2,1)S(1)} %get-tuple-element.25), channel_id=1, source_target_pairs={{32,0},{33,1},{34,2},{35,3},{36,4},{37,5},{38,6},{39,7},{40,8},{41... | collective-permute-start | bytes 589832 | tf_op jit(solution)/shard_map/ppermute | solution.py:35
  135.3 3.4 %collective-permute-start.20 = (bf16[6,128,128]{2,1,0:T(8,128)(2,1)S(1)}, bf16[6,128,128]{2,1,0:T(8,128)(2,1)S(1)}, u32[]{:S(2)}, u32[]{:S(2)}) collective-permute-start(bf16[6,128,128]{2,1,0:T(8,128)(2,1)S(1)} %fusion.12), channel_id=1, source_target_pairs={{128,0},{129,1},{130,2},{131,3},{132,4},{133,5},{134,6},{135,7},{1... | collective-permute-start | bytes 589832 | tf_op jit(solution)/shard_map/ppermute | solution.py:35
  138.0 2.4 collective-permute-start.14
  139.7 15.9 %collective-permute-start.21 = (bf16[6,128,128]{2,1,0:T(8,128)(2,1)S(1)}, bf16[6,128,128]{2,1,0:T(8,128)(2,1)S(1)}, u32[]{:S(2)}, u32[]{:S(2)}) collective-permute-start(bf16[6,128,128]{2,1,0:T(8,128)(2,1)S(1)} %fusion.5), channel_id=1, source_target_pairs={{256,0},{257,1},{258,2},{259,3},{260,4},{261,5},{262,6},{263,7},{2... | collective-permute-start | bytes 589832 | tf_op jit(solution)/shard_map/ppermute | solution.py:35
  140.5 16.2 %collective-permute-start.15 = (bf16[6,128,128]{2,1,0:T(8,128)(2,1)S(1)}, bf16[6,128,128]{2,1,0:T(8,128)(2,1)S(1)}, u32[]{:S(2)}, u32[]{:S(2)}) collective-permute-start(bf16[6,128,128]{2,1,0:T(8,128)(2,1)S(1)} %fusion.11), channel_id=1, source_target_pairs={{128,0},{129,1},{130,2},{131,3},{132,4},{133,5},{134,6},{135,7},{1... | collective-permute-start | bytes 589832 | tf_op jit(solution)/shard_map/ppermute | solution.py:35
  145.0 12.5 %collective-permute-start.6 = (f32[6,128,128]{2,1,0:T(8,128)S(1)}, f32[6,128,128]{2,1,0:T(8,128)S(1)}, u32[]{:S(2)}, u32[]{:S(2)}) collective-permute-start(f32[6,128,128]{2,1,0:T(8,128)S(1)} %get-tuple-element.14), channel_id=1, source_target_pairs={{0,16},{1,17},{2,18},{3,19},{4,20},{5,21},{6,22},{7,23},{8,24},{9,... | collective-permute-start | bytes 1179656 | tf_op jit(solution)/shard_map/ppermute | solution.py:35
  156.8 9.2 %collective-permute-start.16 = (bf16[6,128,128]{2,1,0:T(8,128)(2,1)S(1)}, bf16[6,128,128]{2,1,0:T(8,128)(2,1)S(1)}, u32[]{:S(2)}, u32[]{:S(2)}) collective-permute-start(bf16[6,128,128]{2,1,0:T(8,128)(2,1)S(1)} %fusion.3), channel_id=1, source_target_pairs={{256,0},{257,1},{258,2},{259,3},{260,4},{261,5},{262,6},{263,7},{2... | collective-permute-start | bytes 589832 | tf_op jit(solution)/shard_map/ppermute | solution.py:35
  157.6 7.7 %collective-permute-start.7 = (bf16[6,128,128]{2,1,0:T(8,128)(2,1)S(1)}, bf16[6,128,128]{2,1,0:T(8,128)(2,1)S(1)}, u32[]{:S(2)}, u32[]{:S(2)}) collective-permute-start(bf16[6,128,128]{2,1,0:T(8,128)(2,1)S(1)} %get-tuple-element.27), channel_id=1, source_target_pairs={{32,0},{33,1},{34,2},{35,3},{36,4},{37,5},{38,6},{39,7},{40,8},{41... | collective-permute-start | bytes 589832 | tf_op jit(solution)/shard_map/ppermute | solution.py:35
  162.0 4.9 %collective-permute-start.30 = (bf16[6,128,128]{2,1,0:T(8,128)(2,1)S(1)}, bf16[6,128,128]{2,1,0:T(8,128)(2,1)S(1)}, u32[]{:S(2)}, u32[]{:S(2)}) collective-permute-start(bf16[6,128,128]{2,1,0:T(8,128)(2,1)S(1)} %shard_map.60), channel_id=1, source_target_pairs={{1,0},{2,1},{3,2},{4,3},{5,4},{6,5},{7,6},{8,7},{9,8},{10,9},{11,1... | collective-permute-start | bytes 589832 | tf_op jit(solution)/shard_map/ppermute | solution.py:35
  162.7 4.2 %collective-permute-start.29 = (bf16[6,128,128]{2,1,0:T(8,128)(2,1)S(1)}, bf16[6,128,128]{2,1,0:T(8,128)(2,1)S(1)}, u32[]{:S(2)}, u32[]{:S(2)}) collective-permute-start(bf16[6,128,128]{2,1,0:T(8,128)(2,1)S(1)} %shard_map.60), channel_id=1, source_target_pairs={{0,1},{1,2},{2,3},{3,4},{4,5},{5,6},{6,7},{7,8},{8,9},{9,10},{10,1... | collective-permute-start | bytes 589832 | tf_op jit(solution)/shard_map/ppermute | solution.py:35
  164.0 5.8 %collective-permute-start.34 = (bf16[6,128,128]{2,1,0:T(8,128)(2,1)S(1)}, bf16[6,128,128]{2,1,0:T(8,128)(2,1)S(1)}, u32[]{:S(2)}, u32[]{:S(2)}) collective-permute-start(bf16[6,128,128]{2,1,0:T(8,128)(2,1)S(1)} %shard_map.63), channel_id=1, source_target_pairs={{32,0},{33,1},{34,2},{35,3},{36,4},{37,5},{38,6},{39,7},{40,8},{41... | collective-permute-start | bytes 589832 | tf_op jit(solution)/shard_map/ppermute | solution.py:35
  165.3 0.8 collective-permute-start.8
  166.2 2.7 %collective-permute-start.9 = (bf16[6,128,128]{2,1,0:T(8,128)(2,1)S(1)}, bf16[6,128,128]{2,1,0:T(8,128)(2,1)S(1)}, u32[]{:S(2)}, u32[]{:S(2)}) collective-permute-start(bf16[6,128,128]{2,1,0:T(8,128)(2,1)S(1)} %fusion.10), channel_id=1, source_target_pairs={{128,0},{129,1},{130,2},{131,3},{132,4},{133,5},{134,6},{135,7},{1... | collective-permute-start | bytes 589832 | tf_op jit(solution)/shard_map/ppermute | solution.py:35
  167.6 3.0 %collective-permute-start.32 = (bf16[6,128,128]{2,1,0:T(8,128)(2,1)S(1)}, bf16[6,128,128]{2,1,0:T(8,128)(2,1)S(1)}, u32[]{:S(2)}, u32[]{:S(2)}) collective-permute-start(bf16[6,128,128]{2,1,0:T(8,128)(2,1)S(1)} %shard_map.62), channel_id=1, source_target_pairs={{1,0},{2,1},{3,2},{4,3},{5,4},{6,5},{7,6},{8,7},{9,8},{10,9},{11,1... | collective-permute-start | bytes 589832 | tf_op jit(solution)/shard_map/ppermute | solution.py:35
  168.3 2.3 collective-permute-start.31
  169.1 1.6 collective-permute-start.10
  171.4 0.7 collective-permute-start.35
  172.2 0.7 collective-permute-start.36
  172.9 0.7 collective-permute-start.37
  173.6 76.3 %collective-permute-start.38 = (bf16[6,128,128]{2,1,0:T(8,128)(2,1)S(1)}, bf16[6,128,128]{2,1,0:T(8,128)(2,1)S(1)}, u32[]{:S(2)}, u32[]{:S(2)}) collective-permute-start(bf16[6,128,128]{2,1,0:T(8,128)(2,1)S(1)} %broadcast_select_fusion.2), channel_id=1, source_target_pairs={{0,32},{1,33},{2,34},{3,35},{4,36},{5,37},{6,38},{7,39},{8,40},{9,... | collective-permute-start | bytes 589832 | tf_op jit(solution)/shard_map/ppermute | solution.py:35
  250.0 10.6 %collective-permute-start.39 = (bf16[6,128,128]{2,1,0:T(8,128)(2,1)S(1)}, bf16[6,128,128]{2,1,0:T(8,128)(2,1)S(1)}, u32[]{:S(2)}, u32[]{:S(2)}) collective-permute-start(bf16[6,128,128]{2,1,0:T(8,128)(2,1)S(1)} %broadcast_select_fusion.3.mine_ref), channel_id=1, source_target_pairs={{0,16},{1,17},{2,18},{3,19},{4,20},{5,21},{6,22},{7,23},{8,24},{9,... | collective-permute-start | bytes 589832 | tf_op jit(solution)/shard_map/ppermute | solution.py:35

commit v3 on v2

v3 whole, which is shorter than its diff:
```python
import functools

import jax
import jax.numpy as jnp
from jax import lax
from jax.experimental import pallas as pl
from jax.experimental.pallas import tpu as pltpu
from jax.sharding import PartitionSpec as P

CORES, XS = 2, 4
HALF = 64
AXES = ("lag", "row")


def coords(lag):
    return lag // (XS * CORES), lag // CORES % XS, lag % CORES


def lag_of(z, x, core):
    return (z * XS + x) * CORES + core


def pairs(lags, rows, target):
    out = []
    for lag in range(lags):
        for row in range(rows):
            goal = target(lag, row)
            if goal is not None and 0 <= goal[0] < lags and 0 <= goal[1] < rows:
                out.append((lag * rows + row, goal[0] * rows + goal[1]))
    return out


def send(value, target):
    lags, rows = lax.axis_size("lag"), lax.axis_size("row")
    return lax.ppermute(value, AXES, pairs(lags, rows, target))


def along_z(step, when):
    def target(lag, row):
        z, x, core = coords(lag)
        return (lag_of(z + step, x, core), row) if when(z, x) and z + step >= 0 else None
    return target


def along_x(step, when):
    def target(lag, row):
        z, x, core = coords(lag)
        return (lag_of(z, x + step, core), row) if when(z, x) else None
    return target


def other_core(lag, row):
    return lag ^ 1, row


def sparse_row(z_ref, row, tile, cols, count):
    left = jnp.concatenate([z_ref[row, j] for j in range(count)], axis=1)
    right = jnp.concatenate([tile(cols(j)) for j in range(count)], axis=0)
    return jnp.dot(left, right, preferred_element_type=jnp.float32)


def low_lanes(shape):
    return lax.broadcasted_iota(jnp.int32, shape, len(shape) - 1) < HALF


def pack(first, second):
    low = low_lanes(first.shape)
    return (
        jnp.where(low, first, pltpu.roll(second, HALF, 1)),
        jnp.where(low, pltpu.roll(first, HALF, 1), second),
    )


VMEM = pl.BlockSpec(memory_space=pltpu.VMEM)
SMEM = pl.BlockSpec(memory_space=pltpu.SMEM)
CORE, ROOT, NEXT, HEAD = 0, 1, 2, 8


def call(kernel, out_shape, flops, meta, *args):
    outs = len(out_shape) if isinstance(out_shape, tuple) else 0
    return pl.pallas_call(
        kernel,
        out_shape=out_shape,
        in_specs=[SMEM] + [VMEM] * len(args),
        out_specs=(VMEM,) * outs if outs else VMEM,
        compiler_params=pltpu.CompilerParams(vmem_limit_bytes=14 * 1024 * 1024),
        cost_estimate=pl.CostEstimate(flops=flops, bytes_accessed=5 * 10 ** 6, transcendentals=0),
    )(meta, *args)


def history_kernel(meta, z_ref, *refs):
    pasts, (keep_ref, send_ref) = refs[:-2], refs[-2:]
    blocks, count, width, unused = z_ref.shape

    def tile(col):
        return jnp.concatenate([past[col] for past in pasts], axis=1)

    for pair in range(blocks // 2):
        rows = []
        for row in (2 * pair, 2 * pair + 1):
            base = HEAD + row * count
            rows.append(sparse_row(z_ref, row, tile, lambda j: meta[base + j], count))
        for number in range(len(pasts)):
            lanes = slice(number * width, (number + 1) * width)
            low, high = pack(*(row[:, lanes] for row in rows))
            place = number * (blocks // 2) + pair
            keep_ref[place] = jnp.where(meta[CORE] == 0, low, high)
            send_ref[place] = jnp.where(meta[CORE] == 0, high, low)


def history_partial(meta, zmat, *pasts):
    blocks, count, width, unused = zmat.shape
    half = jax.ShapeDtypeStruct((len(pasts) * blocks // 2, width, width), jnp.float32)
    return call(
        history_kernel, (half, half), 2 * len(pasts) * blocks * count * width ** 3,
        meta, zmat, *pasts,
    )


def packed_rows(meta, z_ref, now_ref, pair):
    count = z_ref.shape[1]
    rows = []
    for row in (2 * pair, 2 * pair + 1):
        base = HEAD + row * count

        def tile(col):
            both = now_ref[col // 2]
            mine = low_lanes(both.shape) == (col % 2 == 0)
            return jnp.where(mine, both, jnp.zeros_like(both))

        total = sparse_row(z_ref, row, tile, lambda j: meta[base + j], count)
        rows.append(total + pltpu.roll(total, HALF, 1))
    return jnp.where(low_lanes(rows[0].shape), rows[0], rows[1])


def lag_kernel(flag, meta, z_ref, now_ref, *rest):
    more, out_ref = rest[:-1], rest[-1]

    @pl.when(meta[flag] != 0)
    def _():
        for pair in range(out_ref.shape[0]):
            total = packed_rows(meta, z_ref, now_ref, pair)
            for ref in more:
                total = total + ref[pair].astype(jnp.float32)
            out_ref[pair] = total.astype(out_ref.dtype)


def lag_product(flag, dtype, meta, zmat, now, *more):
    blocks, count, width, unused = zmat.shape
    return call(
        functools.partial(lag_kernel, flag),
        jax.ShapeDtypeStruct((blocks // 2, width, width), dtype),
        2 * blocks * count * width ** 3, meta, zmat, now, *more,
    )


def step_kernel(place, meta, incident_ref, summed_ref, inverse_ref, *refs):
    out_ref = refs[-1]

    @pl.when(meta[ROOT] != 0)
    def _():
        for pair in range(out_ref.shape[0]):
            low, high = pack(*(incident_ref[2 * pair + p].astype(jnp.float32) for p in range(2)))
            driven = jnp.where(meta[CORE] == 0, low, high) - summed_ref[place * out_ref.shape[0] + pair]
            if len(refs) > 1:
                driven = driven - packed_rows(meta, refs[0], refs[1], pair)
            for old in refs[2:-1]:
                driven = driven - old[pair].astype(jnp.float32)
            solved = [
                jnp.dot(
                    inverse_ref[2 * pair + p], driven,
                    precision=lax.Precision.HIGHEST, preferred_element_type=jnp.float32,
                )
                for p in range(2)
            ]
            out_ref[pair] = jnp.where(low_lanes(driven.shape), *solved).astype(out_ref.dtype)


def solve_step(place, meta, incident, summed, inverse, *more):
    blocks, width, unused = inverse.shape
    return call(
        functools.partial(step_kernel, place),
        jax.ShapeDtypeStruct((blocks // 2, width, width), jnp.bfloat16),
        10 ** 9, meta, incident, summed, inverse, *more,
    )


def unpack_kernel(meta, mine_ref, other_ref, out_ref):
    for pair in range(mine_ref.shape[0]):
        mine, other = mine_ref[pair].astype(jnp.float32), other_ref[pair].astype(jnp.float32)
        low = jnp.where(meta[CORE] == 0, mine, other)
        high = jnp.where(meta[CORE] == 0, other, mine)
        first, second = pack(low, high)
        out_ref[2 * pair] = first.astype(out_ref.dtype)
        out_ref[2 * pair + 1] = second.astype(out_ref.dtype)


def unpack(meta, mine, other):
    count, width, unused = mine.shape
    return call(
        unpack_kernel, jax.ShapeDtypeStruct((2 * count, width, width), mine.dtype),
        10 ** 6, meta, mine, other,
    )


def swap_rows(lag, row):
    return lag, row ^ 1


def next_chip(lag, row):
    return lag, (row + 2 if row % 2 == 0 else row - 2)


def on_root(step):
    def target(lag, row):
        return (lag, row + step) if lag < CORES else None
    return target


def after(value, *done):
    return lax.optimization_barrier((value,) + done)[0]


TREE = (
    along_x(-1, lambda z, x: x % 2 == 1),
    along_x(-2, lambda z, x: x == 2),
    along_z(-1, lambda z, x: x == 0 and z % 2 == 1),
    along_z(-2, lambda z, x: x == 0 and z == 2),
)


def halves(pieces):
    keep, extra = pieces
    return keep + send(extra, other_core)


def stage(total, number):
    moved = send(total.astype(jnp.bfloat16), TREE[number])
    return total + moved.astype(jnp.float32)


def spread(value, got):
    moves = (
        along_z(2, lambda z, x: x == 0 and z == 0),
        along_z(1, lambda z, x: x == 0 and z % 2 == 0),
        along_x(2, lambda z, x: x == 0),
        along_x(1, lambda z, x: x % 2 == 0),
    )
    for move, here in zip(moves, got):
        value = jnp.where(here, send(value, move), value)
    return value


def per_device(z_blocks, block_cols, history, incident, near_inverse):
    blocks, width, unused = near_inverse.shape
    zmat = z_blocks[0]
    lag_pos = lax.axis_index("lag")
    row_pos = lax.axis_index("row")
    z_pos, x_pos, core = coords(lag_pos)
    own = history[0].reshape(blocks, width, width)
    fields = [f.reshape(blocks, width, width) for f in incident]

    cols = block_cols[0].reshape(-1) - (row_pos - 1) * blocks
    group, inside = cols // blocks, cols % blocks
    even = row_pos % 2 == 0
    slot = jnp.where(group == 1, 0, jnp.where((group == 2) == even, 1, 2))
    chip = lag_pos // CORES
    flags = jnp.stack([core, chip == 0, chip == 1] + [0] * (HEAD - 3)).astype(jnp.int32)
    history_meta = jnp.concatenate([flags, slot * blocks + inside])

    def first_chips(lag, row):
        return (lag ^ 1, row) if lag < 2 * CORES else None

    def next_lag(past):
        return send(past, lambda lag, row: (lag + 1, row))

    def wide(value):
        below = send(value, on_root(1))
        above = send(value, on_root(-1))
        return jnp.concatenate([below, value, above], axis=0)

    near = send(own, swap_rows)
    swapped_cols = send(cols, first_chips)
    swapped = send(zmat, first_chips)
    first = jnp.where(core == 0, zmat, swapped)
    second = jnp.where(core == 0, swapped, zmat)
    first_meta = jnp.concatenate([flags, jnp.where(core == 0, cols, swapped_cols)])
    second_meta = jnp.concatenate([flags, jnp.where(core == 0, swapped_cols, cols)])
    x_zero = x_pos == 0
    got = [x_zero & (z_pos == 2), x_zero & (z_pos % 2 == 1), x_pos == 2, x_pos % 2 == 1]
    near, history_meta, first_meta, second_meta, got, first, second = lax.optimization_barrier(
        (near, history_meta, first_meta, second_meta, got, first, second)
    )
    far = send(near, next_chip)
    past0 = jnp.concatenate([own, near, far], axis=0)
    past1 = next_lag(past0)
    past2 = next_lag(past1)
    past3 = next_lag(past2)

    def partial(past):
        return history_partial(history_meta, zmat, past)

    a = stage(halves(partial(past0)), 0)
    part1 = partial(past1)
    a = stage(after(a, part1[0]), 1)
    b = halves(part1)
    a = stage(after(a, b), 2)
    b = stage(b, 0)
    part2 = partial(after(past2, a))
    a = stage(after(a, b), 3)
    b = stage(b, 1)
    c = halves(part2)
    current0 = solve_step(0, first_meta, fields[0], after(a, b, part2[0]), near_inverse)

    b = stage(after(b, current0), 2)
    c0 = wide(current0)
    c = stage(after(c, current0), 0)
    part3 = partial(after(past3, current0))
    b = stage(b, 3)
    c = stage(c, 1)
    d = halves(part3)
    current1 = solve_step(0, first_meta, fields[1], after(b, c, d), near_inverse, first, c0)

    c = stage(after(c, current1), 2)
    d = stage(after(d, current1), 0)
    c1 = wide(current1)
    third = send(after(c0, c, d), along_x(1, lambda z, x: z == 0 and x == 0))
    old = lag_product(ROOT, jnp.float32, second_meta, second, after(c0, c, d))
    c = stage(c, 3)
    d = stage(d, 1)
    current2 = solve_step(0, first_meta, fields[2], after(c, d), near_inverse, first, c1, old)

    third = lag_product(NEXT, jnp.bfloat16, first_meta, first, after(third, current2))
    third = send(third, along_x(-1, lambda z, x: z == 0 and x == 1))
    d = stage(after(d, current2), 2)
    c2 = wide(current2)
    old = lag_product(ROOT, jnp.float32, second_meta, second, after(c1, d))
    d = stage(d, 3)
    c3 = solve_step(0, first_meta, fields[3], d, near_inverse, first, c2, old, third)
    c3 = spread(c3, got)
    out = unpack(history_meta, c3, send(c3, other_core))
    return out.reshape(blocks * width, width)


def solution(mesh):
    return jax.shard_map(
        per_device,
        mesh=mesh,
        in_specs=(
            P("lag", "row", None, None, None),
            P("lag", "row", None),
            P("lag", "row", None),
            P(None, "row", None),
            P("row", None, None),
        ),
        out_specs=P("row", None),
        check_vma=False,
    )
```

time: 263 us -> 226 us (0.86)
  the two profiles are of different devices: /device:TPU:39 before, /device:TPU:479 now
where the time goes in v3:
time: 226 us; the launch traced here: 225 us
  starting transfers between devices  103 us (46%)
  waiting for transfers between devices  97.9 us (43%)
  Pallas kernels  13.7 us (6%)
  other arithmetic  8.62 us (4%)
    ppermute x40, starting transfers between devices, send(): return lax.ppermute(value, AXES, pairs(lags, rows, target))  103 us
    ppermute x40, waiting for transfers between devices, send(): return lax.ppermute(value, AXES, pairs(lags, rows, target))  97.9 us
    pallas_call x12, Pallas kernels, call(): pl.pallas_call(kernel, out_shape=out_shape, in_specs=[SMEM] + [VMEM] * le...  13.7 us
    select_n x1, other arithmetic, per_device(): second = jnp.where(core == 0, swapped, zmat)  6.3 us
  transfers between devices with their start and end apart: 40, of which 9 were waited for; matrix products, arithmetic and copies ran while one was open for 4% of the time, Pallas kernels for 5%

profile of v3, /device:TPU:479, one launch (start us, length us, event | category | flops | bytes accessed | tf_op | source)
XLA Modules:
  0.0 225.3 jit_solution(16276209984963566544)
XLA Ops:
  0.0 2.7 %collective-permute-start.2 = (bf16[12,11,128,128]{3,2,1,0:T(8,128)(2,1)}, bf16[12,11,128,128]{3,2,1,0:T(8,128)(2,1)}, u32[]{:S(2)}, u32[]{:S(2)}) collective-permute-start(bf16[12,11,128,128]{3,2,1,0:T(8,128)(2,1)} %bitcast.12), channel_id=1, source_target_pairs={{0,16},{1,17},{2,18},{3,19},{4,20},{5,21},{6,22},{7,23},{8,24},{9,... | collective-permute-start | bytes 12976136 | tf_op jit(solution)/shard_map/ppermute | solution.py:35
  2.7 0.7 broadcast_subtract_fusion
  3.6 0.7 collective-permute-start.1
  4.2 1.9 collective-permute-start
  6.6 6.3 %broadcast_select_fusion = (bf16[12,11,128,128]{3,2,1,0:T(8,128)(2,1)}, bf16[12,11,128,128]{3,2,1,0:T(8,128)(2,1)S(1)}) fusion(bf16[12,11,128,128]{3,2,1,0:T(8,128)(2,1)} %collective-permute-done.2, pred[]{:T(512)S(6)} %eq.62, bf16[1,12,11,128,128]{4,3,2,1,0:T(8,128)(2,1)} %param.5), kind=kLoop, calls=%fused_computation | loop fusion | flops 4325376 | bytes 17301504 | tf_op jit(solution)/shard_map/jit(_where)/select_n | solution.py:286
  12.9 11.4 %collective-permute-done = bf16[12,128,128]{2,1,0:T(8,128)(2,1)S(1)} collective-permute-done((bf16[12,128,128]{2,1,0:T(8,128)(2,1)}, bf16[12,128,128]{2,1,0:T(8,128)(2,1)S(1)}, u32[]{:S(2)}, u32[]{:S(2)}) %collective-permute-start) | collective-permute-done | bytes 393248 | tf_op jit(solution)/shard_map/ppermute | solution.py:35
  24.3 2.1 collective-permute-start.3
  26.4 7.6 %collective-permute-done.3 = bf16[12,128,128]{2,1,0:T(8,128)(2,1)S(1)} collective-permute-done((bf16[12,128,128]{2,1,0:T(8,128)(2,1)S(1)}, bf16[12,128,128]{2,1,0:T(8,128)(2,1)S(1)}, u32[]{:S(2)}, u32[]{:S(2)}) %collective-permute-start.3) | collective-permute-done | bytes 393248 | tf_op jit(solution)/shard_map/ppermute | solution.py:35
  34.0 0.1 pad_maximum_fusion.refs_0_
  34.1 1.3 collective-permute-start.4
  35.5 2.0 shard_map.55
  37.4 7.8 %collective-permute-start.7 = (f32[6,128,128]{2,1,0:T(8,128)S(1)}, f32[6,128,128]{2,1,0:T(8,128)S(1)}, u32[]{:S(2)}, u32[]{:S(2)}) collective-permute-start(f32[6,128,128]{2,1,0:T(8,128)S(1)} %get-tuple-element.47), channel_id=1, source_target_pairs={{0,16},{1,17},{2,18},{3,19},{4,20},{5,21},{6,22},{7,23},{8,24},{9,... | collective-permute-start | bytes 1179656 | tf_op jit(solution)/shard_map/ppermute | solution.py:35
  45.3 1.3 collective-permute-done.7
  46.7 3.8 %collective-permute-start.8 = (bf16[6,128,128]{2,1,0:T(8,128)(2,1)S(1)}, bf16[6,128,128]{2,1,0:T(8,128)(2,1)S(1)}, u32[]{:S(2)}, u32[]{:S(2)}) collective-permute-start(bf16[6,128,128]{2,1,0:T(8,128)(2,1)S(1)} %get-tuple-element.83), channel_id=1, source_target_pairs={{32,0},{33,1},{34,2},{35,3},{36,4},{37,5},{38,6},{39,7},{40,8},{41... | collective-permute-start | bytes 589832 | tf_op jit(solution)/shard_map/ppermute | solution.py:35
  50.5 2.0 shard_map.56
  52.4 8.4 %collective-permute-start.10 = (f32[6,128,128]{2,1,0:T(8,128)S(1)}, f32[6,128,128]{2,1,0:T(8,128)S(1)}, u32[]{:S(2)}, u32[]{:S(2)}) collective-permute-start(f32[6,128,128]{2,1,0:T(8,128)S(1)} %get-tuple-element.50), channel_id=1, source_target_pairs={{0,16},{1,17},{2,18},{3,19},{4,20},{5,21},{6,22},{7,23},{8,24},{9,... | collective-permute-start | bytes 1179656 | tf_op jit(solution)/shard_map/ppermute | solution.py:35
  61.1 0.7 collective-permute-start.9
  61.7 1.3 collective-permute-start.5
  63.1 9.2 %collective-permute-start.12 = (bf16[6,128,128]{2,1,0:T(8,128)(2,1)S(1)}, bf16[6,128,128]{2,1,0:T(8,128)(2,1)S(1)}, u32[]{:S(2)}, u32[]{:S(2)}) collective-permute-start(bf16[6,128,128]{2,1,0:T(8,128)(2,1)S(1)} %get-tuple-element.81), channel_id=1, source_target_pairs={{32,0},{33,1},{34,2},{35,3},{36,4},{37,5},{38,6},{39,7},{40,8},{41... | collective-permute-start | bytes 589832 | tf_op jit(solution)/shard_map/ppermute | solution.py:35
  72.4 0.7 collective-permute-start.11
  73.1 3.0 %collective-permute-done.12 = bf16[6,128,128]{2,1,0:T(8,128)(2,1)S(1)} collective-permute-done((bf16[6,128,128]{2,1,0:T(8,128)(2,1)S(1)}, bf16[6,128,128]{2,1,0:T(8,128)(2,1)S(1)}, u32[]{:S(2)}, u32[]{:S(2)}) %collective-permute-start.12) | collective-permute-done | bytes 196640 | tf_op jit(solution)/shard_map/ppermute | solution.py:35
  76.1 0.7 collective-permute-start.14
  76.9 0.7 collective-permute-start.13
  77.7 1.4 collective-permute-start.6
  79.1 2.0 shard_map.57
  81.1 12.9 %collective-permute-start.18 = (f32[6,128,128]{2,1,0:T(8,128)S(1)}, f32[6,128,128]{2,1,0:T(8,128)S(1)}, u32[]{:S(2)}, u32[]{:S(2)}) collective-permute-start(f32[6,128,128]{2,1,0:T(8,128)S(1)} %get-tuple-element.60), channel_id=1, source_target_pairs={{0,16},{1,17},{2,18},{3,19},{4,20},{5,21},{6,22},{7,23},{8,24},{9,... | collective-permute-start | bytes 1179656 | tf_op jit(solution)/shard_map/ppermute | solution.py:35
  94.1 0.6 shard_map.58
  94.7 0.7 collective-permute-start.16
  95.3 0.7 collective-permute-start.21
  96.0 0.7 collective-permute-start.22
  96.8 5.4 %collective-permute-start.19 = (bf16[6,128,128]{2,1,0:T(8,128)(2,1)S(1)}, bf16[6,128,128]{2,1,0:T(8,128)(2,1)S(1)}, u32[]{:S(2)}, u32[]{:S(2)}) collective-permute-start(bf16[6,128,128]{2,1,0:T(8,128)(2,1)S(1)} %convert_element_type.114), channel_id=1, source_target_pairs={{32,0},{33,1},{34,2},{35,3},{36,4},{37,5},{38,6},{39,7},{40,8},{41... | collective-permute-start | bytes 589832 | tf_op jit(solution)/shard_map/ppermute | solution.py:35
  102.3 0.7 collective-permute-start.17
  103.0 3.5 %collective-permute-done.19 = bf16[6,128,128]{2,1,0:T(8,128)(2,1)S(1)} collective-permute-done((bf16[6,128,128]{2,1,0:T(8,128)(2,1)S(1)}, bf16[6,128,128]{2,1,0:T(8,128)(2,1)S(1)}, u32[]{:S(2)}, u32[]{:S(2)}) %collective-permute-start.19) | collective-permute-done | bytes 196640 | tf_op jit(solution)/shard_map/ppermute | solution.py:35
  106.5 0.7 collective-permute-start.20
  107.2 2.0 shard_map.59
  109.2 2.7 %collective-permute-start.15 = (f32[6,128,128]{2,1,0:T(8,128)S(1)}, f32[6,128,128]{2,1,0:T(8,128)S(1)}, u32[]{:S(2)}, u32[]{:S(2)}) collective-permute-start(f32[6,128,128]{2,1,0:T(8,128)S(1)} %get-tuple-element.58), channel_id=1, source_target_pairs={{0,16},{1,17},{2,18},{3,19},{4,20},{5,21},{6,22},{7,23},{8,24},{9,... | collective-permute-start | bytes 1179656 | tf_op jit(solution)/shard_map/ppermute | solution.py:35
  112.1 1.2 collective-permute-done.15
  113.3 0.7 shard_map.60
  114.1 0.8 collective-permute-start.25
  114.9 0.7 collective-permute-start.27
  115.6 0.7 collective-permute-start.28
  116.3 11.8 %collective-permute-start.23 = (bf16[6,128,128]{2,1,0:T(8,128)(2,1)S(1)}, bf16[6,128,128]{2,1,0:T(8,128)(2,1)S(1)}, u32[]{:S(2)}, u32[]{:S(2)}) collective-permute-start(bf16[6,128,128]{2,1,0:T(8,128)(2,1)S(1)} %convert_element_type.118), channel_id=1, source_target_pairs={{32,0},{33,1},{34,2},{35,3},{36,4},{37,5},{38,6},{39,7},{40,8},{41... | collective-permute-start | bytes 589832 | tf_op jit(solution)/shard_map/ppermute | solution.py:35
  128.2 0.7 collective-permute-start.26
  128.9 3.1 %collective-permute-done.23 = bf16[6,128,128]{2,1,0:T(8,128)(2,1)S(1)} collective-permute-done((bf16[6,128,128]{2,1,0:T(8,128)(2,1)S(1)}, bf16[6,128,128]{2,1,0:T(8,128)(2,1)S(1)}, u32[]{:S(2)}, u32[]{:S(2)}) %collective-permute-start.23) | collective-permute-done | bytes 196640 | tf_op jit(solution)/shard_map/ppermute | solution.py:35
  132.1 0.7 collective-permute-start.24
  132.8 0.6 shard_map.61.refs_2_
  133.6 0.6 shard_map.62
  134.2 0.7 collective-permute-start.29
  134.8 0.7 collective-permute-start.33
  135.6 0.7 collective-permute-start.31
  136.2 0.7 collective-permute-start.32
  137.0 0.7 collective-permute-start.30
  137.7 0.6 shard_map.63.refs_2_
  138.3 0.8 shard_map.64
  139.1 0.7 collective-permute-start.34
  139.9 0.6 shard_map.65
  140.4 0.7 collective-permute-start.35
  141.2 0.7 collective-permute-start.36
  141.9 0.7 collective-permute-start.37
  142.6 1.3 collective-permute-start.38
  143.9 65.7 %collective-permute-done.38 = bf16[6,128,128]{2,1,0:T(8,128)(2,1)S(1)} collective-permute-done((bf16[6,128,128]{2,1,0:T(8,128)(2,1)S(1)}, bf16[6,128,128]{2,1,0:T(8,128)(2,1)S(1)}, u32[]{:S(2)}, u32[]{:S(2)}) %collective-permute-start.38) | collective-permute-done | bytes 196640 | tf_op jit(solution)/shard_map/ppermute | solution.py:35
  209.6 13.2 %collective-permute-start.39 = (bf16[6,128,128]{2,1,0:T(8,128)(2,1)S(1)}, bf16[6,128,128]{2,1,0:T(8,128)(2,1)S(1)}, u32[]{:S(2)}, u32[]{:S(2)}) collective-permute-start(bf16[6,128,128]{2,1,0:T(8,128)(2,1)S(1)} %broadcast_select_fusion.5.mine_ref), channel_id=1, source_target_pairs={{0,16},{1,17},{2,18},{3,19},{4,20},{5,21},{6,22},{7,23},{8,24},{9,... | collective-permute-start | bytes 589832 | tf_op jit(solution)/shard_map/ppermute | solution.py:35
  222.8 1.0 collective-permute-done.39.other_ref
  223.8 1.5 shard_map.66
  (90 shorter events, 2.1 us)
Async XLA Ops:
  0.0 6.6 %collective-permute-start.2 = (bf16[12,11,128,128]{3,2,1,0:T(8,128)(2,1)}, bf16[12,11,128,128]{3,2,1,0:T(8,128)(2,1)}, u32[]{:S(2)}, u32[]{:S(2)}) collective-permute-start(bf16[12,11,128,128]{3,2,1,0:T(8,128)(2,1)} %bitcast.12), channel_id=1, source_target_pairs={{0,16},{1,17},{2,18},{3,19},{4,20},{5,21},{6,22},{7,23},{8,24},{9,... | collective-permute-start | bytes 12976136 | tf_op jit(solution)/shard_map/ppermute | solution.py:35
  3.6 2.7 %collective-permute-start.1 = (s32[132]{0:T(256)S(1)}, s32[132]{0:T(256)S(1)}, u32[]{:S(2)}, u32[]{:S(2)}) collective-permute-start(s32[132]{0:T(256)S(1)} %sub.30), channel_id=1, source_target_pairs={{0,16},{1,17},{2,18},{3,19},{4,20},{5,21},{6,22},{7,23},{8,24},{9,... | collective-permute-start | bytes 1592 | tf_op jit(solution)/shard_map/ppermute | solution.py:35
  4.2 20.0 %collective-permute-start = (bf16[12,128,128]{2,1,0:T(8,128)(2,1)}, bf16[12,128,128]{2,1,0:T(8,128)(2,1)S(1)}, u32[]{:S(2)}, u32[]{:S(2)}) collective-permute-start(bf16[12,128,128]{2,1,0:T(8,128)(2,1)} %bitcast.25), channel_id=1, source_target_pairs={{0,1},{1,0},{2,3},{3,2},{4,5},{5,4},{6,7},{7,6},{8,9},{9,8},{10,11... | collective-permute-start | bytes 1179656 | tf_op jit(solution)/shard_map/ppermute | solution.py:35
  6.5 29.0 %slice-start = ((s8[4325376]{0:T(1024)(128)(4,1)}), s8[131072]{0:T(1024)(128)(4,1)S(1)}, s32[]{:S(2)}) async-start(s8[4325376]{0:T(1024)(128)(4,1)} %bitcast.13), calls=%async_computation | async-start | bytes 262144
  6.6 27.4 %copy-start.2 = (bf16[1,1536,128]{2,1,0:T(8,128)(2,1)S(1)}, bf16[1,1536,128]{2,1,0:T(8,128)(2,1)}, u32[]{:S(2)}) copy-start(bf16[1,1536,128]{2,1,0:T(8,128)(2,1)} %param.7) | copy-start | bytes 1179652
  6.6 28.9 %slice-start.1 = ((s8[4325376]{0:T(1024)(128)(4,1)}), s8[4194304]{0:T(1024)(128)(4,1)S(1)}, s32[]{:S(2)}) async-start(s8[4325376]{0:T(1024)(128)(4,1)} %bitcast.13), calls=%async_computation.1 | async-start | bytes 8388608
  24.3 9.7 %collective-permute-start.3 = (bf16[12,128,128]{2,1,0:T(8,128)(2,1)S(1)}, bf16[12,128,128]{2,1,0:T(8,128)(2,1)S(1)}, u32[]{:S(2)}, u32[]{:S(2)}) collective-permute-start(bf16[12,128,128]{2,1,0:T(8,128)(2,1)S(1)} %collective-permute-done), channel_id=1, source_target_pairs={{0,2},{2,4},{3,1},{4,6},{5,3},{6,8},{7,5},{8,10},{9,7},{10,12},{11... | collective-permute-start | bytes 1179656 | tf_op jit(solution)/shard_map/ppermute | solution.py:35
  34.1 16.3 %collective-permute-start.4 = (bf16[36,128,128]{2,1,0:T(8,128)(2,1)S(1)}, bf16[36,128,128]{2,1,0:T(8,128)(2,1)S(1)}, u32[]{:S(2)}, u32[]{:S(2)}) collective-permute-start(bf16[36,128,128]{2,1,0:T(8,128)(2,1)S(1)} %pad_maximum_fusion.refs_0_), channel_id=1, source_target_pairs={{0,16},{1,17},{2,18},{3,19},{4,20},{5,21},{6,22},{7,23},{8,24},{9,... | collective-permute-start | bytes 3538952 | tf_op jit(solution)/shard_map/ppermute | solution.py:35
  37.4 9.2 %collective-permute-start.7 = (f32[6,128,128]{2,1,0:T(8,128)S(1)}, f32[6,128,128]{2,1,0:T(8,128)S(1)}, u32[]{:S(2)}, u32[]{:S(2)}) collective-permute-start(f32[6,128,128]{2,1,0:T(8,128)S(1)} %get-tuple-element.47), channel_id=1, source_target_pairs={{0,16},{1,17},{2,18},{3,19},{4,20},{5,21},{6,22},{7,23},{8,24},{9,... | collective-permute-start | bytes 1179656 | tf_op jit(solution)/shard_map/ppermute | solution.py:35
  46.7 14.2 %copy-start.1 = (bf16[4,1536,128]{2,1,0:T(8,128)(2,1)S(1)}, bf16[4,1536,128]{2,1,0:T(8,128)(2,1)}, u32[]{:S(2)}) copy-start(bf16[4,1536,128]{2,1,0:T(8,128)(2,1)} %param.8) | copy-start | bytes 4718596
  46.7 14.3 %collective-permute-start.8 = (bf16[6,128,128]{2,1,0:T(8,128)(2,1)S(1)}, bf16[6,128,128]{2,1,0:T(8,128)(2,1)S(1)}, u32[]{:S(2)}, u32[]{:S(2)}) collective-permute-start(bf16[6,128,128]{2,1,0:T(8,128)(2,1)S(1)} %get-tuple-element.83), channel_id=1, source_target_pairs={{32,0},{33,1},{34,2},{35,3},{36,4},{37,5},{38,6},{39,7},{40,8},{41... | collective-permute-start | bytes 589832 | tf_op jit(solution)/shard_map/ppermute | solution.py:35
  52.4 10.6 %collective-permute-start.10 = (f32[6,128,128]{2,1,0:T(8,128)S(1)}, f32[6,128,128]{2,1,0:T(8,128)S(1)}, u32[]{:S(2)}, u32[]{:S(2)}) collective-permute-start(f32[6,128,128]{2,1,0:T(8,128)S(1)} %get-tuple-element.50), channel_id=1, source_target_pairs={{0,16},{1,17},{2,18},{3,19},{4,20},{5,21},{6,22},{7,23},{8,24},{9,... | collective-permute-start | bytes 1179656 | tf_op jit(solution)/shard_map/ppermute | solution.py:35
  61.1 11.3 %collective-permute-start.9 = (bf16[6,128,128]{2,1,0:T(8,128)(2,1)S(1)}, bf16[6,128,128]{2,1,0:T(8,128)(2,1)S(1)}, u32[]{:S(2)}, u32[]{:S(2)}) collective-permute-start(bf16[6,128,128]{2,1,0:T(8,128)(2,1)S(1)} %convert_element_type.100), channel_id=1, source_target_pairs={{64,0},{65,1},{66,2},{67,3},{68,4},{69,5},{70,6},{71,7},{72,8},{73... | collective-permute-start | bytes 589832 | tf_op jit(solution)/shard_map/ppermute | solution.py:35
  61.7 15.9 %collective-permute-start.5 = (bf16[36,128,128]{2,1,0:T(8,128)(2,1)S(1)}, bf16[36,128,128]{2,1,0:T(8,128)(2,1)S(1)}, u32[]{:S(2)}, u32[]{:S(2)}) collective-permute-start(bf16[36,128,128]{2,1,0:T(8,128)(2,1)S(1)} %collective-permute-done.4.refs_0_), channel_id=1, source_target_pairs={{0,16},{1,17},{2,18},{3,19},{4,20},{5,21},{6,22},{7,23},{8,24},{9,... | collective-permute-start | bytes 3538952 | tf_op jit(solution)/shard_map/ppermute | solution.py:35
  63.1 12.9 %collective-permute-start.12 = (bf16[6,128,128]{2,1,0:T(8,128)(2,1)S(1)}, bf16[6,128,128]{2,1,0:T(8,128)(2,1)S(1)}, u32[]{:S(2)}, u32[]{:S(2)}) collective-permute-start(bf16[6,128,128]{2,1,0:T(8,128)(2,1)S(1)} %get-tuple-element.81), channel_id=1, source_target_pairs={{32,0},{33,1},{34,2},{35,3},{36,4},{37,5},{38,6},{39,7},{40,8},{41... | collective-permute-start | bytes 589832 | tf_op jit(solution)/shard_map/ppermute | solution.py:35
  72.4 4.4 %collective-permute-start.11 = (bf16[6,128,128]{2,1,0:T(8,128)(2,1)S(1)}, bf16[6,128,128]{2,1,0:T(8,128)(2,1)S(1)}, u32[]{:S(2)}, u32[]{:S(2)}) collective-permute-start(bf16[6,128,128]{2,1,0:T(8,128)(2,1)S(1)} %convert_element_type.102), channel_id=1, source_target_pairs={{128,0},{129,1},{130,2},{131,3},{132,4},{133,5},{134,6},{135,7},{1... | collective-permute-start | bytes 589832 | tf_op jit(solution)/shard_map/ppermute | solution.py:35
  76.1 1.5 collective-permute-start.14
  76.9 17.1 %collective-permute-start.13 = (bf16[6,128,128]{2,1,0:T(8,128)(2,1)S(1)}, bf16[6,128,128]{2,1,0:T(8,128)(2,1)S(1)}, u32[]{:S(2)}, u32[]{:S(2)}) collective-permute-start(bf16[6,128,128]{2,1,0:T(8,128)(2,1)S(1)} %convert_element_type.106), channel_id=1, source_target_pairs={{256,0},{257,1},{258,2},{259,3},{260,4},{261,5},{262,6},{263,7},{2... | collective-permute-start | bytes 589832 | tf_op jit(solution)/shard_map/ppermute | solution.py:35
  77.6 16.4 %copy-start = (f32[12,128,128]{2,1,0:T(8,128)S(1)}, f32[12,128,128]{2,1,0:T(8,128)}, u32[]{:S(2)}) copy-start(f32[12,128,128]{2,1,0:T(8,128)} %inverse_ref.7) | copy-start | bytes 2359300
  77.7 29.6 %collective-permute-start.6 = (bf16[36,128,128]{2,1,0:T(8,128)(2,1)S(1)}, bf16[36,128,128]{2,1,0:T(8,128)(2,1)S(1)}, u32[]{:S(2)}, u32[]{:S(2)}) collective-permute-start(bf16[36,128,128]{2,1,0:T(8,128)(2,1)S(1)} %collective-permute-done.5.refs_0_), channel_id=1, source_target_pairs={{0,16},{1,17},{2,18},{3,19},{4,20},{5,21},{6,22},{7,23},{8,24},{9,... | collective-permute-start | bytes 3538952 | tf_op jit(solution)/shard_map/ppermute | solution.py:35
  81.1 15.6 %collective-permute-start.18 = (f32[6,128,128]{2,1,0:T(8,128)S(1)}, f32[6,128,128]{2,1,0:T(8,128)S(1)}, u32[]{:S(2)}, u32[]{:S(2)}) collective-permute-start(f32[6,128,128]{2,1,0:T(8,128)S(1)} %get-tuple-element.60), channel_id=1, source_target_pairs={{0,16},{1,17},{2,18},{3,19},{4,20},{5,21},{6,22},{7,23},{8,24},{9,... | collective-permute-start | bytes 1179656 | tf_op jit(solution)/shard_map/ppermute | solution.py:35
  94.7 7.5 %collective-permute-start.16 = (bf16[6,128,128]{2,1,0:T(8,128)(2,1)S(1)}, bf16[6,128,128]{2,1,0:T(8,128)(2,1)S(1)}, u32[]{:S(2)}, u32[]{:S(2)}) collective-permute-start(bf16[6,128,128]{2,1,0:T(8,128)(2,1)S(1)} %convert_element_type.110), channel_id=1, source_target_pairs={{128,0},{129,1},{130,2},{131,3},{132,4},{133,5},{134,6},{135,7},{1... | collective-permute-start | bytes 589832 | tf_op jit(solution)/shard_map/ppermute | solution.py:35
  95.3 7.6 %collective-permute-start.21 = (bf16[6,128,128]{2,1,0:T(8,128)(2,1)S(1)}, bf16[6,128,128]{2,1,0:T(8,128)(2,1)S(1)}, u32[]{:S(2)}, u32[]{:S(2)}) collective-permute-start(bf16[6,128,128]{2,1,0:T(8,128)(2,1)S(1)} %shard_map.58), channel_id=1, source_target_pairs={{0,1},{1,2},{2,3},{3,4},{4,5},{5,6},{6,7},{7,8},{8,9},{9,10},{10,1... | collective-permute-start | bytes 589832 | tf_op jit(solution)/shard_map/ppermute | solution.py:35
  96.0 6.9 %collective-permute-start.22 = (bf16[6,128,128]{2,1,0:T(8,128)(2,1)S(1)}, bf16[6,128,128]{2,1,0:T(8,128)(2,1)S(1)}, u32[]{:S(2)}, u32[]{:S(2)}) collective-permute-start(bf16[6,128,128]{2,1,0:T(8,128)(2,1)S(1)} %shard_map.58), channel_id=1, source_target_pairs={{1,0},{2,1},{3,2},{4,3},{5,4},{6,5},{7,6},{8,7},{9,8},{10,9},{11,1... | collective-permute-start | bytes 589832 | tf_op jit(solution)/shard_map/ppermute | solution.py:35
  96.8 9.7 %collective-permute-start.19 = (bf16[6,128,128]{2,1,0:T(8,128)(2,1)S(1)}, bf16[6,128,128]{2,1,0:T(8,128)(2,1)S(1)}, u32[]{:S(2)}, u32[]{:S(2)}) collective-permute-start(bf16[6,128,128]{2,1,0:T(8,128)(2,1)S(1)} %convert_element_type.114), channel_id=1, source_target_pairs={{32,0},{33,1},{34,2},{35,3},{36,4},{37,5},{38,6},{39,7},{40,8},{41... | collective-permute-start | bytes 589832 | tf_op jit(solution)/shard_map/ppermute | solution.py:35
  102.3 9.7 %collective-permute-start.17 = (bf16[6,128,128]{2,1,0:T(8,128)(2,1)S(1)}, bf16[6,128,128]{2,1,0:T(8,128)(2,1)S(1)}, u32[]{:S(2)}, u32[]{:S(2)}) collective-permute-start(bf16[6,128,128]{2,1,0:T(8,128)(2,1)S(1)} %fusion), channel_id=1, source_target_pairs={{256,0},{257,1},{258,2},{259,3},{260,4},{261,5},{262,6},{263,7},{2... | collective-permute-start | bytes 589832 | tf_op jit(solution)/shard_map/ppermute | solution.py:35
  106.5 5.5 %collective-permute-start.20 = (bf16[6,128,128]{2,1,0:T(8,128)(2,1)S(1)}, bf16[6,128,128]{2,1,0:T(8,128)(2,1)S(1)}, u32[]{:S(2)}, u32[]{:S(2)}) collective-permute-start(bf16[6,128,128]{2,1,0:T(8,128)(2,1)S(1)} %fusion.1), channel_id=1, source_target_pairs={{64,0},{65,1},{66,2},{67,3},{68,4},{69,5},{70,6},{71,7},{72,8},{73... | collective-permute-start | bytes 589832 | tf_op jit(solution)/shard_map/ppermute | solution.py:35
  109.2 4.0 %collective-permute-start.15 = (f32[6,128,128]{2,1,0:T(8,128)S(1)}, f32[6,128,128]{2,1,0:T(8,128)S(1)}, u32[]{:S(2)}, u32[]{:S(2)}) collective-permute-start(f32[6,128,128]{2,1,0:T(8,128)S(1)} %get-tuple-element.58), channel_id=1, source_target_pairs={{0,16},{1,17},{2,18},{3,19},{4,20},{5,21},{6,22},{7,23},{8,24},{9,... | collective-permute-start | bytes 1179656 | tf_op jit(solution)/shard_map/ppermute | solution.py:35
  113.3 19.5 %slice-start.2 = ((s8[4325376]{0:T(1024)(128)(4,1)}), s8[4194304]{0:T(1024)(128)(4,1)S(1)}, s32[]{:S(2)}) async-start(s8[4325376]{0:T(1024)(128)(4,1)} %bitcast.19), calls=%async_computation.2 | async-start | bytes 8388608
  113.3 19.5 %slice-start.3 = ((s8[4325376]{0:T(1024)(128)(4,1)}), s8[131072]{0:T(1024)(128)(4,1)S(1)}, s32[]{:S(2)}) async-start(s8[4325376]{0:T(1024)(128)(4,1)} %bitcast.19), calls=%async_computation.3 | async-start | bytes 262144
  114.1 14.0 %collective-permute-start.25 = (bf16[6,128,128]{2,1,0:T(8,128)(2,1)S(1)}, bf16[6,128,128]{2,1,0:T(8,128)(2,1)S(1)}, u32[]{:S(2)}, u32[]{:S(2)}) collective-permute-start(bf16[6,128,128]{2,1,0:T(8,128)(2,1)S(1)} %convert_element_type.122), channel_id=1, source_target_pairs={{128,0},{129,1},{130,2},{131,3},{132,4},{133,5},{134,6},{135,7},{1... | collective-permute-start | bytes 589832 | tf_op jit(solution)/shard_map/ppermute | solution.py:35
  114.9 18.5 %collective-permute-start.27 = (bf16[6,128,128]{2,1,0:T(8,128)(2,1)S(1)}, bf16[6,128,128]{2,1,0:T(8,128)(2,1)S(1)}, u32[]{:S(2)}, u32[]{:S(2)}) collective-permute-start(bf16[6,128,128]{2,1,0:T(8,128)(2,1)S(1)} %shard_map.60), channel_id=1, source_target_pairs={{0,1},{1,2},{2,3},{3,4},{4,5},{5,6},{6,7},{7,8},{8,9},{9,10},{10,1... | collective-permute-start | bytes 589832 | tf_op jit(solution)/shard_map/ppermute | solution.py:35
  115.6 17.8 %collective-permute-start.28 = (bf16[6,128,128]{2,1,0:T(8,128)(2,1)S(1)}, bf16[6,128,128]{2,1,0:T(8,128)(2,1)S(1)}, u32[]{:S(2)}, u32[]{:S(2)}) collective-permute-start(bf16[6,128,128]{2,1,0:T(8,128)(2,1)S(1)} %shard_map.60), channel_id=1, source_target_pairs={{1,0},{2,1},{3,2},{4,3},{5,4},{6,5},{7,6},{8,7},{9,8},{10,9},{11,1... | collective-permute-start | bytes 589832 | tf_op jit(solution)/shard_map/ppermute | solution.py:35
  116.3 15.7 %collective-permute-start.23 = (bf16[6,128,128]{2,1,0:T(8,128)(2,1)S(1)}, bf16[6,128,128]{2,1,0:T(8,128)(2,1)S(1)}, u32[]{:S(2)}, u32[]{:S(2)}) collective-permute-start(bf16[6,128,128]{2,1,0:T(8,128)(2,1)S(1)} %convert_element_type.118), channel_id=1, source_target_pairs={{32,0},{33,1},{34,2},{35,3},{36,4},{37,5},{38,6},{39,7},{40,8},{41... | collective-permute-start | bytes 589832 | tf_op jit(solution)/shard_map/ppermute | solution.py:35
  128.2 5.2 %collective-permute-start.26 = (bf16[6,128,128]{2,1,0:T(8,128)(2,1)S(1)}, bf16[6,128,128]{2,1,0:T(8,128)(2,1)S(1)}, u32[]{:S(2)}, u32[]{:S(2)}) collective-permute-start(bf16[6,128,128]{2,1,0:T(8,128)(2,1)S(1)} %get-tuple-element.75), channel_id=1, source_target_pairs={{256,0},{257,1},{258,2},{259,3},{260,4},{261,5},{262,6},{263,7},{2... | collective-permute-start | bytes 589832 | tf_op jit(solution)/shard_map/ppermute | solution.py:35
  132.1 1.4 collective-permute-start.24
  134.2 2.8 %collective-permute-start.29 = (bf16[6,128,128]{2,1,0:T(8,128)(2,1)S(1)}, bf16[6,128,128]{2,1,0:T(8,128)(2,1)S(1)}, u32[]{:S(2)}, u32[]{:S(2)}) collective-permute-start(bf16[6,128,128]{2,1,0:T(8,128)(2,1)S(1)} %convert_element_type.126), channel_id=1, source_target_pairs={{128,0},{129,1},{130,2},{131,3},{132,4},{133,5},{134,6},{135,7},{1... | collective-permute-start | bytes 589832 | tf_op jit(solution)/shard_map/ppermute | solution.py:35
  134.8 3.5 %collective-permute-start.33 = (bf16[18,128,128]{2,1,0:T(8,128)(2,1)S(1)}, bf16[18,128,128]{2,1,0:T(8,128)(2,1)S(1)}, u32[]{:S(2)}, u32[]{:S(2)}) collective-permute-start(bf16[18,128,128]{2,1,0:T(8,128)(2,1)S(1)} %pad_maximum_fusion.1.refs_1_.now_ref), channel_id=1, source_target_pairs={{0,32},{1,33},{2,34},{3,35},{4,36},{5,37},{6,38},{7,39},{8,40},{9,... | collective-permute-start | bytes 1769480 | tf_op jit(solution)/shard_map/ppermute | solution.py:35
  135.6 2.7 %collective-permute-start.31 = (bf16[6,128,128]{2,1,0:T(8,128)(2,1)S(1)}, bf16[6,128,128]{2,1,0:T(8,128)(2,1)S(1)}, u32[]{:S(2)}, u32[]{:S(2)}) collective-permute-start(bf16[6,128,128]{2,1,0:T(8,128)(2,1)S(1)} %shard_map.62), channel_id=1, source_target_pairs={{0,1},{1,2},{2,3},{3,4},{4,5},{5,6},{6,7},{7,8},{8,9},{9,10},{10,1... | collective-permute-start | bytes 589832 | tf_op jit(solution)/shard_map/ppermute | solution.py:35
  136.2 2.0 collective-permute-start.32
  137.0 2.8 %collective-permute-start.30 = (bf16[6,128,128]{2,1,0:T(8,128)(2,1)S(1)}, bf16[6,128,128]{2,1,0:T(8,128)(2,1)S(1)}, u32[]{:S(2)}, u32[]{:S(2)}) collective-permute-start(bf16[6,128,128]{2,1,0:T(8,128)(2,1)S(1)} %get-tuple-element.73), channel_id=1, source_target_pairs={{256,0},{257,1},{258,2},{259,3},{260,4},{261,5},{262,6},{263,7},{2... | collective-permute-start | bytes 589832 | tf_op jit(solution)/shard_map/ppermute | solution.py:35
  139.1 0.7 collective-permute-start.34
  140.4 0.7 collective-permute-start.35
  141.2 0.7 collective-permute-start.36
  141.9 0.7 collective-permute-start.37
  142.6 67.0 %collective-permute-start.38 = (bf16[6,128,128]{2,1,0:T(8,128)(2,1)S(1)}, bf16[6,128,128]{2,1,0:T(8,128)(2,1)S(1)}, u32[]{:S(2)}, u32[]{:S(2)}) collective-permute-start(bf16[6,128,128]{2,1,0:T(8,128)(2,1)S(1)} %broadcast_select_fusion.4), channel_id=1, source_target_pairs={{0,32},{1,33},{2,34},{3,35},{4,36},{5,37},{6,38},{7,39},{8,40},{9,... | collective-permute-start | bytes 589832 | tf_op jit(solution)/shard_map/ppermute | solution.py:35
  209.6 14.2 %collective-permute-start.39 = (bf16[6,128,128]{2,1,0:T(8,128)(2,1)S(1)}, bf16[6,128,128]{2,1,0:T(8,128)(2,1)S(1)}, u32[]{:S(2)}, u32[]{:S(2)}) collective-permute-start(bf16[6,128,128]{2,1,0:T(8,128)(2,1)S(1)} %broadcast_select_fusion.5.mine_ref), channel_id=1, source_target_pairs={{0,16},{1,17},{2,18},{3,19},{4,20},{5,21},{6,22},{7,23},{8,24},{9,... | collective-permute-start | bytes 589832 | tf_op jit(solution)/shard_map/ppermute | solution.py:35

commit v4 on v3

--- a/solution.py
+++ b/solution.py
@@ -294,8 +294,6 @@
     far = send(near, next_chip)
     past0 = jnp.concatenate([own, near, far], axis=0)
     past1 = next_lag(past0)
-    past2 = next_lag(past1)
-    past3 = next_lag(past2)
 
     def partial(past):
         return history_partial(history_meta, zmat, past)
@@ -304,13 +302,15 @@
     part1 = partial(past1)
     a = stage(after(a, part1[0]), 1)
     b = halves(part1)
+    past2 = next_lag(after(past1, a))
     a = stage(after(a, b), 2)
     b = stage(b, 0)
-    part2 = partial(after(past2, a))
     a = stage(after(a, b), 3)
     b = stage(b, 1)
+    current0 = solve_step(0, first_meta, fields[0], after(a, b), near_inverse)
+    part2 = partial(after(past2, current0))
+    past3 = next_lag(after(past2, current0))
     c = halves(part2)
-    current0 = solve_step(0, first_meta, fields[0], after(a, b, part2[0]), near_inverse)
 
     b = stage(after(b, current0), 2)
     c0 = wide(current0)
@@ -319,19 +319,19 @@
     b = stage(b, 3)
     c = stage(c, 1)
     d = halves(part3)
-    current1 = solve_step(0, first_meta, fields[1], after(b, c, d), near_inverse, first, c0)
+    current1 = solve_step(0, first_meta, fields[1], after(b, d), near_inverse, first, c0)
 
     c = stage(after(c, current1), 2)
     d = stage(after(d, current1), 0)
+    third = send(after(c0, current1), along_x(1, lambda z, x: z == 0 and x == 0))
     c1 = wide(current1)
-    third = send(after(c0, c, d), along_x(1, lambda z, x: z == 0 and x == 0))
     old = lag_product(ROOT, jnp.float32, second_meta, second, after(c0, c, d))
     c = stage(c, 3)
     d = stage(d, 1)
-    current2 = solve_step(0, first_meta, fields[2], after(c, d), near_inverse, first, c1, old)
-
-    third = lag_product(NEXT, jnp.bfloat16, first_meta, first, after(third, current2))
-    third = send(third, along_x(-1, lambda z, x: z == 0 and x == 1))
+    third = lag_product(NEXT, jnp.bfloat16, first_meta, first, third)
+    current2 = solve_step(0, first_meta, fields[2], c, near_inverse, first, c1, old)
+
+    third = send(after(third, current2), along_x(-1, lambda z, x: z == 0 and x == 1))
     d = stage(after(d, current2), 2)
     c2 = wide(current2)
     old = lag_product(ROOT, jnp.float32, second_meta, second, after(c1, d))

time: 226 us -> 228 us (level)
  the two profiles are of different devices: /device:TPU:479 before, /device:TPU:39 now
where the time goes in v4:
time: 228 us; the launch traced here: 227 us
  starting transfers between devices  103 us (45%)
  waiting for transfers between devices  99.3 us (44%)
  Pallas kernels  13.7 us (6%)
  other arithmetic  8.71 us (4%)
    ppermute x40, starting transfers between devices, send(): return lax.ppermute(value, AXES, pairs(lags, rows, target))  103 us
    ppermute x40, waiting for transfers between devices, send(): return lax.ppermute(value, AXES, pairs(lags, rows, target))  99.3 us
    pallas_call x12, Pallas kernels, call(): pl.pallas_call(kernel, out_shape=out_shape, in_specs=[SMEM] + [VMEM] * le...  13.7 us
    select_n x1, other arithmetic, per_device(): second = jnp.where(core == 0, swapped, zmat)  6.3 us
  transfers between devices with their start and end apart: 40, of which 11 were waited for; matrix products, arithmetic and copies ran while one was open for 4% of the time, Pallas kernels for 5%

profile of v4, /device:TPU:39, one launch (start us, length us, event | category | flops | bytes accessed | tf_op | source)
XLA Modules:
  0.0 226.7 jit_solution(17409754673113151106)
XLA Ops:
  0.0 2.7 %collective-permute-start.2 = (bf16[12,11,128,128]{3,2,1,0:T(8,128)(2,1)}, bf16[12,11,128,128]{3,2,1,0:T(8,128)(2,1)}, u32[]{:S(2)}, u32[]{:S(2)}) collective-permute-start(bf16[12,11,128,128]{3,2,1,0:T(8,128)(2,1)} %bitcast.12), channel_id=1, source_target_pairs={{0,16},{1,17},{2,18},{3,19},{4,20},{5,21},{6,22},{7,23},{8,24},{9,... | collective-permute-start | bytes 12976136 | tf_op jit(solution)/shard_map/ppermute | solution.py:35
  2.7 10.6 %collective-permute-start = (bf16[12,128,128]{2,1,0:T(8,128)(2,1)}, bf16[12,128,128]{2,1,0:T(8,128)(2,1)S(1)}, u32[]{:S(2)}, u32[]{:S(2)}) collective-permute-start(bf16[12,128,128]{2,1,0:T(8,128)(2,1)} %bitcast.25), channel_id=1, source_target_pairs={{0,1},{1,0},{2,3},{3,2},{4,5},{5,4},{6,7},{7,6},{8,9},{9,8},{10,11... | collective-permute-start | bytes 1179656 | tf_op jit(solution)/shard_map/ppermute | solution.py:35
  13.3 0.7 broadcast_subtract_fusion
  14.2 0.7 collective-permute-start.1
  15.3 6.3 %broadcast_select_fusion = (bf16[12,11,128,128]{3,2,1,0:T(8,128)(2,1)}, bf16[12,11,128,128]{3,2,1,0:T(8,128)(2,1)S(1)}) fusion(bf16[12,11,128,128]{3,2,1,0:T(8,128)(2,1)} %collective-permute-done.2, pred[]{:T(512)S(6)} %eq.62, bf16[1,12,11,128,128]{4,3,2,1,0:T(8,128)(2,1)} %param.5), kind=kLoop, calls=%fused_computation | loop fusion | flops 4325376 | bytes 17301504 | tf_op jit(solution)/shard_map/jit(_where)/select_n | solution.py:286
  21.6 0.9 collective-permute-done
  22.5 2.3 %collective-permute-start.3 = (bf16[12,128,128]{2,1,0:T(8,128)(2,1)S(1)}, bf16[12,128,128]{2,1,0:T(8,128)(2,1)S(1)}, u32[]{:S(2)}, u32[]{:S(2)}) collective-permute-start(bf16[12,128,128]{2,1,0:T(8,128)(2,1)S(1)} %collective-permute-done), channel_id=1, source_target_pairs={{0,2},{2,4},{3,1},{4,6},{5,3},{6,8},{7,5},{8,10},{9,7},{10,12},{11... | collective-permute-start | bytes 1179656 | tf_op jit(solution)/shard_map/ppermute | solution.py:35
  24.8 10.1 %collective-permute-done.3 = bf16[12,128,128]{2,1,0:T(8,128)(2,1)S(1)} collective-permute-done((bf16[12,128,128]{2,1,0:T(8,128)(2,1)S(1)}, bf16[12,128,128]{2,1,0:T(8,128)(2,1)S(1)}, u32[]{:S(2)}, u32[]{:S(2)}) %collective-permute-start.3) | collective-permute-done | bytes 393248 | tf_op jit(solution)/shard_map/ppermute | solution.py:35
  35.0 13.4 %collective-permute-start.4 = (bf16[36,128,128]{2,1,0:T(8,128)(2,1)S(1)}, bf16[36,128,128]{2,1,0:T(8,128)(2,1)S(1)}, u32[]{:S(2)}, u32[]{:S(2)}) collective-permute-start(bf16[36,128,128]{2,1,0:T(8,128)(2,1)S(1)} %pad_maximum_fusion.refs_0_), channel_id=1, source_target_pairs={{0,16},{1,17},{2,18},{3,19},{4,20},{5,21},{6,22},{7,23},{8,24},{9,... | collective-permute-start | bytes 3538952 | tf_op jit(solution)/shard_map/ppermute | solution.py:35
  48.5 2.0 shard_map.55
  50.5 1.9 collective-permute-start.5
  52.4 1.7 collective-permute-done.5
  54.1 1.3 collective-permute-start.6
  55.4 6.1 %collective-permute-done.4.refs_0_ = bf16[36,128,128]{2,1,0:T(8,128)(2,1)S(1)} collective-permute-done((bf16[36,128,128]{2,1,0:T(8,128)(2,1)S(1)}, bf16[36,128,128]{2,1,0:T(8,128)(2,1)S(1)}, u32[]{:S(2)}, u32[]{:S(2)}) %collective-permute-start.4) | collective-permute-done | bytes 1179680 | tf_op jit(solution)/shard_map/ppermute | solution.py:35
  61.6 2.0 shard_map.56
  63.6 1.9 collective-permute-start.9
  65.6 0.7 collective-permute-start.7
  66.3 0.9 collective-permute-done.9
  67.2 1.3 collective-permute-start.11
  68.6 14.2 %collective-permute-start.8 = (bf16[36,128,128]{2,1,0:T(8,128)(2,1)S(1)}, bf16[36,128,128]{2,1,0:T(8,128)(2,1)S(1)}, u32[]{:S(2)}, u32[]{:S(2)}) collective-permute-start(bf16[36,128,128]{2,1,0:T(8,128)(2,1)S(1)} %collective-permute-done.4.refs_0_), channel_id=1, source_target_pairs={{0,16},{1,17},{2,18},{3,19},{4,20},{5,21},{6,22},{7,23},{8,24},{9,... | collective-permute-start | bytes 3538952 | tf_op jit(solution)/shard_map/ppermute | solution.py:35
  82.9 0.8 collective-permute-start.10
  83.9 0.7 collective-permute-start.12
  84.7 0.8 collective-permute-start.13
  86.4 13.6 %collective-permute-done.8.refs_0_ = bf16[36,128,128]{2,1,0:T(8,128)(2,1)S(1)} collective-permute-done((bf16[36,128,128]{2,1,0:T(8,128)(2,1)S(1)}, bf16[36,128,128]{2,1,0:T(8,128)(2,1)S(1)}, u32[]{:S(2)}, u32[]{:S(2)}) %collective-permute-start.8) | collective-permute-done | bytes 1179680 | tf_op jit(solution)/shard_map/ppermute | solution.py:35
  99.9 6.7 %collective-permute-start.14 = (bf16[36,128,128]{2,1,0:T(8,128)(2,1)S(1)}, bf16[36,128,128]{2,1,0:T(8,128)(2,1)S(1)}, u32[]{:S(2)}, u32[]{:S(2)}) collective-permute-start(bf16[36,128,128]{2,1,0:T(8,128)(2,1)S(1)} %collective-permute-done.8.refs_0_), channel_id=1, source_target_pairs={{0,16},{1,17},{2,18},{3,19},{4,20},{5,21},{6,22},{7,23},{8,24},{9,... | collective-permute-start | bytes 3538952 | tf_op jit(solution)/shard_map/ppermute | solution.py:35
  106.7 2.0 shard_map.60
  108.7 1.9 collective-permute-start.22
  110.6 0.7 collective-permute-start.16
  111.3 0.7 collective-permute-start.19
  112.0 0.7 collective-permute-start.18
  112.8 1.3 collective-permute-start.23
  114.1 0.7 collective-permute-start.17
  114.9 4.9 %collective-permute-done.14.refs_0_ = bf16[36,128,128]{2,1,0:T(8,128)(2,1)S(1)} collective-permute-done((bf16[36,128,128]{2,1,0:T(8,128)(2,1)S(1)}, bf16[36,128,128]{2,1,0:T(8,128)(2,1)S(1)}, u32[]{:S(2)}, u32[]{:S(2)}) %collective-permute-start.14) | collective-permute-done | bytes 1179680 | tf_op jit(solution)/shard_map/ppermute | solution.py:35
  119.8 2.0 shard_map.58
  121.8 1.9 collective-permute-start.15
  123.8 0.7 collective-permute-start.24
  124.5 0.9 collective-permute-done.15
  125.5 0.7 shard_map.59
  126.3 14.2 %collective-permute-start.20 = (bf16[6,128,128]{2,1,0:T(8,128)(2,1)S(1)}, bf16[6,128,128]{2,1,0:T(8,128)(2,1)S(1)}, u32[]{:S(2)}, u32[]{:S(2)}) collective-permute-start(bf16[6,128,128]{2,1,0:T(8,128)(2,1)S(1)} %convert_element_type.114), channel_id=1, source_target_pairs={{32,0},{33,1},{34,2},{35,3},{36,4},{37,5},{38,6},{39,7},{40,8},{41... | collective-permute-start | bytes 589832 | tf_op jit(solution)/shard_map/ppermute | solution.py:35
  140.6 0.7 collective-permute-start.28
  141.2 0.7 collective-permute-start.27
  142.0 0.7 collective-permute-start.25
  142.6 0.7 collective-permute-start.33
  143.3 1.1 collective-permute-done.20
  144.5 0.7 collective-permute-start.21
  145.3 0.7 collective-permute-start.26
  146.0 0.6 shard_map.61.refs_2_
  146.8 0.6 shard_map.62
  147.4 0.7 collective-permute-start.29
  148.1 0.7 collective-permute-start.32
  148.7 0.7 collective-permute-start.31
  149.5 0.7 collective-permute-start.30
  150.2 0.6 shard_map.64
  150.8 0.7 collective-permute-start.34
  151.4 0.8 shard_map.63.refs_2_
  152.4 0.6 shard_map.65
  153.0 0.7 collective-permute-start.35
  153.7 0.7 collective-permute-start.36
  154.4 0.7 collective-permute-start.37
  155.1 1.3 collective-permute-start.38
  156.4 58.1 %collective-permute-done.38 = bf16[6,128,128]{2,1,0:T(8,128)(2,1)S(1)} collective-permute-done((bf16[6,128,128]{2,1,0:T(8,128)(2,1)S(1)}, bf16[6,128,128]{2,1,0:T(8,128)(2,1)S(1)}, u32[]{:S(2)}, u32[]{:S(2)}) %collective-permute-start.38) | collective-permute-done | bytes 196640 | tf_op jit(solution)/shard_map/ppermute | solution.py:35
  214.5 9.7 %collective-permute-start.39 = (bf16[6,128,128]{2,1,0:T(8,128)(2,1)S(1)}, bf16[6,128,128]{2,1,0:T(8,128)(2,1)S(1)}, u32[]{:S(2)}, u32[]{:S(2)}) collective-permute-start(bf16[6,128,128]{2,1,0:T(8,128)(2,1)S(1)} %broadcast_select_fusion.5.mine_ref), channel_id=1, source_target_pairs={{0,16},{1,17},{2,18},{3,19},{4,20},{5,21},{6,22},{7,23},{8,24},{9,... | collective-permute-start | bytes 589832 | tf_op jit(solution)/shard_map/ppermute | solution.py:35
  224.2 1.0 collective-permute-done.39.other_ref
  225.2 1.5 shard_map.66
  (90 shorter events, 3.1 us)
Async XLA Ops:
  0.0 15.3 %collective-permute-start.2 = (bf16[12,11,128,128]{3,2,1,0:T(8,128)(2,1)}, bf16[12,11,128,128]{3,2,1,0:T(8,128)(2,1)}, u32[]{:S(2)}, u32[]{:S(2)}) collective-permute-start(bf16[12,11,128,128]{3,2,1,0:T(8,128)(2,1)} %bitcast.12), channel_id=1, source_target_pairs={{0,16},{1,17},{2,18},{3,19},{4,20},{5,21},{6,22},{7,23},{8,24},{9,... | collective-permute-start | bytes 12976136 | tf_op jit(solution)/shard_map/ppermute | solution.py:35
  2.7 19.8 %collective-permute-start = (bf16[12,128,128]{2,1,0:T(8,128)(2,1)}, bf16[12,128,128]{2,1,0:T(8,128)(2,1)S(1)}, u32[]{:S(2)}, u32[]{:S(2)}) collective-permute-start(bf16[12,128,128]{2,1,0:T(8,128)(2,1)} %bitcast.25), channel_id=1, source_target_pairs={{0,1},{1,0},{2,3},{3,2},{4,5},{5,4},{6,7},{7,6},{8,9},{9,8},{10,11... | collective-permute-start | bytes 1179656 | tf_op jit(solution)/shard_map/ppermute | solution.py:35
  14.2 0.8 collective-permute-start.1
  15.2 33.3 %slice-start = ((s8[4325376]{0:T(1024)(128)(4,1)}), s8[131072]{0:T(1024)(128)(4,1)S(1)}, s32[]{:S(2)}) async-start(s8[4325376]{0:T(1024)(128)(4,1)} %bitcast.13), calls=%async_computation | async-start | bytes 262144
  15.3 19.6 %copy-start.2 = (bf16[1,1536,128]{2,1,0:T(8,128)(2,1)S(1)}, bf16[1,1536,128]{2,1,0:T(8,128)(2,1)}, u32[]{:S(2)}) copy-start(bf16[1,1536,128]{2,1,0:T(8,128)(2,1)} %param.7) | copy-start | bytes 1179652
  15.3 33.2 %slice-start.1 = ((s8[4325376]{0:T(1024)(128)(4,1)}), s8[4194304]{0:T(1024)(128)(4,1)S(1)}, s32[]{:S(2)}) async-start(s8[4325376]{0:T(1024)(128)(4,1)} %bitcast.13), calls=%async_computation.1 | async-start | bytes 8388608
  22.5 12.4 %collective-permute-start.3 = (bf16[12,128,128]{2,1,0:T(8,128)(2,1)S(1)}, bf16[12,128,128]{2,1,0:T(8,128)(2,1)S(1)}, u32[]{:S(2)}, u32[]{:S(2)}) collective-permute-start(bf16[12,128,128]{2,1,0:T(8,128)(2,1)S(1)} %collective-permute-done), channel_id=1, source_target_pairs={{0,2},{2,4},{3,1},{4,6},{5,3},{6,8},{7,5},{8,10},{9,7},{10,12},{11... | collective-permute-start | bytes 1179656 | tf_op jit(solution)/shard_map/ppermute | solution.py:35
  35.0 26.6 %collective-permute-start.4 = (bf16[36,128,128]{2,1,0:T(8,128)(2,1)S(1)}, bf16[36,128,128]{2,1,0:T(8,128)(2,1)S(1)}, u32[]{:S(2)}, u32[]{:S(2)}) collective-permute-start(bf16[36,128,128]{2,1,0:T(8,128)(2,1)S(1)} %pad_maximum_fusion.refs_0_), channel_id=1, source_target_pairs={{0,16},{1,17},{2,18},{3,19},{4,20},{5,21},{6,22},{7,23},{8,24},{9,... | collective-permute-start | bytes 3538952 | tf_op jit(solution)/shard_map/ppermute | solution.py:35
  50.5 3.6 %collective-permute-start.5 = (f32[6,128,128]{2,1,0:T(8,128)S(1)}, f32[6,128,128]{2,1,0:T(8,128)S(1)}, u32[]{:S(2)}, u32[]{:S(2)}) collective-permute-start(f32[6,128,128]{2,1,0:T(8,128)S(1)} %get-tuple-element.48), channel_id=1, source_target_pairs={{0,16},{1,17},{2,18},{3,19},{4,20},{5,21},{6,22},{7,23},{8,24},{9,... | collective-permute-start | bytes 1179656 | tf_op jit(solution)/shard_map/ppermute | solution.py:35
  54.1 11.3 %collective-permute-start.6 = (bf16[6,128,128]{2,1,0:T(8,128)(2,1)S(1)}, bf16[6,128,128]{2,1,0:T(8,128)(2,1)S(1)}, u32[]{:S(2)}, u32[]{:S(2)}) collective-permute-start(bf16[6,128,128]{2,1,0:T(8,128)(2,1)S(1)} %get-tuple-element.85), channel_id=1, source_target_pairs={{32,0},{33,1},{34,2},{35,3},{36,4},{37,5},{38,6},{39,7},{40,8},{41... | collective-permute-start | bytes 589832 | tf_op jit(solution)/shard_map/ppermute | solution.py:35
  63.6 3.6 %collective-permute-start.9 = (f32[6,128,128]{2,1,0:T(8,128)S(1)}, f32[6,128,128]{2,1,0:T(8,128)S(1)}, u32[]{:S(2)}, u32[]{:S(2)}) collective-permute-start(f32[6,128,128]{2,1,0:T(8,128)S(1)} %get-tuple-element.52), channel_id=1, source_target_pairs={{0,16},{1,17},{2,18},{3,19},{4,20},{5,21},{6,22},{7,23},{8,24},{9,... | collective-permute-start | bytes 1179656 | tf_op jit(solution)/shard_map/ppermute | solution.py:35
  65.6 3.0 %collective-permute-start.7 = (bf16[6,128,128]{2,1,0:T(8,128)(2,1)S(1)}, bf16[6,128,128]{2,1,0:T(8,128)(2,1)S(1)}, u32[]{:S(2)}, u32[]{:S(2)}) collective-permute-start(bf16[6,128,128]{2,1,0:T(8,128)(2,1)S(1)} %convert_element_type.100), channel_id=1, source_target_pairs={{64,0},{65,1},{66,2},{67,3},{68,4},{69,5},{70,6},{71,7},{72,8},{73... | collective-permute-start | bytes 589832 | tf_op jit(solution)/shard_map/ppermute | solution.py:35
  67.2 16.5 %collective-permute-start.11 = (bf16[6,128,128]{2,1,0:T(8,128)(2,1)S(1)}, bf16[6,128,128]{2,1,0:T(8,128)(2,1)S(1)}, u32[]{:S(2)}, u32[]{:S(2)}) collective-permute-start(bf16[6,128,128]{2,1,0:T(8,128)(2,1)S(1)} %get-tuple-element.83), channel_id=1, source_target_pairs={{32,0},{33,1},{34,2},{35,3},{36,4},{37,5},{38,6},{39,7},{40,8},{41... | collective-permute-start | bytes 589832 | tf_op jit(solution)/shard_map/ppermute | solution.py:35
  68.6 31.3 %collective-permute-start.8 = (bf16[36,128,128]{2,1,0:T(8,128)(2,1)S(1)}, bf16[36,128,128]{2,1,0:T(8,128)(2,1)S(1)}, u32[]{:S(2)}, u32[]{:S(2)}) collective-permute-start(bf16[36,128,128]{2,1,0:T(8,128)(2,1)S(1)} %collective-permute-done.4.refs_0_), channel_id=1, source_target_pairs={{0,16},{1,17},{2,18},{3,19},{4,20},{5,21},{6,22},{7,23},{8,24},{9,... | collective-permute-start | bytes 3538952 | tf_op jit(solution)/shard_map/ppermute | solution.py:35
  82.8 1.7 copy-start.1
  82.9 0.9 collective-permute-start.10
  83.9 1.6 collective-permute-start.12
  84.7 1.1 copy-start
  84.7 0.9 collective-permute-start.13
  99.9 19.9 %collective-permute-start.14 = (bf16[36,128,128]{2,1,0:T(8,128)(2,1)S(1)}, bf16[36,128,128]{2,1,0:T(8,128)(2,1)S(1)}, u32[]{:S(2)}, u32[]{:S(2)}) collective-permute-start(bf16[36,128,128]{2,1,0:T(8,128)(2,1)S(1)} %collective-permute-done.8.refs_0_), channel_id=1, source_target_pairs={{0,16},{1,17},{2,18},{3,19},{4,20},{5,21},{6,22},{7,23},{8,24},{9,... | collective-permute-start | bytes 3538952 | tf_op jit(solution)/shard_map/ppermute | solution.py:35
  108.7 4.0 %collective-permute-start.22 = (f32[6,128,128]{2,1,0:T(8,128)S(1)}, f32[6,128,128]{2,1,0:T(8,128)S(1)}, u32[]{:S(2)}, u32[]{:S(2)}) collective-permute-start(f32[6,128,128]{2,1,0:T(8,128)S(1)} %get-tuple-element.65), channel_id=1, source_target_pairs={{0,16},{1,17},{2,18},{3,19},{4,20},{5,21},{6,22},{7,23},{8,24},{9,... | collective-permute-start | bytes 1179656 | tf_op jit(solution)/shard_map/ppermute | solution.py:35
  110.6 3.5 %collective-permute-start.16 = (bf16[6,128,128]{2,1,0:T(8,128)(2,1)S(1)}, bf16[6,128,128]{2,1,0:T(8,128)(2,1)S(1)}, u32[]{:S(2)}, u32[]{:S(2)}) collective-permute-start(bf16[6,128,128]{2,1,0:T(8,128)(2,1)S(1)} %convert_element_type.110), channel_id=1, source_target_pairs={{128,0},{129,1},{130,2},{131,3},{132,4},{133,5},{134,6},{135,7},{1... | collective-permute-start | bytes 589832 | tf_op jit(solution)/shard_map/ppermute | solution.py:35
  111.3 3.5 %collective-permute-start.19 = (bf16[6,128,128]{2,1,0:T(8,128)(2,1)S(1)}, bf16[6,128,128]{2,1,0:T(8,128)(2,1)S(1)}, u32[]{:S(2)}, u32[]{:S(2)}) collective-permute-start(bf16[6,128,128]{2,1,0:T(8,128)(2,1)S(1)} %shard_map.57), channel_id=1, source_target_pairs={{1,0},{2,1},{3,2},{4,3},{5,4},{6,5},{7,6},{8,7},{9,8},{10,9},{11,1... | collective-permute-start | bytes 589832 | tf_op jit(solution)/shard_map/ppermute | solution.py:35
  112.0 2.9 %collective-permute-start.18 = (bf16[6,128,128]{2,1,0:T(8,128)(2,1)S(1)}, bf16[6,128,128]{2,1,0:T(8,128)(2,1)S(1)}, u32[]{:S(2)}, u32[]{:S(2)}) collective-permute-start(bf16[6,128,128]{2,1,0:T(8,128)(2,1)S(1)} %shard_map.57), channel_id=1, source_target_pairs={{0,1},{1,2},{2,3},{3,4},{4,5},{5,6},{6,7},{7,8},{8,9},{9,10},{10,1... | collective-permute-start | bytes 589832 | tf_op jit(solution)/shard_map/ppermute | solution.py:35
  112.8 10.9 %collective-permute-start.23 = (bf16[6,128,128]{2,1,0:T(8,128)(2,1)S(1)}, bf16[6,128,128]{2,1,0:T(8,128)(2,1)S(1)}, u32[]{:S(2)}, u32[]{:S(2)}) collective-permute-start(bf16[6,128,128]{2,1,0:T(8,128)(2,1)S(1)} %convert_element_type.118), channel_id=1, source_target_pairs={{32,0},{33,1},{34,2},{35,3},{36,4},{37,5},{38,6},{39,7},{40,8},{41... | collective-permute-start | bytes 589832 | tf_op jit(solution)/shard_map/ppermute | solution.py:35
  114.1 10.3 %collective-permute-start.17 = (bf16[6,128,128]{2,1,0:T(8,128)(2,1)S(1)}, bf16[6,128,128]{2,1,0:T(8,128)(2,1)S(1)}, u32[]{:S(2)}, u32[]{:S(2)}) collective-permute-start(bf16[6,128,128]{2,1,0:T(8,128)(2,1)S(1)} %fusion), channel_id=1, source_target_pairs={{256,0},{257,1},{258,2},{259,3},{260,4},{261,5},{262,6},{263,7},{2... | collective-permute-start | bytes 589832 | tf_op jit(solution)/shard_map/ppermute | solution.py:35
  121.8 3.6 %collective-permute-start.15 = (f32[6,128,128]{2,1,0:T(8,128)S(1)}, f32[6,128,128]{2,1,0:T(8,128)S(1)}, u32[]{:S(2)}, u32[]{:S(2)}) collective-permute-start(f32[6,128,128]{2,1,0:T(8,128)S(1)} %get-tuple-element.59), channel_id=1, source_target_pairs={{0,16},{1,17},{2,18},{3,19},{4,20},{5,21},{6,22},{7,23},{8,24},{9,... | collective-permute-start | bytes 1179656 | tf_op jit(solution)/shard_map/ppermute | solution.py:35
  123.8 16.7 %collective-permute-start.24 = (bf16[6,128,128]{2,1,0:T(8,128)(2,1)S(1)}, bf16[6,128,128]{2,1,0:T(8,128)(2,1)S(1)}, u32[]{:S(2)}, u32[]{:S(2)}) collective-permute-start(bf16[6,128,128]{2,1,0:T(8,128)(2,1)S(1)} %fusion.1), channel_id=1, source_target_pairs={{64,0},{65,1},{66,2},{67,3},{68,4},{69,5},{70,6},{71,7},{72,8},{73... | collective-permute-start | bytes 589832 | tf_op jit(solution)/shard_map/ppermute | solution.py:35
  125.4 20.5 %slice-start.2 = ((s8[4325376]{0:T(1024)(128)(4,1)}), s8[4194304]{0:T(1024)(128)(4,1)S(1)}, s32[]{:S(2)}) async-start(s8[4325376]{0:T(1024)(128)(4,1)} %bitcast.19), calls=%async_computation.2 | async-start | bytes 8388608
  125.5 20.5 %slice-start.3 = ((s8[4325376]{0:T(1024)(128)(4,1)}), s8[131072]{0:T(1024)(128)(4,1)S(1)}, s32[]{:S(2)}) async-start(s8[4325376]{0:T(1024)(128)(4,1)} %bitcast.19), calls=%async_computation.3 | async-start | bytes 262144
  126.3 18.2 %collective-permute-start.20 = (bf16[6,128,128]{2,1,0:T(8,128)(2,1)S(1)}, bf16[6,128,128]{2,1,0:T(8,128)(2,1)S(1)}, u32[]{:S(2)}, u32[]{:S(2)}) collective-permute-start(bf16[6,128,128]{2,1,0:T(8,128)(2,1)S(1)} %convert_element_type.114), channel_id=1, source_target_pairs={{32,0},{33,1},{34,2},{35,3},{36,4},{37,5},{38,6},{39,7},{40,8},{41... | collective-permute-start | bytes 589832 | tf_op jit(solution)/shard_map/ppermute | solution.py:35
  140.6 6.0 %collective-permute-start.28 = (bf16[6,128,128]{2,1,0:T(8,128)(2,1)S(1)}, bf16[6,128,128]{2,1,0:T(8,128)(2,1)S(1)}, u32[]{:S(2)}, u32[]{:S(2)}) collective-permute-start(bf16[6,128,128]{2,1,0:T(8,128)(2,1)S(1)} %shard_map.59), channel_id=1, source_target_pairs={{1,0},{2,1},{3,2},{4,3},{5,4},{6,5},{7,6},{8,7},{9,8},{10,9},{11,1... | collective-permute-start | bytes 589832 | tf_op jit(solution)/shard_map/ppermute | solution.py:35
  141.2 5.3 %collective-permute-start.27 = (bf16[6,128,128]{2,1,0:T(8,128)(2,1)S(1)}, bf16[6,128,128]{2,1,0:T(8,128)(2,1)S(1)}, u32[]{:S(2)}, u32[]{:S(2)}) collective-permute-start(bf16[6,128,128]{2,1,0:T(8,128)(2,1)S(1)} %shard_map.59), channel_id=1, source_target_pairs={{0,1},{1,2},{2,3},{3,4},{4,5},{5,6},{6,7},{7,8},{8,9},{9,10},{10,1... | collective-permute-start | bytes 589832 | tf_op jit(solution)/shard_map/ppermute | solution.py:35
  142.0 3.2 %collective-permute-start.25 = (bf16[6,128,128]{2,1,0:T(8,128)(2,1)S(1)}, bf16[6,128,128]{2,1,0:T(8,128)(2,1)S(1)}, u32[]{:S(2)}, u32[]{:S(2)}) collective-permute-start(bf16[6,128,128]{2,1,0:T(8,128)(2,1)S(1)} %convert_element_type.122), channel_id=1, source_target_pairs={{128,0},{129,1},{130,2},{131,3},{132,4},{133,5},{134,6},{135,7},{1... | collective-permute-start | bytes 589832 | tf_op jit(solution)/shard_map/ppermute | solution.py:35
  142.6 7.5 %collective-permute-start.33 = (bf16[18,128,128]{2,1,0:T(8,128)(2,1)S(1)}, bf16[18,128,128]{2,1,0:T(8,128)(2,1)S(1)}, u32[]{:S(2)}, u32[]{:S(2)}) collective-permute-start(bf16[18,128,128]{2,1,0:T(8,128)(2,1)S(1)} %pad_maximum_fusion.1.refs_1_.now_ref), channel_id=1, source_target_pairs={{0,32},{1,33},{2,34},{3,35},{4,36},{5,37},{6,38},{7,39},{8,40},{9,... | collective-permute-start | bytes 1769480 | tf_op jit(solution)/shard_map/ppermute | solution.py:35
  144.5 2.1 collective-permute-start.21
  145.3 1.4 collective-permute-start.26
  147.4 2.0 collective-permute-start.29
  148.1 4.2 %collective-permute-start.32 = (bf16[6,128,128]{2,1,0:T(8,128)(2,1)S(1)}, bf16[6,128,128]{2,1,0:T(8,128)(2,1)S(1)}, u32[]{:S(2)}, u32[]{:S(2)}) collective-permute-start(bf16[6,128,128]{2,1,0:T(8,128)(2,1)S(1)} %shard_map.62), channel_id=1, source_target_pairs={{1,0},{2,1},{3,2},{4,3},{5,4},{6,5},{7,6},{8,7},{9,8},{10,9},{11,1... | collective-permute-start | bytes 589832 | tf_op jit(solution)/shard_map/ppermute | solution.py:35
  148.7 3.5 %collective-permute-start.31 = (bf16[6,128,128]{2,1,0:T(8,128)(2,1)S(1)}, bf16[6,128,128]{2,1,0:T(8,128)(2,1)S(1)}, u32[]{:S(2)}, u32[]{:S(2)}) collective-permute-start(bf16[6,128,128]{2,1,0:T(8,128)(2,1)S(1)} %shard_map.62), channel_id=1, source_target_pairs={{0,1},{1,2},{2,3},{3,4},{4,5},{5,6},{6,7},{7,8},{8,9},{9,10},{10,1... | collective-permute-start | bytes 589832 | tf_op jit(solution)/shard_map/ppermute | solution.py:35
  149.5 2.8 %collective-permute-start.30 = (bf16[6,128,128]{2,1,0:T(8,128)(2,1)S(1)}, bf16[6,128,128]{2,1,0:T(8,128)(2,1)S(1)}, u32[]{:S(2)}, u32[]{:S(2)}) collective-permute-start(bf16[6,128,128]{2,1,0:T(8,128)(2,1)S(1)} %get-tuple-element.75), channel_id=1, source_target_pairs={{256,0},{257,1},{258,2},{259,3},{260,4},{261,5},{262,6},{263,7},{2... | collective-permute-start | bytes 589832 | tf_op jit(solution)/shard_map/ppermute | solution.py:35
  150.8 1.6 collective-permute-start.34
  153.0 0.7 collective-permute-start.35
  153.7 0.7 collective-permute-start.36
  154.4 0.7 collective-permute-start.37
  155.1 59.4 %collective-permute-start.38 = (bf16[6,128,128]{2,1,0:T(8,128)(2,1)S(1)}, bf16[6,128,128]{2,1,0:T(8,128)(2,1)S(1)}, u32[]{:S(2)}, u32[]{:S(2)}) collective-permute-start(bf16[6,128,128]{2,1,0:T(8,128)(2,1)S(1)} %broadcast_select_fusion.4), channel_id=1, source_target_pairs={{0,32},{1,33},{2,34},{3,35},{4,36},{5,37},{6,38},{7,39},{8,40},{9,... | collective-permute-start | bytes 589832 | tf_op jit(solution)/shard_map/ppermute | solution.py:35
  214.5 10.7 %collective-permute-start.39 = (bf16[6,128,128]{2,1,0:T(8,128)(2,1)S(1)}, bf16[6,128,128]{2,1,0:T(8,128)(2,1)S(1)}, u32[]{:S(2)}, u32[]{:S(2)}) collective-permute-start(bf16[6,128,128]{2,1,0:T(8,128)(2,1)S(1)} %broadcast_select_fusion.5.mine_ref), channel_id=1, source_target_pairs={{0,16},{1,17},{2,18},{3,19},{4,20},{5,21},{6,22},{7,23},{8,24},{9,... | collective-permute-start | bytes 589832 | tf_op jit(solution)/shard_map/ppermute | solution.py:35

commit v5 on v3

--- a/solution.py
+++ b/solution.py
@@ -324,14 +324,14 @@
     c = stage(after(c, current1), 2)
     d = stage(after(d, current1), 0)
     c1 = wide(current1)
-    third = send(after(c0, c, d), along_x(1, lambda z, x: z == 0 and x == 0))
+    third = send(after(c0, current1), along_x(1, lambda z, x: z == 0 and x == 0))
     old = lag_product(ROOT, jnp.float32, second_meta, second, after(c0, c, d))
     c = stage(c, 3)
     d = stage(d, 1)
     current2 = solve_step(0, first_meta, fields[2], after(c, d), near_inverse, first, c1, old)
 
-    third = lag_product(NEXT, jnp.bfloat16, first_meta, first, after(third, current2))
-    third = send(third, along_x(-1, lambda z, x: z == 0 and x == 1))
+    third = lag_product(NEXT, jnp.bfloat16, first_meta, first, third)
+    third = send(after(third, current2), along_x(-1, lambda z, x: z == 0 and x == 1))
     d = stage(after(d, current2), 2)
     c2 = wide(current2)
     old = lag_product(ROOT, jnp.float32, second_meta, second, after(c1, d))

time: 226 us -> 223 us (0.987)
  the two profiles are of different devices: /device:TPU:479 before, /device:TPU:39 now
where the time goes in v5:
time: 223 us; the launch traced here: 222 us
  starting transfers between devices  99.7 us (45%)
  waiting for transfers between devices  97.9 us (44%)
  Pallas kernels  13.7 us (6%)
  other arithmetic  8.64 us (4%)
    ppermute x40, starting transfers between devices, send(): return lax.ppermute(value, AXES, pairs(lags, rows, target))  99.7 us
    ppermute x40, waiting for transfers between devices, send(): return lax.ppermute(value, AXES, pairs(lags, rows, target))  97.9 us
    pallas_call x12, Pallas kernels, call(): pl.pallas_call(kernel, out_shape=out_shape, in_specs=[SMEM] + [VMEM] * le...  13.7 us
    select_n x1, other arithmetic, per_device(): second = jnp.where(core == 0, swapped, zmat)  6.3 us
  transfers between devices with their start and end apart: 40, of which 12 were waited for; matrix products, arithmetic and copies ran while one was open for 4% of the time, Pallas kernels for 5%

profile of v5, /device:TPU:39, one launch (start us, length us, event | category | flops | bytes accessed | tf_op | source)
XLA Modules:
  0.0 221.6 jit_solution(1432776082218333838)
XLA Ops:
  0.0 2.7 %collective-permute-start.2 = (bf16[12,11,128,128]{3,2,1,0:T(8,128)(2,1)}, bf16[12,11,128,128]{3,2,1,0:T(8,128)(2,1)}, u32[]{:S(2)}, u32[]{:S(2)}) collective-permute-start(bf16[12,11,128,128]{3,2,1,0:T(8,128)(2,1)} %bitcast.12), channel_id=1, source_target_pairs={{0,16},{1,17},{2,18},{3,19},{4,20},{5,21},{6,22},{7,23},{8,24},{9,... | collective-permute-start | bytes 12976136 | tf_op jit(solution)/shard_map/ppermute | solution.py:35
  2.7 0.7 broadcast_subtract_fusion
  3.6 0.7 collective-permute-start.1
  4.2 10.6 %collective-permute-start = (bf16[12,128,128]{2,1,0:T(8,128)(2,1)}, bf16[12,128,128]{2,1,0:T(8,128)(2,1)S(1)}, u32[]{:S(2)}, u32[]{:S(2)}) collective-permute-start(bf16[12,128,128]{2,1,0:T(8,128)(2,1)} %bitcast.25), channel_id=1, source_target_pairs={{0,1},{1,0},{2,3},{3,2},{4,5},{5,4},{6,7},{7,6},{8,9},{9,8},{10,11... | collective-permute-start | bytes 1179656 | tf_op jit(solution)/shard_map/ppermute | solution.py:35
  15.3 6.3 %broadcast_select_fusion = (bf16[12,11,128,128]{3,2,1,0:T(8,128)(2,1)}, bf16[12,11,128,128]{3,2,1,0:T(8,128)(2,1)S(1)}) fusion(bf16[12,11,128,128]{3,2,1,0:T(8,128)(2,1)} %collective-permute-done.2, pred[]{:T(512)S(6)} %eq.62, bf16[1,12,11,128,128]{4,3,2,1,0:T(8,128)(2,1)} %param.5), kind=kLoop, calls=%fused_computation | loop fusion | flops 4325376 | bytes 17301504 | tf_op jit(solution)/shard_map/jit(_where)/select_n | solution.py:286
  21.6 2.4 %collective-permute-done = bf16[12,128,128]{2,1,0:T(8,128)(2,1)S(1)} collective-permute-done((bf16[12,128,128]{2,1,0:T(8,128)(2,1)}, bf16[12,128,128]{2,1,0:T(8,128)(2,1)S(1)}, u32[]{:S(2)}, u32[]{:S(2)}) %collective-permute-start) | collective-permute-done | bytes 393248 | tf_op jit(solution)/shard_map/ppermute | solution.py:35
  24.0 2.3 %collective-permute-start.3 = (bf16[12,128,128]{2,1,0:T(8,128)(2,1)S(1)}, bf16[12,128,128]{2,1,0:T(8,128)(2,1)S(1)}, u32[]{:S(2)}, u32[]{:S(2)}) collective-permute-start(bf16[12,128,128]{2,1,0:T(8,128)(2,1)S(1)} %collective-permute-done), channel_id=1, source_target_pairs={{0,2},{2,4},{3,1},{4,6},{5,3},{6,8},{7,5},{8,10},{9,7},{10,12},{11... | collective-permute-start | bytes 1179656 | tf_op jit(solution)/shard_map/ppermute | solution.py:35
  26.3 10.1 %collective-permute-done.3 = bf16[12,128,128]{2,1,0:T(8,128)(2,1)S(1)} collective-permute-done((bf16[12,128,128]{2,1,0:T(8,128)(2,1)S(1)}, bf16[12,128,128]{2,1,0:T(8,128)(2,1)S(1)}, u32[]{:S(2)}, u32[]{:S(2)}) %collective-permute-start.3) | collective-permute-done | bytes 393248 | tf_op jit(solution)/shard_map/ppermute | solution.py:35
  36.6 13.4 %collective-permute-start.4 = (bf16[36,128,128]{2,1,0:T(8,128)(2,1)S(1)}, bf16[36,128,128]{2,1,0:T(8,128)(2,1)S(1)}, u32[]{:S(2)}, u32[]{:S(2)}) collective-permute-start(bf16[36,128,128]{2,1,0:T(8,128)(2,1)S(1)} %pad_maximum_fusion.refs_0_), channel_id=1, source_target_pairs={{0,16},{1,17},{2,18},{3,19},{4,20},{5,21},{6,22},{7,23},{8,24},{9,... | collective-permute-start | bytes 3538952 | tf_op jit(solution)/shard_map/ppermute | solution.py:35
  50.0 2.0 shard_map.55
  52.0 1.9 collective-permute-start.7
  53.9 1.7 collective-permute-done.7
  55.7 1.4 collective-permute-start.8
  57.2 6.0 %collective-permute-done.4.refs_0_ = bf16[36,128,128]{2,1,0:T(8,128)(2,1)S(1)} collective-permute-done((bf16[36,128,128]{2,1,0:T(8,128)(2,1)S(1)}, bf16[36,128,128]{2,1,0:T(8,128)(2,1)S(1)}, u32[]{:S(2)}, u32[]{:S(2)}) %collective-permute-start.4) | collective-permute-done | bytes 1179680 | tf_op jit(solution)/shard_map/ppermute | solution.py:35
  63.1 2.0 shard_map.56
  65.1 1.9 collective-permute-start.10
  67.3 0.7 collective-permute-start.9
  67.9 7.1 %collective-permute-start.5 = (bf16[36,128,128]{2,1,0:T(8,128)(2,1)S(1)}, bf16[36,128,128]{2,1,0:T(8,128)(2,1)S(1)}, u32[]{:S(2)}, u32[]{:S(2)}) collective-permute-start(bf16[36,128,128]{2,1,0:T(8,128)(2,1)S(1)} %collective-permute-done.4.refs_0_), channel_id=1, source_target_pairs={{0,16},{1,17},{2,18},{3,19},{4,20},{5,21},{6,22},{7,23},{8,24},{9,... | collective-permute-start | bytes 3538952 | tf_op jit(solution)/shard_map/ppermute | solution.py:35
  75.1 1.3 collective-permute-start.12
  76.5 0.7 collective-permute-start.11
  77.2 1.8 collective-permute-done.12
  79.1 0.7 collective-permute-start.14
  79.9 0.7 collective-permute-start.13
  80.6 10.3 %collective-permute-done.5.refs_0_ = bf16[36,128,128]{2,1,0:T(8,128)(2,1)S(1)} collective-permute-done((bf16[36,128,128]{2,1,0:T(8,128)(2,1)S(1)}, bf16[36,128,128]{2,1,0:T(8,128)(2,1)S(1)}, u32[]{:S(2)}, u32[]{:S(2)}) %collective-permute-start.5) | collective-permute-done | bytes 1179680 | tf_op jit(solution)/shard_map/ppermute | solution.py:35
  90.9 8.8 %collective-permute-start.6 = (bf16[36,128,128]{2,1,0:T(8,128)(2,1)S(1)}, bf16[36,128,128]{2,1,0:T(8,128)(2,1)S(1)}, u32[]{:S(2)}, u32[]{:S(2)}) collective-permute-start(bf16[36,128,128]{2,1,0:T(8,128)(2,1)S(1)} %collective-permute-done.5.refs_0_), channel_id=1, source_target_pairs={{0,16},{1,17},{2,18},{3,19},{4,20},{5,21},{6,22},{7,23},{8,24},{9,... | collective-permute-start | bytes 3538952 | tf_op jit(solution)/shard_map/ppermute | solution.py:35
  99.8 2.0 shard_map.57
  101.7 1.9 collective-permute-start.18
  103.7 0.6 shard_map.58
  104.3 0.7 collective-permute-start.16
  105.0 0.7 collective-permute-start.21
  105.7 0.7 collective-permute-start.22
  106.5 1.3 collective-permute-start.19
  107.9 0.7 collective-permute-start.17
  108.6 3.2 %collective-permute-done.19 = bf16[6,128,128]{2,1,0:T(8,128)(2,1)S(1)} collective-permute-done((bf16[6,128,128]{2,1,0:T(8,128)(2,1)S(1)}, bf16[6,128,128]{2,1,0:T(8,128)(2,1)S(1)}, u32[]{:S(2)}, u32[]{:S(2)}) %collective-permute-start.19) | collective-permute-done | bytes 196640 | tf_op jit(solution)/shard_map/ppermute | solution.py:35
  111.9 0.7 collective-permute-start.20
  112.9 2.0 shard_map.59
  114.9 2.6 %collective-permute-start.15 = (f32[6,128,128]{2,1,0:T(8,128)S(1)}, f32[6,128,128]{2,1,0:T(8,128)S(1)}, u32[]{:S(2)}, u32[]{:S(2)}) collective-permute-start(f32[6,128,128]{2,1,0:T(8,128)S(1)} %get-tuple-element.59), channel_id=1, source_target_pairs={{0,16},{1,17},{2,18},{3,19},{4,20},{5,21},{6,22},{7,23},{8,24},{9,... | collective-permute-start | bytes 1179656 | tf_op jit(solution)/shard_map/ppermute | solution.py:35
  117.7 1.2 collective-permute-done.15
  118.9 0.7 shard_map.60
  119.7 0.8 collective-permute-start.25
  120.5 0.7 collective-permute-start.27
  121.2 0.7 collective-permute-start.28
  121.9 0.7 collective-permute-start.33
  122.6 13.2 %collective-permute-start.23 = (bf16[6,128,128]{2,1,0:T(8,128)(2,1)S(1)}, bf16[6,128,128]{2,1,0:T(8,128)(2,1)S(1)}, u32[]{:S(2)}, u32[]{:S(2)}) collective-permute-start(bf16[6,128,128]{2,1,0:T(8,128)(2,1)S(1)} %convert_element_type.118), channel_id=1, source_target_pairs={{32,0},{33,1},{34,2},{35,3},{36,4},{37,5},{38,6},{39,7},{40,8},{41... | collective-permute-start | bytes 589832 | tf_op jit(solution)/shard_map/ppermute | solution.py:35
  135.9 0.7 collective-permute-start.26
  136.5 3.1 %collective-permute-done.23 = bf16[6,128,128]{2,1,0:T(8,128)(2,1)S(1)} collective-permute-done((bf16[6,128,128]{2,1,0:T(8,128)(2,1)S(1)}, bf16[6,128,128]{2,1,0:T(8,128)(2,1)S(1)}, u32[]{:S(2)}, u32[]{:S(2)}) %collective-permute-start.23) | collective-permute-done | bytes 196640 | tf_op jit(solution)/shard_map/ppermute | solution.py:35
  139.7 0.7 collective-permute-start.24
  141.2 0.6 shard_map.62
  141.8 0.7 collective-permute-start.29
  142.5 0.7 collective-permute-start.31
  143.2 0.7 collective-permute-start.32
  144.0 0.7 collective-permute-start.30
  144.7 0.6 shard_map.64
  145.2 0.7 collective-permute-start.34
  145.9 0.8 shard_map.63.refs_2_
  146.8 0.6 shard_map.65
  147.4 0.7 collective-permute-start.35
  148.1 0.7 collective-permute-start.36
  148.9 0.7 collective-permute-start.37
  149.6 1.3 collective-permute-start.38
  150.9 56.7 %collective-permute-done.38 = bf16[6,128,128]{2,1,0:T(8,128)(2,1)S(1)} collective-permute-done((bf16[6,128,128]{2,1,0:T(8,128)(2,1)S(1)}, bf16[6,128,128]{2,1,0:T(8,128)(2,1)S(1)}, u32[]{:S(2)}, u32[]{:S(2)}) %collective-permute-start.38) | collective-permute-done | bytes 196640 | tf_op jit(solution)/shard_map/ppermute | solution.py:35
  207.6 11.5 %collective-permute-start.39 = (bf16[6,128,128]{2,1,0:T(8,128)(2,1)S(1)}, bf16[6,128,128]{2,1,0:T(8,128)(2,1)S(1)}, u32[]{:S(2)}, u32[]{:S(2)}) collective-permute-start(bf16[6,128,128]{2,1,0:T(8,128)(2,1)S(1)} %broadcast_select_fusion.5.mine_ref), channel_id=1, source_target_pairs={{0,16},{1,17},{2,18},{3,19},{4,20},{5,21},{6,22},{7,23},{8,24},{9,... | collective-permute-start | bytes 589832 | tf_op jit(solution)/shard_map/ppermute | solution.py:35
  219.1 1.0 collective-permute-done.39.other_ref
  220.1 1.5 shard_map.66
  (90 shorter events, 3.2 us)
Async XLA Ops:
  0.0 15.3 %collective-permute-start.2 = (bf16[12,11,128,128]{3,2,1,0:T(8,128)(2,1)}, bf16[12,11,128,128]{3,2,1,0:T(8,128)(2,1)}, u32[]{:S(2)}, u32[]{:S(2)}) collective-permute-start(bf16[12,11,128,128]{3,2,1,0:T(8,128)(2,1)} %bitcast.12), channel_id=1, source_target_pairs={{0,16},{1,17},{2,18},{3,19},{4,20},{5,21},{6,22},{7,23},{8,24},{9,... | collective-permute-start | bytes 12976136 | tf_op jit(solution)/shard_map/ppermute | solution.py:35
  3.6 11.4 %collective-permute-start.1 = (s32[132]{0:T(256)S(1)}, s32[132]{0:T(256)S(1)}, u32[]{:S(2)}, u32[]{:S(2)}) collective-permute-start(s32[132]{0:T(256)S(1)} %sub.30), channel_id=1, source_target_pairs={{0,16},{1,17},{2,18},{3,19},{4,20},{5,21},{6,22},{7,23},{8,24},{9,... | collective-permute-start | bytes 1592 | tf_op jit(solution)/shard_map/ppermute | solution.py:35
  4.2 19.8 %collective-permute-start = (bf16[12,128,128]{2,1,0:T(8,128)(2,1)}, bf16[12,128,128]{2,1,0:T(8,128)(2,1)S(1)}, u32[]{:S(2)}, u32[]{:S(2)}) collective-permute-start(bf16[12,128,128]{2,1,0:T(8,128)(2,1)} %bitcast.25), channel_id=1, source_target_pairs={{0,1},{1,0},{2,3},{3,2},{4,5},{5,4},{6,7},{7,6},{8,9},{9,8},{10,11... | collective-permute-start | bytes 1179656 | tf_op jit(solution)/shard_map/ppermute | solution.py:35
  15.2 34.8 %slice-start = ((s8[4325376]{0:T(1024)(128)(4,1)}), s8[131072]{0:T(1024)(128)(4,1)S(1)}, s32[]{:S(2)}) async-start(s8[4325376]{0:T(1024)(128)(4,1)} %bitcast.13), calls=%async_computation | async-start | bytes 262144
  15.3 21.2 %copy-start.2 = (bf16[1,1536,128]{2,1,0:T(8,128)(2,1)S(1)}, bf16[1,1536,128]{2,1,0:T(8,128)(2,1)}, u32[]{:S(2)}) copy-start(bf16[1,1536,128]{2,1,0:T(8,128)(2,1)} %param.7) | copy-start | bytes 1179652
  15.3 34.8 %slice-start.1 = ((s8[4325376]{0:T(1024)(128)(4,1)}), s8[4194304]{0:T(1024)(128)(4,1)S(1)}, s32[]{:S(2)}) async-start(s8[4325376]{0:T(1024)(128)(4,1)} %bitcast.13), calls=%async_computation.1 | async-start | bytes 8388608
  24.0 12.4 %collective-permute-start.3 = (bf16[12,128,128]{2,1,0:T(8,128)(2,1)S(1)}, bf16[12,128,128]{2,1,0:T(8,128)(2,1)S(1)}, u32[]{:S(2)}, u32[]{:S(2)}) collective-permute-start(bf16[12,128,128]{2,1,0:T(8,128)(2,1)S(1)} %collective-permute-done), channel_id=1, source_target_pairs={{0,2},{2,4},{3,1},{4,6},{5,3},{6,8},{7,5},{8,10},{9,7},{10,12},{11... | collective-permute-start | bytes 1179656 | tf_op jit(solution)/shard_map/ppermute | solution.py:35
  36.6 26.6 %collective-permute-start.4 = (bf16[36,128,128]{2,1,0:T(8,128)(2,1)S(1)}, bf16[36,128,128]{2,1,0:T(8,128)(2,1)S(1)}, u32[]{:S(2)}, u32[]{:S(2)}) collective-permute-start(bf16[36,128,128]{2,1,0:T(8,128)(2,1)S(1)} %pad_maximum_fusion.refs_0_), channel_id=1, source_target_pairs={{0,16},{1,17},{2,18},{3,19},{4,20},{5,21},{6,22},{7,23},{8,24},{9,... | collective-permute-start | bytes 3538952 | tf_op jit(solution)/shard_map/ppermute | solution.py:35
  52.0 3.6 %collective-permute-start.7 = (f32[6,128,128]{2,1,0:T(8,128)S(1)}, f32[6,128,128]{2,1,0:T(8,128)S(1)}, u32[]{:S(2)}, u32[]{:S(2)}) collective-permute-start(f32[6,128,128]{2,1,0:T(8,128)S(1)} %get-tuple-element.48), channel_id=1, source_target_pairs={{0,16},{1,17},{2,18},{3,19},{4,20},{5,21},{6,22},{7,23},{8,24},{9,... | collective-permute-start | bytes 1179656 | tf_op jit(solution)/shard_map/ppermute | solution.py:35
  55.7 11.3 %copy-start.1 = (bf16[4,1536,128]{2,1,0:T(8,128)(2,1)S(1)}, bf16[4,1536,128]{2,1,0:T(8,128)(2,1)}, u32[]{:S(2)}) copy-start(bf16[4,1536,128]{2,1,0:T(8,128)(2,1)} %param.8) | copy-start | bytes 4718596
  55.7 11.5 %collective-permute-start.8 = (bf16[6,128,128]{2,1,0:T(8,128)(2,1)S(1)}, bf16[6,128,128]{2,1,0:T(8,128)(2,1)S(1)}, u32[]{:S(2)}, u32[]{:S(2)}) collective-permute-start(bf16[6,128,128]{2,1,0:T(8,128)(2,1)S(1)} %get-tuple-element.85), channel_id=1, source_target_pairs={{32,0},{33,1},{34,2},{35,3},{36,4},{37,5},{38,6},{39,7},{40,8},{41... | collective-permute-start | bytes 589832 | tf_op jit(solution)/shard_map/ppermute | solution.py:35
  65.1 10.0 %collective-permute-start.10 = (f32[6,128,128]{2,1,0:T(8,128)S(1)}, f32[6,128,128]{2,1,0:T(8,128)S(1)}, u32[]{:S(2)}, u32[]{:S(2)}) collective-permute-start(f32[6,128,128]{2,1,0:T(8,128)S(1)} %get-tuple-element.51), channel_id=1, source_target_pairs={{0,16},{1,17},{2,18},{3,19},{4,20},{5,21},{6,22},{7,23},{8,24},{9,... | collective-permute-start | bytes 1179656 | tf_op jit(solution)/shard_map/ppermute | solution.py:35
  67.3 9.2 %collective-permute-start.9 = (bf16[6,128,128]{2,1,0:T(8,128)(2,1)S(1)}, bf16[6,128,128]{2,1,0:T(8,128)(2,1)S(1)}, u32[]{:S(2)}, u32[]{:S(2)}) collective-permute-start(bf16[6,128,128]{2,1,0:T(8,128)(2,1)S(1)} %convert_element_type.100), channel_id=1, source_target_pairs={{64,0},{65,1},{66,2},{67,3},{68,4},{69,5},{70,6},{71,7},{72,8},{73... | collective-permute-start | bytes 589832 | tf_op jit(solution)/shard_map/ppermute | solution.py:35
  67.9 23.0 %collective-permute-start.5 = (bf16[36,128,128]{2,1,0:T(8,128)(2,1)S(1)}, bf16[36,128,128]{2,1,0:T(8,128)(2,1)S(1)}, u32[]{:S(2)}, u32[]{:S(2)}) collective-permute-start(bf16[36,128,128]{2,1,0:T(8,128)(2,1)S(1)} %collective-permute-done.4.refs_0_), channel_id=1, source_target_pairs={{0,16},{1,17},{2,18},{3,19},{4,20},{5,21},{6,22},{7,23},{8,24},{9,... | collective-permute-start | bytes 3538952 | tf_op jit(solution)/shard_map/ppermute | solution.py:35
  75.1 3.9 %collective-permute-start.12 = (bf16[6,128,128]{2,1,0:T(8,128)(2,1)S(1)}, bf16[6,128,128]{2,1,0:T(8,128)(2,1)S(1)}, u32[]{:S(2)}, u32[]{:S(2)}) collective-permute-start(bf16[6,128,128]{2,1,0:T(8,128)(2,1)S(1)} %get-tuple-element.83), channel_id=1, source_target_pairs={{32,0},{33,1},{34,2},{35,3},{36,4},{37,5},{38,6},{39,7},{40,8},{41... | collective-permute-start | bytes 589832 | tf_op jit(solution)/shard_map/ppermute | solution.py:35
  76.5 3.2 %collective-permute-start.11 = (bf16[6,128,128]{2,1,0:T(8,128)(2,1)S(1)}, bf16[6,128,128]{2,1,0:T(8,128)(2,1)S(1)}, u32[]{:S(2)}, u32[]{:S(2)}) collective-permute-start(bf16[6,128,128]{2,1,0:T(8,128)(2,1)S(1)} %convert_element_type.102), channel_id=1, source_target_pairs={{128,0},{129,1},{130,2},{131,3},{132,4},{133,5},{134,6},{135,7},{1... | collective-permute-start | bytes 589832 | tf_op jit(solution)/shard_map/ppermute | solution.py:35
  79.1 1.5 collective-permute-start.14
  79.9 23.8 %collective-permute-start.13 = (bf16[6,128,128]{2,1,0:T(8,128)(2,1)S(1)}, bf16[6,128,128]{2,1,0:T(8,128)(2,1)S(1)}, u32[]{:S(2)}, u32[]{:S(2)}) collective-permute-start(bf16[6,128,128]{2,1,0:T(8,128)(2,1)S(1)} %convert_element_type.106), channel_id=1, source_target_pairs={{256,0},{257,1},{258,2},{259,3},{260,4},{261,5},{262,6},{263,7},{2... | collective-permute-start | bytes 589832 | tf_op jit(solution)/shard_map/ppermute | solution.py:35
  80.6 23.1 %copy-start = (f32[12,128,128]{2,1,0:T(8,128)S(1)}, f32[12,128,128]{2,1,0:T(8,128)}, u32[]{:S(2)}) copy-start(f32[12,128,128]{2,1,0:T(8,128)} %inverse_ref.7) | copy-start | bytes 2359300
  90.9 22.0 %collective-permute-start.6 = (bf16[36,128,128]{2,1,0:T(8,128)(2,1)S(1)}, bf16[36,128,128]{2,1,0:T(8,128)(2,1)S(1)}, u32[]{:S(2)}, u32[]{:S(2)}) collective-permute-start(bf16[36,128,128]{2,1,0:T(8,128)(2,1)S(1)} %collective-permute-done.5.refs_0_), channel_id=1, source_target_pairs={{0,16},{1,17},{2,18},{3,19},{4,20},{5,21},{6,22},{7,23},{8,24},{9,... | collective-permute-start | bytes 3538952 | tf_op jit(solution)/shard_map/ppermute | solution.py:35
  101.7 4.6 %collective-permute-start.18 = (f32[6,128,128]{2,1,0:T(8,128)S(1)}, f32[6,128,128]{2,1,0:T(8,128)S(1)}, u32[]{:S(2)}, u32[]{:S(2)}) collective-permute-start(f32[6,128,128]{2,1,0:T(8,128)S(1)} %get-tuple-element.61), channel_id=1, source_target_pairs={{0,16},{1,17},{2,18},{3,19},{4,20},{5,21},{6,22},{7,23},{8,24},{9,... | collective-permute-start | bytes 1179656 | tf_op jit(solution)/shard_map/ppermute | solution.py:35
  104.3 3.5 %collective-permute-start.16 = (bf16[6,128,128]{2,1,0:T(8,128)(2,1)S(1)}, bf16[6,128,128]{2,1,0:T(8,128)(2,1)S(1)}, u32[]{:S(2)}, u32[]{:S(2)}) collective-permute-start(bf16[6,128,128]{2,1,0:T(8,128)(2,1)S(1)} %convert_element_type.110), channel_id=1, source_target_pairs={{128,0},{129,1},{130,2},{131,3},{132,4},{133,5},{134,6},{135,7},{1... | collective-permute-start | bytes 589832 | tf_op jit(solution)/shard_map/ppermute | solution.py:35
  105.0 3.5 %collective-permute-start.21 = (bf16[6,128,128]{2,1,0:T(8,128)(2,1)S(1)}, bf16[6,128,128]{2,1,0:T(8,128)(2,1)S(1)}, u32[]{:S(2)}, u32[]{:S(2)}) collective-permute-start(bf16[6,128,128]{2,1,0:T(8,128)(2,1)S(1)} %shard_map.58), channel_id=1, source_target_pairs={{0,1},{1,2},{2,3},{3,4},{4,5},{5,6},{6,7},{7,8},{8,9},{9,10},{10,1... | collective-permute-start | bytes 589832 | tf_op jit(solution)/shard_map/ppermute | solution.py:35
  105.7 2.8 %collective-permute-start.22 = (bf16[6,128,128]{2,1,0:T(8,128)(2,1)S(1)}, bf16[6,128,128]{2,1,0:T(8,128)(2,1)S(1)}, u32[]{:S(2)}, u32[]{:S(2)}) collective-permute-start(bf16[6,128,128]{2,1,0:T(8,128)(2,1)S(1)} %shard_map.58), channel_id=1, source_target_pairs={{1,0},{2,1},{3,2},{4,3},{5,4},{6,5},{7,6},{8,7},{9,8},{10,9},{11,1... | collective-permute-start | bytes 589832 | tf_op jit(solution)/shard_map/ppermute | solution.py:35
  106.5 5.4 %collective-permute-start.19 = (bf16[6,128,128]{2,1,0:T(8,128)(2,1)S(1)}, bf16[6,128,128]{2,1,0:T(8,128)(2,1)S(1)}, u32[]{:S(2)}, u32[]{:S(2)}) collective-permute-start(bf16[6,128,128]{2,1,0:T(8,128)(2,1)S(1)} %convert_element_type.114), channel_id=1, source_target_pairs={{32,0},{33,1},{34,2},{35,3},{36,4},{37,5},{38,6},{39,7},{40,8},{41... | collective-permute-start | bytes 589832 | tf_op jit(solution)/shard_map/ppermute | solution.py:35
  107.9 9.7 %collective-permute-start.17 = (bf16[6,128,128]{2,1,0:T(8,128)(2,1)S(1)}, bf16[6,128,128]{2,1,0:T(8,128)(2,1)S(1)}, u32[]{:S(2)}, u32[]{:S(2)}) collective-permute-start(bf16[6,128,128]{2,1,0:T(8,128)(2,1)S(1)} %fusion), channel_id=1, source_target_pairs={{256,0},{257,1},{258,2},{259,3},{260,4},{261,5},{262,6},{263,7},{2... | collective-permute-start | bytes 589832 | tf_op jit(solution)/shard_map/ppermute | solution.py:35
  111.9 5.7 %collective-permute-start.20 = (bf16[6,128,128]{2,1,0:T(8,128)(2,1)S(1)}, bf16[6,128,128]{2,1,0:T(8,128)(2,1)S(1)}, u32[]{:S(2)}, u32[]{:S(2)}) collective-permute-start(bf16[6,128,128]{2,1,0:T(8,128)(2,1)S(1)} %fusion.1), channel_id=1, source_target_pairs={{64,0},{65,1},{66,2},{67,3},{68,4},{69,5},{70,6},{71,7},{72,8},{73... | collective-permute-start | bytes 589832 | tf_op jit(solution)/shard_map/ppermute | solution.py:35
  114.9 4.0 %collective-permute-start.15 = (f32[6,128,128]{2,1,0:T(8,128)S(1)}, f32[6,128,128]{2,1,0:T(8,128)S(1)}, u32[]{:S(2)}, u32[]{:S(2)}) collective-permute-start(f32[6,128,128]{2,1,0:T(8,128)S(1)} %get-tuple-element.59), channel_id=1, source_target_pairs={{0,16},{1,17},{2,18},{3,19},{4,20},{5,21},{6,22},{7,23},{8,24},{9,... | collective-permute-start | bytes 1179656 | tf_op jit(solution)/shard_map/ppermute | solution.py:35
  118.9 21.5 %slice-start.2 = ((s8[4325376]{0:T(1024)(128)(4,1)}), s8[4194304]{0:T(1024)(128)(4,1)S(1)}, s32[]{:S(2)}) async-start(s8[4325376]{0:T(1024)(128)(4,1)} %bitcast.19), calls=%async_computation.2 | async-start | bytes 8388608
  118.9 21.5 %slice-start.3 = ((s8[4325376]{0:T(1024)(128)(4,1)}), s8[131072]{0:T(1024)(128)(4,1)S(1)}, s32[]{:S(2)}) async-start(s8[4325376]{0:T(1024)(128)(4,1)} %bitcast.19), calls=%async_computation.3 | async-start | bytes 262144
  119.7 16.1 %collective-permute-start.25 = (bf16[6,128,128]{2,1,0:T(8,128)(2,1)S(1)}, bf16[6,128,128]{2,1,0:T(8,128)(2,1)S(1)}, u32[]{:S(2)}, u32[]{:S(2)}) collective-permute-start(bf16[6,128,128]{2,1,0:T(8,128)(2,1)S(1)} %convert_element_type.122), channel_id=1, source_target_pairs={{128,0},{129,1},{130,2},{131,3},{132,4},{133,5},{134,6},{135,7},{1... | collective-permute-start | bytes 589832 | tf_op jit(solution)/shard_map/ppermute | solution.py:35
  120.5 20.5 %collective-permute-start.27 = (bf16[6,128,128]{2,1,0:T(8,128)(2,1)S(1)}, bf16[6,128,128]{2,1,0:T(8,128)(2,1)S(1)}, u32[]{:S(2)}, u32[]{:S(2)}) collective-permute-start(bf16[6,128,128]{2,1,0:T(8,128)(2,1)S(1)} %shard_map.60), channel_id=1, source_target_pairs={{0,1},{1,2},{2,3},{3,4},{4,5},{5,6},{6,7},{7,8},{8,9},{9,10},{10,1... | collective-permute-start | bytes 589832 | tf_op jit(solution)/shard_map/ppermute | solution.py:35
  121.2 19.9 %collective-permute-start.28 = (bf16[6,128,128]{2,1,0:T(8,128)(2,1)S(1)}, bf16[6,128,128]{2,1,0:T(8,128)(2,1)S(1)}, u32[]{:S(2)}, u32[]{:S(2)}) collective-permute-start(bf16[6,128,128]{2,1,0:T(8,128)(2,1)S(1)} %shard_map.60), channel_id=1, source_target_pairs={{1,0},{2,1},{3,2},{4,3},{5,4},{6,5},{7,6},{8,7},{9,8},{10,9},{11,1... | collective-permute-start | bytes 589832 | tf_op jit(solution)/shard_map/ppermute | solution.py:35
  121.9 22.8 %collective-permute-start.33 = (bf16[18,128,128]{2,1,0:T(8,128)(2,1)S(1)}, bf16[18,128,128]{2,1,0:T(8,128)(2,1)S(1)}, u32[]{:S(2)}, u32[]{:S(2)}) collective-permute-start(bf16[18,128,128]{2,1,0:T(8,128)(2,1)S(1)} %pad_maximum_fusion.1.refs_1_.now_ref), channel_id=1, source_target_pairs={{0,32},{1,33},{2,34},{3,35},{4,36},{5,37},{6,38},{7,39},{8,40},{9,... | collective-permute-start | bytes 1769480 | tf_op jit(solution)/shard_map/ppermute | solution.py:35
  122.6 17.1 %collective-permute-start.23 = (bf16[6,128,128]{2,1,0:T(8,128)(2,1)S(1)}, bf16[6,128,128]{2,1,0:T(8,128)(2,1)S(1)}, u32[]{:S(2)}, u32[]{:S(2)}) collective-permute-start(bf16[6,128,128]{2,1,0:T(8,128)(2,1)S(1)} %convert_element_type.118), channel_id=1, source_target_pairs={{32,0},{33,1},{34,2},{35,3},{36,4},{37,5},{38,6},{39,7},{40,8},{41... | collective-permute-start | bytes 589832 | tf_op jit(solution)/shard_map/ppermute | solution.py:35
  135.9 5.3 %collective-permute-start.26 = (bf16[6,128,128]{2,1,0:T(8,128)(2,1)S(1)}, bf16[6,128,128]{2,1,0:T(8,128)(2,1)S(1)}, u32[]{:S(2)}, u32[]{:S(2)}) collective-permute-start(bf16[6,128,128]{2,1,0:T(8,128)(2,1)S(1)} %get-tuple-element.77), channel_id=1, source_target_pairs={{256,0},{257,1},{258,2},{259,3},{260,4},{261,5},{262,6},{263,7},{2... | collective-permute-start | bytes 589832 | tf_op jit(solution)/shard_map/ppermute | solution.py:35
  139.7 1.4 collective-permute-start.24
  141.8 2.0 collective-permute-start.29
  142.5 4.2 %collective-permute-start.31 = (bf16[6,128,128]{2,1,0:T(8,128)(2,1)S(1)}, bf16[6,128,128]{2,1,0:T(8,128)(2,1)S(1)}, u32[]{:S(2)}, u32[]{:S(2)}) collective-permute-start(bf16[6,128,128]{2,1,0:T(8,128)(2,1)S(1)} %shard_map.62), channel_id=1, source_target_pairs={{0,1},{1,2},{2,3},{3,4},{4,5},{5,6},{6,7},{7,8},{8,9},{9,10},{10,1... | collective-permute-start | bytes 589832 | tf_op jit(solution)/shard_map/ppermute | solution.py:35
  143.2 3.5 %collective-permute-start.32 = (bf16[6,128,128]{2,1,0:T(8,128)(2,1)S(1)}, bf16[6,128,128]{2,1,0:T(8,128)(2,1)S(1)}, u32[]{:S(2)}, u32[]{:S(2)}) collective-permute-start(bf16[6,128,128]{2,1,0:T(8,128)(2,1)S(1)} %shard_map.62), channel_id=1, source_target_pairs={{1,0},{2,1},{3,2},{4,3},{5,4},{6,5},{7,6},{8,7},{9,8},{10,9},{11,1... | collective-permute-start | bytes 589832 | tf_op jit(solution)/shard_map/ppermute | solution.py:35
  144.0 2.8 %collective-permute-start.30 = (bf16[6,128,128]{2,1,0:T(8,128)(2,1)S(1)}, bf16[6,128,128]{2,1,0:T(8,128)(2,1)S(1)}, u32[]{:S(2)}, u32[]{:S(2)}) collective-permute-start(bf16[6,128,128]{2,1,0:T(8,128)(2,1)S(1)} %get-tuple-element.75), channel_id=1, source_target_pairs={{256,0},{257,1},{258,2},{259,3},{260,4},{261,5},{262,6},{263,7},{2... | collective-permute-start | bytes 589832 | tf_op jit(solution)/shard_map/ppermute | solution.py:35
  145.2 1.6 collective-permute-start.34
  147.4 0.7 collective-permute-start.35
  148.1 0.7 collective-permute-start.36
  148.9 0.7 collective-permute-start.37
  149.6 58.0 %collective-permute-start.38 = (bf16[6,128,128]{2,1,0:T(8,128)(2,1)S(1)}, bf16[6,128,128]{2,1,0:T(8,128)(2,1)S(1)}, u32[]{:S(2)}, u32[]{:S(2)}) collective-permute-start(bf16[6,128,128]{2,1,0:T(8,128)(2,1)S(1)} %broadcast_select_fusion.4), channel_id=1, source_target_pairs={{0,32},{1,33},{2,34},{3,35},{4,36},{5,37},{6,38},{7,39},{8,40},{9,... | collective-permute-start | bytes 589832 | tf_op jit(solution)/shard_map/ppermute | solution.py:35
  207.6 12.5 %collective-permute-start.39 = (bf16[6,128,128]{2,1,0:T(8,128)(2,1)S(1)}, bf16[6,128,128]{2,1,0:T(8,128)(2,1)S(1)}, u32[]{:S(2)}, u32[]{:S(2)}) collective-permute-start(bf16[6,128,128]{2,1,0:T(8,128)(2,1)S(1)} %broadcast_select_fusion.5.mine_ref), channel_id=1, source_target_pairs={{0,16},{1,17},{2,18},{3,19},{4,20},{5,21},{6,22},{7,23},{8,24},{9,... | collective-permute-start | bytes 589832 | tf_op jit(solution)/shard_map/ppermute | solution.py:35
